TPU v7x, 32 devices: a whole 2x2x4 slice. The times are simulated.
32 devices in a mesh: fsdp: 8 (over z, x), tp: 4 (over y, core).
Axes of the slice: x: 2, y: 2, z: 4, core: 2. Of those that a mesh axis runs over, the one named last changes fastest.
Arguments:
- residual_in: bfloat16 [16384, 1024], P(('fsdp', 'tp')), may hold values from -6 to 6
- out_cotangent: bfloat16 [16384, 1024], P(('fsdp', 'tp')), may hold values from -6 to 6
- expert_index: int32 [16384, 1], P(('fsdp', 'tp')), may hold values from 0 to 15; in each aligned block of 512 rows (0 to 511, 512 to 1023, ...) at most 64 rows name the same one
- document_index: int32 [8, 2048], P('fsdp', 'tp'), may hold values from 0 to 3, never falling along the last dimension, each value on 1 to 1024 neighbouring positions
- piece_starts: int32 [8, 2], P('fsdp'), may hold values from 0 to 1792, as said below
- first_norm_gain: float32 [1024], replicated, may hold values from 0.5 to 1.5
- first_norm_shift: float32 [1024], replicated, may hold values from -0.6 to 0.6
- input_weight: bfloat16 [1024, 3, 1024], P('fsdp', None, 'tp'), may hold values from -0.1875 to 0.1875
- input_bias: bfloat16 [2, 16, 64], P(None, 'tp', 'fsdp'), may hold values from -0.59765625 to 0.59765625
- output_weight: bfloat16 [1024, 1024], P('tp', 'fsdp'), may hold values from -0.5 to 0.5
- output_bias: float32 [1024], replicated, may hold values from -0.6 to 0.6
- second_norm_gain: float32 [1024], replicated, may hold values from 0.5 to 1.5
- second_norm_shift: float32 [1024], replicated, may hold values from -0.6 to 0.6
- expert_up: bfloat16 [16, 1024, 4096], P('fsdp', None, 'tp'), may hold values from -0.1875 to 0.1875
- expert_up_bias: float32 [16, 4096], P('fsdp', 'tp'), may hold values from -0.6 to 0.6
- expert_down: bfloat16 [16, 4096, 1024], P('fsdp', 'tp'), may hold values from -0.125 to 0.125
- expert_down_bias: float32 [16, 1024], P('fsdp'), may hold values from -2.4 to 2.4
Outputs:
- block_output: bfloat16 [16384, 1024], P(('fsdp', 'tp'))
- back_residual: float32 [16384, 1024], P(('fsdp', 'tp'))
- back_first_gain: float32 [1024], replicated
- back_first_shift: float32 [1024], replicated
- back_input_weight: float32 [1024, 3, 1024], P('fsdp', None, 'tp')
- back_input_bias: float32 [2, 16, 64], P(None, 'tp', 'fsdp')
- back_output_weight: float32 [1024, 1024], P('tp', 'fsdp')
- back_output_bias: float32 [1024], replicated
- back_second_gain: float32 [1024], replicated
- back_second_shift: float32 [1024], replicated
- back_expert_up: float32 [16, 1024, 4096], P('fsdp', None, 'tp')
- back_expert_up_bias: float32 [16, 4096], P('fsdp', 'tp')
- back_expert_down: float32 [16, 4096, 1024], P('fsdp', 'tp')
- back_expert_down_bias: float32 [16, 1024], P('fsdp')
Inputs may be any that keep to these rules, and one draw needn't show every extreme that they name: `expert_index`: among the tokens of one device no expert is named by more than 64 tokens, a bound that some block reaches. `document_index`: document numbers never fall along a sequence; a document has 1 to 1024 positions. `piece_starts`: piece p of a sequence starts within positions p * (1024) to (p + 1) * 1024 - 256, so pieces never meet.
All inputs are finite; a program needn't handle non-finite values.
Results may differ from a plain program's by a relative error of at most 0.02.
Values may be sent and summed in bfloat16 or wider, within the bound.
No kernel may reach another device: no remote copies, remote signals or barrier semaphores. Data moves between devices by JAX's collectives and lax.ppermute only.
A program may use at most 256 MiB of HBM per device.

v0:
```python
import jax
import jax.numpy as jnp
from jax import lax
from jax.sharding import PartitionSpec as P

HEAD_DIM = 64
EXP_DEV = 2
PIECE = 256


EPSILON = 1e-05
MASKED = -1e30


def smooth_gelu(values):
    return jax.nn.gelu(values, approximate=True)


def layer_norm(values, gain, shift):
    center = jnp.mean(values, axis=-1, keepdims=True)
    centered = values - center
    inverse = lax.rsqrt(jnp.mean(centered * centered, axis=-1, keepdims=True) + EPSILON)
    unit = centered * inverse
    return (unit * gain + shift, unit, inverse)


def norm_back(incoming, unit, inverse, gain):
    scaled = incoming * gain
    return inverse * (
        scaled
        - jnp.mean(scaled, axis=-1, keepdims=True)
        - unit * jnp.mean(scaled * unit, axis=-1, keepdims=True)
    )


def piece_labels(starts, length):
    places = jnp.arange(length, dtype=jnp.int32)
    inside = (places[None, :] >= starts[:, None]) & (places[None, :] < starts[:, None] + PIECE)
    labels = jnp.arange(1, starts.shape[0] + 1, dtype=jnp.int32)
    return jnp.sum(jnp.where(inside, labels[:, None], 0), axis=0)


def block_mask(first_row, block_rows, docs, labels):
    row_places = first_row + jnp.arange(block_rows, dtype=jnp.int32)
    column_places = jnp.arange(docs.shape[0], dtype=jnp.int32)
    row_docs = lax.dynamic_slice_in_dim(docs, first_row, block_rows)
    row_labels = lax.dynamic_slice_in_dim(labels, first_row, block_rows)
    same_doc = row_docs[:, None] == docs[None, :]
    causal = column_places[None, :] <= row_places[:, None]
    same_piece = (row_labels[:, None] == labels[None, :]) & (row_labels[:, None] > 0)
    return same_doc & (causal | same_piece)


def expert_forward(rows_in, upper, upper_bias, lower):
    pre = (
        jnp.einsum("secd,edf->secf", rows_in, upper, preferred_element_type=jnp.float32)
        + upper_bias[None, :, None, :]
    )
    act = smooth_gelu(pre).astype(jnp.bfloat16)
    partial_out = jnp.einsum("secf,efd->secd", act, lower, preferred_element_type=jnp.float32)
    return (pre, act, partial_out)


def expert_backward(rows_in, cotangent_rows, pre, act, upper, lower):
    lower_back = jnp.einsum(
        "secf,secd->efd", act, cotangent_rows, preferred_element_type=jnp.float32
    )
    lower_bias_back = jnp.sum(cotangent_rows, axis=(0, 2), dtype=jnp.float32)
    act_back = jnp.einsum(
        "secd,efd->secf", cotangent_rows, lower, preferred_element_type=jnp.float32
    )
    unused, gelu_pull = jax.vjp(smooth_gelu, pre)
    pre_back = gelu_pull(act_back)[0].astype(jnp.bfloat16)
    upper_back = jnp.einsum("secd,secf->edf", rows_in, pre_back, preferred_element_type=jnp.float32)
    upper_bias_back = jnp.sum(pre_back, axis=(0, 2), dtype=jnp.float32)
    rows_back_part = jnp.einsum(
        "secf,edf->secd", pre_back, upper, preferred_element_type=jnp.float32
    )
    return (upper_back, upper_bias_back, lower_back, lower_bias_back, rows_back_part)


def sum_shares(partial_out):
    return lax.psum_scatter(
        partial_out.astype(jnp.bfloat16), "tp", scatter_dimension=2, tiled=True
    ).astype(jnp.float32)


def send_home(block):
    return lax.all_to_all(block, "fsdp", split_axis=0, concat_axis=0, tiled=True)


def local(
    residual_in,
    out_cotangent,
    expert_index,
    document_index,
    piece_starts,
    first_norm_gain,
    first_norm_shift,
    input_weight,
    input_bias,
    output_weight,
    output_bias,
    second_norm_gain,
    second_norm_shift,
    expert_up,
    expert_up_bias,
    expert_down,
    expert_down_bias,
):
    width = residual_in.shape[1]
    fsdp_size = lax.axis_size("fsdp")
    residual = residual_in.astype(jnp.float32)
    first_normed, first_unit, first_inverse = layer_norm(
        residual, first_norm_gain, first_norm_shift
    )
    whole_normed, whole_docs = (
        lax.all_gather(first_normed.astype(jnp.bfloat16), "tp", axis=0, tiled=True),
        lax.all_gather(document_index, "tp", axis=1, tiled=True),
    )
    input_full, output_full, bias_full = (
        lax.all_gather(input_weight, "fsdp", axis=0, tiled=True),
        lax.all_gather(output_weight, "fsdp", axis=1, tiled=True),
        lax.all_gather(input_bias, "fsdp", axis=2, tiled=True),
    )
    docs = whole_docs[0]
    length = whole_normed.shape[0]
    local_width = input_full.shape[2]
    local_heads = local_width // HEAD_DIM
    projected = jnp.einsum(
        "sd,djc->sjc", whole_normed, input_full, preferred_element_type=jnp.float32
    )
    bias_flat = bias_full.reshape(2, local_width).astype(jnp.float32)
    queries = (
        ((projected[:, 0] + bias_flat[0]) * 0.125)
        .astype(jnp.bfloat16)
        .reshape(length, local_heads, HEAD_DIM)
    )
    keys = projected[:, 1].astype(jnp.bfloat16).reshape(length, local_heads, HEAD_DIM)
    values = (
        (projected[:, 2] + bias_flat[1]).astype(jnp.bfloat16).reshape(length, local_heads, HEAD_DIM)
    )
    labels = piece_labels(piece_starts[0], length)
    block_rows = min(512, length)
    blocks = length // block_rows

    def block_scores(first_row):
        query_block = lax.dynamic_slice_in_dim(queries, first_row, block_rows)
        scores = jnp.einsum("qhc,khc->hqk", query_block, keys, preferred_element_type=jnp.float32)
        allowed = block_mask(first_row, block_rows, docs, labels)
        return (query_block, jnp.where(allowed[None], scores, MASKED))

    def forward_block(block_number):
        query_block, scores = block_scores(block_number * block_rows)
        highest = jnp.max(scores, axis=-1, keepdims=True)
        weights = jnp.exp(scores - highest)
        total = jnp.sum(weights, axis=-1, keepdims=True)
        probs_low = (weights / total).astype(jnp.bfloat16)
        context_block = jnp.einsum(
            "hqk,khc->qhc", probs_low, values, preferred_element_type=jnp.float32
        )
        return (context_block.astype(jnp.bfloat16), (highest + jnp.log(total))[..., 0])

    contexts, log_totals = lax.map(forward_block, jnp.arange(blocks, dtype=jnp.int32))
    context = contexts.reshape(length, local_width)
    attention_part = jnp.dot(context, output_full, preferred_element_type=jnp.float32)
    attention_rows = lax.psum_scatter(
        attention_part.astype(jnp.bfloat16), "tp", scatter_dimension=0, tiled=True
    ).astype(jnp.float32)
    mixed = residual + attention_rows + output_bias
    second_normed, second_unit, second_inverse = layer_norm(
        mixed, second_norm_gain, second_norm_shift
    )
    choice_ids = expert_index[:, 0]
    rows_here = choice_ids.shape[0]
    experts_all = EXP_DEV * fsdp_size
    capacity = 2 * rows_here // experts_all
    row_order = jnp.arange(rows_here, dtype=jnp.int32)
    earlier = (choice_ids[:, None] == choice_ids[None, :]) & (
        row_order[None, :] < row_order[:, None]
    )
    rank = jnp.sum(earlier.astype(jnp.int32), axis=1)
    flat_slot = choice_ids * capacity + rank
    slot_rows = (
        jnp.zeros((experts_all * capacity, width), jnp.bfloat16)
        .at[flat_slot]
        .set(second_normed.astype(jnp.bfloat16))
    )
    slot_cotangent = (
        jnp.zeros((experts_all * capacity, width), jnp.bfloat16).at[flat_slot].set(out_cotangent)
    )
    sent_rows = slot_rows.reshape(fsdp_size, EXP_DEV, capacity, width)
    sent_cotangent = slot_cotangent.reshape(fsdp_size, EXP_DEV, capacity, width)
    got_rows, got_cotangent = (
        lax.all_to_all(sent_rows, "fsdp", split_axis=0, concat_axis=0, tiled=True),
        lax.all_to_all(sent_cotangent, "fsdp", split_axis=0, concat_axis=0, tiled=True),
    )
    rows_in, cotangent_rows = (
        lax.all_gather(got_rows, "tp", axis=2, tiled=True),
        lax.all_gather(got_cotangent, "tp", axis=2, tiled=True),
    )
    pre, act, partial_out = expert_forward(rows_in, expert_up, expert_up_bias, expert_down)
    summed = sum_shares(partial_out)
    returned = send_home((summed + expert_down_bias[None, :, None, :]).astype(jnp.bfloat16))
    upper_back, upper_bias_back, lower_back, lower_bias_back, rows_back_part = expert_backward(
        rows_in, cotangent_rows, pre, act, expert_up, expert_down
    )
    rows_back = send_home(sum_shares(rows_back_part).astype(jnp.bfloat16))
    expert_result = returned.reshape(-1, width)[flat_slot].astype(jnp.float32)
    block_output = (mixed + expert_result).astype(jnp.bfloat16)
    second_back = rows_back.reshape(-1, width)[flat_slot].astype(jnp.float32)
    cotangent = out_cotangent.astype(jnp.float32)
    mixed_back = cotangent + norm_back(second_back, second_unit, second_inverse, second_norm_gain)
    second_gain_back = jnp.sum(second_back * second_unit, axis=0)
    second_shift_back = jnp.sum(second_back, axis=0)
    output_bias_back = jnp.sum(mixed_back, axis=0)
    whole_back = lax.all_gather(mixed_back.astype(jnp.bfloat16), "tp", axis=0, tiled=True)
    output_weight_back = jnp.einsum(
        "sc,sd->cd", context, whole_back, preferred_element_type=jnp.float32
    )
    context_back = jnp.einsum(
        "sd,cd->sc", whole_back, output_full, preferred_element_type=jnp.float32
    )
    context_back = context_back.astype(jnp.bfloat16).reshape(length, local_heads, HEAD_DIM)

    def backward_block(carry, block_number):
        key_back, value_back = carry
        first_row = block_number * block_rows
        query_block, scores = block_scores(first_row)
        probs = jnp.exp(scores - log_totals[block_number][..., None])
        probs_low = probs.astype(jnp.bfloat16)
        context_block = lax.dynamic_slice_in_dim(context_back, first_row, block_rows)
        value_back = value_back + jnp.einsum(
            "hqk,qhc->khc", probs_low, context_block, preferred_element_type=jnp.float32
        )
        probs_back = jnp.einsum(
            "qhc,khc->hqk", context_block, values, preferred_element_type=jnp.float32
        )
        inner = jnp.sum(probs_back * probs, axis=-1, keepdims=True)
        scores_back = (probs * (probs_back - inner)).astype(jnp.bfloat16)
        query_back = jnp.einsum(
            "hqk,khc->qhc", scores_back, keys, preferred_element_type=jnp.float32
        )
        key_back = key_back + jnp.einsum(
            "hqk,qhc->khc", scores_back, query_block, preferred_element_type=jnp.float32
        )
        return ((key_back, value_back), query_back)

    empty = jnp.zeros((length, local_heads, HEAD_DIM), jnp.float32)
    (key_back, value_back), query_back = lax.scan(
        backward_block, (empty, empty), jnp.arange(blocks, dtype=jnp.int32)
    )
    query_low = query_back.reshape(length, local_width).astype(jnp.bfloat16) * jnp.bfloat16(0.125)
    projected_back = jnp.stack(
        [
            query_low,
            key_back.reshape(length, local_width).astype(jnp.bfloat16),
            value_back.reshape(length, local_width).astype(jnp.bfloat16),
        ],
        axis=1,
    )
    input_weight_back = jnp.einsum(
        "sd,sjc->djc", whole_normed, projected_back, preferred_element_type=jnp.float32
    )
    input_bias_back = jnp.stack(
        [
            jnp.sum(projected_back[:, 0], axis=0, dtype=jnp.float32),
            jnp.sum(projected_back[:, 2], axis=0, dtype=jnp.float32),
        ]
    ).reshape(2, local_heads, HEAD_DIM)
    first_back_part = jnp.einsum(
        "sjc,djc->sd", projected_back, input_full, preferred_element_type=jnp.float32
    )
    first_back = lax.psum_scatter(
        first_back_part.astype(jnp.bfloat16), "tp", scatter_dimension=0, tiled=True
    ).astype(jnp.float32)
    residual_back = mixed_back + norm_back(first_back, first_unit, first_inverse, first_norm_gain)
    first_gain_back = jnp.sum(first_back * first_unit, axis=0)
    first_shift_back = jnp.sum(first_back, axis=0)
    weight_shard, bias_shard, output_shard = (
        lax.psum_scatter(
            input_weight_back.astype(jnp.bfloat16), "fsdp", scatter_dimension=0, tiled=True
        ).astype(jnp.float32),
        lax.psum_scatter(
            input_bias_back.astype(jnp.bfloat16), "fsdp", scatter_dimension=2, tiled=True
        ).astype(jnp.float32),
        lax.psum_scatter(
            output_weight_back.astype(jnp.bfloat16), "fsdp", scatter_dimension=1, tiled=True
        ).astype(jnp.float32),
    )
    (
        first_gain_total,
        first_shift_total,
        second_gain_total,
        second_shift_total,
        output_bias_total,
    ) = lax.psum(
        (first_gain_back, first_shift_back, second_gain_back, second_shift_back, output_bias_back),
        ("fsdp", "tp"),
    )
    return (
        block_output,
        residual_back,
        first_gain_total,
        first_shift_total,
        weight_shard,
        bias_shard,
        output_shard,
        output_bias_total,
        second_gain_total,
        second_shift_total,
        upper_back,
        upper_bias_back,
        lower_back,
        lower_bias_back,
    )


def solution(mesh):
    in_specs = (
        P(("fsdp", "tp"), None),
        P(("fsdp", "tp"), None),
        P(("fsdp", "tp"), None),
        P("fsdp", "tp"),
        P("fsdp", None),
        P(),
        P(),
        P("fsdp", None, "tp"),
        P(None, "tp", "fsdp"),
        P("tp", "fsdp"),
        P(),
        P(),
        P(),
        P("fsdp", None, "tp"),
        P("fsdp", "tp"),
        P("fsdp", "tp", None),
        P("fsdp", None),
    )
    out_specs = (
        P(("fsdp", "tp"), None),
        P(("fsdp", "tp"), None),
        P(),
        P(),
        P("fsdp", None, "tp"),
        P(None, "tp", "fsdp"),
        P("tp", "fsdp"),
        P(),
        P(),
        P(),
        P("fsdp", None, "tp"),
        P("fsdp", "tp"),
        P("fsdp", "tp", None),
        P("fsdp", None),
    )
    return jax.shard_map(local, mesh=mesh, in_specs=in_specs, out_specs=out_specs, check_vma=False)
```

profile of v0, /device:TPU:9, one launch (start us, length us, event | category | flops | bytes accessed | tf_op | source)
XLA Modules:
  0.0 1045.7 jit_solution(7034967775080072151)
XLA Ops:
  15.6 21.8 %all_gather.27 = bf16[2,4,64]{1,0,2:T(2,128)(2,1)S(1)} all-gather(bf16[2,4,8]{1,0,2:T(2,128)(2,1)S(1)} %copy.68), channel_id=1, replica_groups=mesh['fsdp'=8,'tp'=4] {'fsdp'}, dimensions={2}, use_global_device_ids=true | all-gather | bytes 1152 | tf_op jit(solution)/shard_map/all_gather | solution.py:124
  37.6 11.8 %all_gather.24 = s32[1,2048]{1,0:T(1,128)S(1)} all-gather(s32[1,512]{1,0:T(1,128)S(1)} %copy-done.35), channel_id=1, replica_groups=mesh['fsdp'=8,'tp'=4] {'tp'}, dimensions={1}, use_global_device_ids=true | all-gather | bytes 10240 | tf_op jit(solution)/shard_map/all_gather | solution.py:119
  49.6 26.9 %all_gather.28 = bf16[256,1024]{1,0:T(8,128)(2,1)} all-gather(bf16[256,128]{1,0:T(8,128)(2,1)S(1)} %copy-done.21), channel_id=1, replica_groups=mesh['fsdp'=8,'tp'=4] {'fsdp'}, dimensions={1}, use_global_device_ids=true | all-gather | bytes 589824 | tf_op jit(solution)/shard_map/all_gather | solution.py:123
  76.5 17.4 %all-gather.6.cloned.1.call-done = bf16[2048,1024]{1,0:T(8,128)(2,1)} async-done(((bf16[512,1024]{1,0:T(8,128)(2,1)}), bf16[2048,1024]{1,0:T(8,128)(2,1)}) %all-gather.6.cloned.1.call-update) | async-done | bytes 4194320 | tf_op jit(solution)/shard_map/all_gather | solution.py:118
  100.7 65.7 %while.27 = (s32[]{:T(128)}, bf16[4,512,4,64]{1,3,2,0:T(8,128)(2,1)}, f32[4,4,512]{2,1,0:T(4,128)}, s32[4]{0:T(128)S(1)}, s32[2048]{0:T(1024)S(1)}, /*index=5*/s...) while((s32[]{:T(128)}, ...), condition=%wide.region_6.7_spmd, body=%wide.region_3.6_spmd.sunk | while | flops 1117912064 | bytes 57246944 | solution.py:164
  174.7 43.4 %reduce-scatter.10.cloned.1.call-done = bf16[512,1024]{1,0:T(8,128)(2,1)} async-done(((bf16[2048,1024]{1,0:T(8,128)(2,1)}), bf16[512,1024]{1,0:T(8,128)(2,1)}) %reduce-scatter.10.cloned.1.call-update) | async-done | bytes 1048592 | tf_op jit(solution)/shard_map/reduce_scatter | solution.py:167
  226.2 51.9 %all_to_all.20 = bf16[8,2,64,1024]{3,2,1,0:T(8,128)(2,1)S(1)} all-to-all(bf16[8,2,64,1024]{3,2,1,0:T(8,128)(2,1)} %bitcast.183), channel_id=1, replica_groups=mesh['fsdp'=8,'tp'=4] {'fsdp'}, dimensions={0} | all-to-all | bytes 4194304 | tf_op jit(solution)/shard_map/all_to_all | solution.py:195
  284.5 51.4 %all_to_all.21 = bf16[8,2,64,1024]{3,2,1,0:T(8,128)(2,1)S(1)} all-to-all(bf16[8,2,64,1024]{3,2,1,0:T(8,128)(2,1)} %bitcast.182), channel_id=1, replica_groups=mesh['fsdp'=8,'tp'=4] {'fsdp'}, dimensions={0} | all-to-all | bytes 4194304 | tf_op jit(solution)/shard_map/all_to_all | solution.py:196
  338.4 16.4 %fusion.50 = f32[2,8,256,1024]{3,2,1,0:T(8,128)} fusion(bf16[8,2,256,1024]{3,2,0,1:T(8,128)(2,1)} %all-gather.10.cloned.1.call-done, bf16[2,1024,1024]{2,1,0:T(8,128)(2,1)} %param.34), kind=kOutput, calls=%fused_computation.75 | convolution fusion | flops 8589934592 | bytes 29360128 | tf_op jit(solution)/shard_map/secd,edf->secf/dot_general | solution.py:56
  354.8 16.9 %convert_bitcast_fusion.1 = bf16[8,2,256,1024]{3,2,0,1:T(8,128)(2,1)} fusion(bf16[2,1024,1024]{2,1,0:T(8,128)(2,1)S(1)} %copy-done.37, f32[2,8,256,1024]{3,2,1,0:T(8,128)} %fusion.50, f32[2,1024]{1,0:T(2,128)S(1)} %copy-done.38), kind=kOutput, calls=%fused_computation.73 | convolution fusion | flops 8636071936 | bytes 29368320 | tf_op jit(solution)/shard_map/secf,efd->secd/dot_general | solution.py:60
  372.2 26.6 %all-gather.12.cloned.1.call-done = bf16[8,2,256,1024]{3,2,0,1:T(8,128)(2,1)} async-done(((bf16[8,2,64,1024]{3,2,0,1:T(8,128)(2,1)}), bf16[8,2,256,1024]{3,2,0,1:T(8,128)(2,1)}) %all-gather.12.cloned.1.call-update) | async-done | bytes 8388624 | tf_op jit(solution)/shard_map/all_gather | solution.py:200
  398.8 27.4 %convert_reduce_fusion.1 = (f32[2,1024]{1,0:T(2,128)}, bf16[8,2,256,1024]{3,2,0,1:T(8,128)(2,1)}) fusion(f32[2,8,256,1024]{3,2,1,0:T(8,128)} %fusion.50, f32[2,1024]{1,0:T(2,128)S(1)} %copy-done.38, bf16[8,2,256,1024]{3,2,0,1:T(8,128)(2,1)} %all-gather.12.cloned.1.call-done, bf16[2,1024,1024]{2,1,0:T(8,128)(2,1)} %param.36), kind=kOutput, calls=%fused_computation.70 | convolution fusion | flops 8686401536 | bytes 37765120 | tf_op jit(solution)/shard_map/secd,efd->secf/dot_general | solution.py:69
  426.2 14.7 %convert_bitcast_fusion = bf16[8,2,256,1024]{3,2,0,1:T(8,128)(2,1)} fusion(bf16[8,2,256,1024]{3,2,0,1:T(8,128)(2,1)} %get-tuple-element.262, bf16[2,1024,1024]{2,1,0:T(8,128)(2,1)} %param.34), kind=kOutput, calls=%fused_computation.72 | convolution fusion | flops 8594128896 | bytes 20971520 | tf_op jit(solution)/shard_map/secf,edf->secd/dot_general | solution.py:76
  441.0 31.8 %reduce-scatter.12.cloned.1.call-done = bf16[8,2,64,1024]{3,2,0,1:T(8,128)(2,1)} async-done(((bf16[8,2,256,1024]{3,2,0,1:T(8,128)(2,1)}), bf16[8,2,64,1024]{3,2,0,1:T(8,128)(2,1)}) %reduce-scatter.12.cloned.1.call-update) | async-done | bytes 2097168 | tf_op jit(solution)/shard_map/reduce_scatter | solution.py:83
  481.9 65.8 %reduce-scatter.14.cloned.1.call-done = bf16[8,2,64,1024]{3,2,0,1:T(8,128)(2,1)} async-done(((bf16[8,2,256,1024]{3,2,0,1:T(8,128)(2,1)}), bf16[8,2,64,1024]{3,2,0,1:T(8,128)(2,1)}) %reduce-scatter.14.cloned.1.call-update) | async-done | bytes 2097168 | tf_op jit(solution)/shard_map/reduce_scatter | solution.py:83
  561.7 41.2 %all-to-all-done.3 = bf16[8,2,64,1024]{3,2,1,0:T(8,128)(2,1)} async-done(((bf16[8,2,64,1024]{3,2,1,0:T(8,128)(2,1)}), bf16[8,2,64,1024]{3,2,1,0:T(8,128)(2,1)}, u32[]{:S(2)}, u32[]{:S(2)}) %all-to-all-start.3) | async-done | bytes 2097184 | tf_op jit(solution)/shard_map/all_to_all | solution.py:89
  617.9 34.9 %all-gather.14.cloned.1.call-done = bf16[2048,1024]{1,0:T(8,128)(2,1)} async-done(((bf16[512,1024]{1,0:T(8,128)(2,1)}), bf16[2048,1024]{1,0:T(8,128)(2,1)}) %all-gather.14.cloned.1.call-update) | async-done | bytes 4194320 | tf_op jit(solution)/shard_map/all_gather | solution.py:217
  661.8 202.4 %while.28 = (s32[]{:T(128)}, f32[2048,4,64]{0,2,1:T(8,128)}, f32[2048,4,64]{0,2,1:T(8,128)}, bf16[4,512,4,64]{1,3,2,0:T(8,128)(2,1)}, s32[4]{0:T(128)S(1)}, /*in...) while((s32[]{:T(128)}, f32[2048,4,64]{0,2,1:T(8,128)}, ...), condition=%wide.region_19.20_spmd.clone, body=%wide.region_17.19_spmd.clone.sunk | while | flops 2743073792 | bytes 185296384 | solution.py:250
  678.9 10.9 %multiply_reduce_fusion.3 = (f32[4,512]{1,0:T(4,128)}, f32[4,512,2048]{2,1,0:T(8,128)}) fusion(f32[4,512,2048]{2,1,0:T(8,128)S(1)} %fusion.161, f32[4,512]{1,0:T(4,128)S(1)} %dynamic-slice_bitcast_fusion.2, pred[512,2048]{1,0:T(8,128)(4,1)S(1)} %fusion.162, bf16[2048,4,64]{0,2,1:T(8,128)(2,1)} %get-tuple-element.513, ...), kind=kOutput, calls=%fused_computation.23.clone.1 | convolution fusion | flops 553646080 | bytes 35930116 | tf_op jit(solution)/shard_map/while/body/eval_jaxpr/qhc,khc->hqk/dot_general | solution.py:236
  689.8 10.6 %multiply_convert_fusion.3 = bf16[4,512,2048]{2,1,0:T(8,128)(2,1)} fusion(f32[4,512,2048]{2,1,0:T(8,128)} %get-tuple-element.421, f32[4,512,2048]{2,1,0:T(8,128)S(1)} %fusion.161, f32[4,512]{1,0:T(4,128)} %get-tuple-element.422, f32[4,512]{1,0:T(4,128)S(1)} %dynamic-slice_bitcast_fusion.2, pred[512,2048]{1,0:T(8,128)(4,1)S(1)} %fusion.162), kind=kLoop, calls=%fused_computation.22.clone.1 | loop fusion | flops 20971520 | bytes 43008000 | tf_op jit(solution)/shard_map/while/body/eval_jaxpr/convert_element_type | solution.py:240
  729.1 10.9 %multiply_reduce_fusion.3 = (f32[4,512]{1,0:T(4,128)}, f32[4,512,2048]{2,1,0:T(8,128)}) fusion(f32[4,512,2048]{2,1,0:T(8,128)S(1)} %fusion.161, f32[4,512]{1,0:T(4,128)S(1)} %dynamic-slice_bitcast_fusion.2, pred[512,2048]{1,0:T(8,128)(4,1)S(1)} %fusion.162, bf16[2048,4,64]{0,2,1:T(8,128)(2,1)} %get-tuple-element.513, ...), kind=kOutput, calls=%fused_computation.23.clone.1 | convolution fusion | flops 553646080 | bytes 35930116 | tf_op jit(solution)/shard_map/while/body/eval_jaxpr/qhc,khc->hqk/dot_general | solution.py:236
  740.0 10.6 %multiply_convert_fusion.3 = bf16[4,512,2048]{2,1,0:T(8,128)(2,1)} fusion(f32[4,512,2048]{2,1,0:T(8,128)} %get-tuple-element.421, f32[4,512,2048]{2,1,0:T(8,128)S(1)} %fusion.161, f32[4,512]{1,0:T(4,128)} %get-tuple-element.422, f32[4,512]{1,0:T(4,128)S(1)} %dynamic-slice_bitcast_fusion.2, pred[512,2048]{1,0:T(8,128)(4,1)S(1)} %fusion.162), kind=kLoop, calls=%fused_computation.22.clone.1 | loop fusion | flops 20971520 | bytes 43008000 | tf_op jit(solution)/shard_map/while/body/eval_jaxpr/convert_element_type | solution.py:240
  779.9 10.9 %multiply_reduce_fusion.3 = (f32[4,512]{1,0:T(4,128)}, f32[4,512,2048]{2,1,0:T(8,128)}) fusion(f32[4,512,2048]{2,1,0:T(8,128)S(1)} %fusion.161, f32[4,512]{1,0:T(4,128)S(1)} %dynamic-slice_bitcast_fusion.2, pred[512,2048]{1,0:T(8,128)(4,1)S(1)} %fusion.162, bf16[2048,4,64]{0,2,1:T(8,128)(2,1)} %get-tuple-element.513, ...), kind=kOutput, calls=%fused_computation.23.clone.1 | convolution fusion | flops 553646080 | bytes 35930116 | tf_op jit(solution)/shard_map/while/body/eval_jaxpr/qhc,khc->hqk/dot_general | solution.py:236
  790.8 10.6 %multiply_convert_fusion.3 = bf16[4,512,2048]{2,1,0:T(8,128)(2,1)} fusion(f32[4,512,2048]{2,1,0:T(8,128)} %get-tuple-element.421, f32[4,512,2048]{2,1,0:T(8,128)S(1)} %fusion.161, f32[4,512]{1,0:T(4,128)} %get-tuple-element.422, f32[4,512]{1,0:T(4,128)S(1)} %dynamic-slice_bitcast_fusion.2, pred[512,2048]{1,0:T(8,128)(4,1)S(1)} %fusion.162), kind=kLoop, calls=%fused_computation.22.clone.1 | loop fusion | flops 20971520 | bytes 43008000 | tf_op jit(solution)/shard_map/while/body/eval_jaxpr/convert_element_type | solution.py:240
  830.7 10.9 %multiply_reduce_fusion.3 = (f32[4,512]{1,0:T(4,128)}, f32[4,512,2048]{2,1,0:T(8,128)}) fusion(f32[4,512,2048]{2,1,0:T(8,128)S(1)} %fusion.161, f32[4,512]{1,0:T(4,128)S(1)} %dynamic-slice_bitcast_fusion.2, pred[512,2048]{1,0:T(8,128)(4,1)S(1)} %fusion.162, bf16[2048,4,64]{0,2,1:T(8,128)(2,1)} %get-tuple-element.513, ...), kind=kOutput, calls=%fused_computation.23.clone.1 | convolution fusion | flops 553646080 | bytes 35930116 | tf_op jit(solution)/shard_map/while/body/eval_jaxpr/qhc,khc->hqk/dot_general | solution.py:236
  841.6 10.6 %multiply_convert_fusion.3 = bf16[4,512,2048]{2,1,0:T(8,128)(2,1)} fusion(f32[4,512,2048]{2,1,0:T(8,128)} %get-tuple-element.421, f32[4,512,2048]{2,1,0:T(8,128)S(1)} %fusion.161, f32[4,512]{1,0:T(4,128)} %get-tuple-element.422, f32[4,512]{1,0:T(4,128)S(1)} %dynamic-slice_bitcast_fusion.2, pred[512,2048]{1,0:T(8,128)(4,1)S(1)} %fusion.162), kind=kLoop, calls=%fused_computation.22.clone.1 | loop fusion | flops 20971520 | bytes 43008000 | tf_op jit(solution)/shard_map/while/body/eval_jaxpr/convert_element_type | solution.py:240
  874.7 7.6 fusion.82
  896.4 16.1 %convolution_bitcast_fusion.3 = f32[2,1024,1024]{2,1,0:T(8,128)} fusion(bf16[8,2,256,1024]{3,2,0,1:T(8,128)(2,1)} %all-gather.10.cloned.1.call-done, bf16[8,2,256,1024]{3,2,0,1:T(8,128)(2,1)} %get-tuple-element.262), kind=kOutput, calls=%fused_computation.86 | convolution fusion | flops 8589934592 | bytes 25165824 | tf_op jit(solution)/shard_map/secd,secf->edf/dot_general | solution.py:74
  912.6 17.1 %convolution_bitcast_fusion.2 = f32[2,1024,1024]{2,1,0:T(8,128)} fusion(bf16[8,2,256,1024]{3,2,0,1:T(8,128)(2,1)S(1)} %bitcast.181, f32[2,8,256,1024]{3,2,1,0:T(8,128)} %fusion.50, f32[2,1024]{1,0:T(2,128)S(1)} %copy-done.39), kind=kOutput, calls=%fused_computation.85 | convolution fusion | flops 8631877632 | bytes 33562624 | tf_op jit(solution)/shard_map/secf,secd->efd/dot_general | solution.py:65
  929.7 16.0 %all-reduce = bf16[2,4,64]{2,1,0:T(4,128)(2,1)S(1)} all-reduce(bf16[2,4,64]{2,1,0:T(4,128)(2,1)S(1)} %pad_maximum_fusion.3), channel_id=7, replica_groups=mesh['fsdp'=8,'tp'=4] {'fsdp'}, use_global_device_ids=true, to_apply=%region_30.31.clone | all-reduce | flops 512 | bytes 2048
  949.6 44.2 %reduce-scatter.16.cloned.1.call-done = bf16[512,1024]{1,0:T(8,128)(2,1)} async-done(((bf16[2048,1024]{1,0:T(8,128)(2,1)}), bf16[512,1024]{1,0:T(8,128)(2,1)}) %reduce-scatter.16.cloned.1.call-update) | async-done | bytes 1048592 | tf_op jit(solution)/shard_map/reduce_scatter | solution.py:274
  996.2 39.5 %all-reduce.1 = (f32[1024]{0:T(1024)}, f32[1024]{0:T(1024)}, f32[1024]{0:T(1024)}, f32[1024]{0:T(1024)}, f32[1024]{0:T(1024)}) all-reduce(f32[1024]{0:T(1024)S(1)} %get-tuple-element.185, f32[1024]{0:T(1024)S(1)} %get-tuple-element.190, f32[1024]{0:T(1024)S(1)} %copy-done.31, ...), channel_id=1, replica_groups=mesh['fsdp'=8,'tp'=4] {'fsdp','tp'}, use_global_device_ids=true, to_apply=%region_24.25 | all-reduce | flops 5120 | bytes 40960 | tf_op jit(solution)/shard_map/psum | solution.py:297
  (303 shorter events, 289.7 us)
Async XLA Ops:
  7.2 30.4 %copy-start.35 = (s32[1,512]{1,0:T(1,128)S(1)}, s32[1,512]{1,0:T(1,128)}, u32[]{:S(2)}) copy-start(s32[1,512]{1,0:T(1,128)} %param.24) | copy-start | bytes 6148
  7.2 42.2 %copy-start.36 = (s32[1,2]{1,0:T(1,128)S(1)}, s32[1,2]{1,0:T(1,128)}, u32[]{:S(2)}) copy-start(s32[1,2]{1,0:T(1,128)} %param.25) | copy-start | bytes 28
  7.2 42.3 %copy-start.21 = (bf16[256,128]{1,0:T(8,128)(2,1)S(1)}, bf16[256,128]{1,0:T(8,128)(2,1)}, u32[]{:S(2)}) copy-start(bf16[256,128]{1,0:T(8,128)(2,1)} %param.30) | copy-start | bytes 196612
  7.2 69.2 %all-gather.8.cloned.1.call-start = ((), (), s32[]{:S(2)}) async-start(), calls=%async_computation.11 | async-start | bytes 1769472 | tf_op jit(solution)/shard_map/all_gather | solution.py:122
  9.0 84.9 %all-gather.6.cloned.1.call-start = ((), (), s32[]{:S(2)}) async-start(), calls=%async_computation.10 | async-start | bytes 5242880 | tf_op jit(solution)/shard_map/all_gather | solution.py:118
  15.5 202.6 %reduce-scatter.10.cloned.1.call-start = ((), (), s32[]{:S(2)}) async-start(), calls=%async_computation.12 | async-start | bytes 5242880 | tf_op jit(solution)/shard_map/reduce_scatter | solution.py:167
  173.8 44.3 %copy-start.3 = (bf16[512,1024]{1,0:T(8,128)(2,1)S(1)}, bf16[512,1024]{1,0:T(8,128)(2,1)}, u32[]{:S(2)}) copy-start(bf16[512,1024]{1,0:T(8,128)(2,1)} %param.21) | copy-start | bytes 3145732
  173.8 44.3 %copy-start.20 = (f32[1024]{0:T(1024)S(1)}, f32[1024]{0:T(1024)}, u32[]{:S(2)}) copy-start(f32[1024]{0:T(1024)} %param.31) | copy-start | bytes 12292
  173.8 47.9 %copy-start.24 = (f32[1024]{0:T(1024)S(1)}, f32[1024]{0:T(1024)}, u32[]{:S(2)}) copy-start(f32[1024]{0:T(1024)} %param.32) | copy-start | bytes 12292
  173.8 47.9 %copy-start.33 = (f32[1024]{0:T(1024)S(1)}, f32[1024]{0:T(1024)}, u32[]{:S(2)}) copy-start(f32[1024]{0:T(1024)} %param.33) | copy-start | bytes 12292
  173.8 164.6 %all-gather.10.cloned.1.call-start = ((), (), s32[]{:S(2)}) async-start(), calls=%async_computation.13 | async-start | bytes 10485760 | tf_op jit(solution)/shard_map/all_gather | solution.py:199
  279.6 119.2 %all-gather.12.cloned.1.call-start = ((), (), s32[]{:S(2)}) async-start(), calls=%async_computation.15 | async-start | bytes 10485760 | tf_op jit(solution)/shard_map/all_gather | solution.py:200
  337.4 135.4 %reduce-scatter.12.cloned.1.call-start = ((), (), s32[]{:S(2)}) async-start(), calls=%async_computation.14 | async-start | bytes 10485760 | tf_op jit(solution)/shard_map/reduce_scatter | solution.py:83
  371.8 175.9 %reduce-scatter.14.cloned.1.call-start = ((), (), s32[]{:S(2)}) async-start(), calls=%async_computation.16 | async-start | bytes 10485760 | tf_op jit(solution)/shard_map/reduce_scatter | solution.py:83
  441.0 31.8 %copy-start.32 = (f32[2,1024]{1,0:T(2,128)S(1)}, f32[2,1024]{1,0:T(2,128)}, u32[]{:S(2)}) copy-start(f32[2,1024]{1,0:T(2,128)} %param.37) | copy-start | bytes 24580
  476.4 74.4 %all-to-all-start.1 = ((bf16[8,2,64,1024]{3,2,1,0:T(8,128)(2,1)}), bf16[8,2,64,1024]{3,2,1,0:T(8,128)(2,1)}, u32[]{:S(2)}, u32[]{:S(2)}) async-start(bf16[8,2,64,1024]{3,2,1,0:T(8,128)(2,1)} %copy.73), calls=%async_computation.3 | async-start | bytes 4194304 | tf_op jit(solution)/shard_map/all_to_all | solution.py:89
  550.8 52.0 %all-to-all-start.3 = ((bf16[8,2,64,1024]{3,2,1,0:T(8,128)(2,1)}), bf16[8,2,64,1024]{3,2,1,0:T(8,128)(2,1)}, u32[]{:S(2)}, u32[]{:S(2)}) async-start(bf16[8,2,64,1024]{3,2,1,0:T(8,128)(2,1)} %copy.75), calls=%async_computation.6 | async-start | bytes 4194304 | tf_op jit(solution)/shard_map/all_to_all | solution.py:89
  556.3 96.5 %all-gather.14.cloned.1.call-start = ((), (), s32[]{:S(2)}) async-start(), calls=%async_computation.17 | async-start | bytes 5242880 | tf_op jit(solution)/shard_map/all_gather | solution.py:217
  615.3 37.5 %copy-start.11 = (bf16[32,8,4,512]{3,1,2,0:T(8,128)(2,1)S(1)}, bf16[32,8,4,512]{3,1,2,0:T(8,128)(2,1)}, u32[]{:S(2)}) copy-start(bf16[32,8,4,512]{3,1,2,0:T(8,128)(2,1)} %copy-done.10) | copy-start | bytes 3145732
  617.8 328.5 %reduce-scatter.20.cloned.1.call-start = ((), (), s32[]{:S(2)}) async-start(), calls=%async_computation.20 | async-start | bytes 589824
  617.9 39.5 %copy-start.13 = (bf16[256,1024]{1,0:T(8,128)(2,1)S(1)}, bf16[256,1024]{1,0:T(8,128)(2,1)}, u32[]{:S(2)}) copy-start(bf16[256,1024]{1,0:T(8,128)(2,1)} %all_gather.28) | copy-start | bytes 1572868
  657.3 290.6 %reduce-scatter.18.cloned.1.call-start = ((), (), s32[]{:S(2)}) async-start(), calls=%async_computation.19 | async-start | bytes 1769472 | tf_op jit(solution)/shard_map/reduce_scatter | solution.py:281
  882.3 111.5 %reduce-scatter.16.cloned.1.call-start = ((), (), s32[]{:S(2)}) async-start(), calls=%async_computation.18 | async-start | bytes 5242880 | tf_op jit(solution)/shard_map/reduce_scatter | solution.py:274
  890.6 21.9 %slice-start = ((s8[8388608]{0:T(1024)(128)(4,1)}), s8[4194304]{0:T(1024)(128)(4,1)S(1)}, s32[]{:S(2)}) async-start(s8[8388608]{0:T(1024)(128)(4,1)} %bitcast.180), calls=%async_computation.21 | async-start | bytes 8388608
  912.5 81.4 %copy-start.4 = (bf16[512,1024]{1,0:T(8,128)(2,1)S(1)}, bf16[512,1024]{1,0:T(8,128)(2,1)}, u32[]{:S(2)}) copy-start(bf16[512,1024]{1,0:T(8,128)(2,1)} %param.21) | copy-start | bytes 3145732
  912.5 81.4 %copy-start.23 = (f32[512]{0:T(512)S(1)}, f32[512]{0:T(512)}, u32[]{:S(2)}) copy-start(f32[512]{0:T(512)} %copy-done.22) | copy-start | bytes 6148
  912.5 81.4 %copy-start.25 = (f32[1024]{0:T(1024)S(1)}, f32[1024]{0:T(1024)}, u32[]{:S(2)}) copy-start(f32[1024]{0:T(1024)} %param.26) | copy-start | bytes 12292
  912.5 81.3 %copy-start.27 = (f32[512]{0:T(512)S(1)}, f32[512]{0:T(512)}, u32[]{:S(2)}) copy-start(f32[512]{0:T(512)} %copy-done.26) | copy-start | bytes 6148
  912.6 83.6 %copy-start.29 = (f32[1024]{0:T(1024)S(1)}, f32[1024]{0:T(1024)}, u32[]{:S(2)}) copy-start(f32[1024]{0:T(1024)} %get-tuple-element.183) | copy-start | bytes 12292
  912.6 83.6 %copy-start.30 = (f32[1024]{0:T(1024)S(1)}, f32[1024]{0:T(1024)}, u32[]{:S(2)}) copy-start(f32[1024]{0:T(1024)} %get-tuple-element.189) | copy-start | bytes 12292
  912.6 83.6 %copy-start.31 = (f32[1024]{0:T(1024)S(1)}, f32[1024]{0:T(1024)}, u32[]{:S(2)}) copy-start(f32[1024]{0:T(1024)} %get-tuple-element.250) | copy-start | bytes 12292
  929.7 106.0 %copy-start.9 = (f32[512,1024]{1,0:T(8,128)S(1)}, f32[512,1024]{1,0:T(8,128)}, u32[]{:S(2)}) copy-start(f32[512,1024]{1,0:T(8,128)} %copy-done.8) | copy-start | bytes 6291460
  (45 other events, 246.8 us)
Sparse Core Ops, SparseCore 0:
  10.7 45.8 all-gather.7
  58.7 35.1 all-gather.5
  173.9 44.1 reduce-scatter.9
  279.7 58.6 all-gather.9
  340.5 58.2 all-gather.11
  401.4 71.3 reduce-scatter.11
  475.9 71.7 reduce-scatter.13
  617.9 34.8 all-gather.13
  657.4 59.4 reduce-scatter.19
  882.5 63.4 reduce-scatter.17
  948.7 45.1 reduce-scatter.15
where the time goes:
time: 1060 us; the launch traced here: 1050 us
  matrix products  307 us (29%)
  waiting for transfers between devices  306 us (29%)
  blocking collectives  219 us (21%)
  other arithmetic  122 us (12%)
  local copies, waits for them, and re-layouts  49.4 us (5%)
  between operations  15.3 us (1%)
  loops' own time  14 us (1%)
  starting transfers between devices  12.2 us (1%)
    reduce_scatter x2, waiting for transfers between devices, sum_shares(): lax.psum_scatter(partial_out.astype(jnp.bfloat16), 'tp', scatter_dimensio...  97.6 us
    all_to_all x1, blocking collectives, local(): lax.all_to_all(sent_rows, 'fsdp', split_axis=0, concat_axis=0, tiled=True)  51.9 us
    all_to_all x1, blocking collectives, local(): lax.all_to_all(sent_cotangent, 'fsdp', split_axis=0, concat_axis=0, tiled...  51.4 us
    reduce_scatter x1, waiting for transfers between devices, local(): lax.psum_scatter(first_back_part.astype(jnp.bfloat16), 'tp', scatter_dime...  44.2 us
    dot_general x4, matrix products, backward_block(): jnp.einsum('qhc,khc->hqk', context_block, values, preferred_element_type=...  43.6 us
    reduce_scatter x1, waiting for transfers between devices, local(): lax.psum_scatter(attention_part.astype(jnp.bfloat16), 'tp', scatter_dimen...  43.4 us
    convert_element_type x4, other arithmetic, backward_block(): scores_back = (probs * (probs_back - inner)).astype(jnp.bfloat16)  42.4 us
    all_to_all x2, waiting for transfers between devices, send_home(): lax.all_to_all(block, 'fsdp', split_axis=0, concat_axis=0, tiled=True)  41.2 us
  transfers between devices with their start and end apart: 13, of which 9 were waited for; matrix products, arithmetic and copies ran while one was open for 35% of the time, Pallas kernels for 0%

commit v1 on v0

--- a/solution.py
+++ b/solution.py
@@ -1,11 +1,19 @@
+import functools
+
 import jax
 import jax.numpy as jnp
 from jax import lax
+from jax.experimental import pallas as pl
+from jax.experimental.pallas import tpu as pltpu
 from jax.sharding import PartitionSpec as P
 
+f32 = jnp.float32
+bf16 = jnp.bfloat16
 HEAD_DIM = 64
 EXP_DEV = 2
 PIECE = 256
+BLOCK_Q = 512
+BLOCK_K = 256
 
 
 EPSILON = 1e-05
@@ -33,22 +41,140 @@
     )
 
 
-def piece_labels(starts, length):
-    places = jnp.arange(length, dtype=jnp.int32)
-    inside = (places[None, :] >= starts[:, None]) & (places[None, :] < starts[:, None] + PIECE)
-    labels = jnp.arange(1, starts.shape[0] + 1, dtype=jnp.int32)
-    return jnp.sum(jnp.where(inside, labels[:, None], 0), axis=0)
-
-
-def block_mask(first_row, block_rows, docs, labels):
-    row_places = first_row + jnp.arange(block_rows, dtype=jnp.int32)
-    column_places = jnp.arange(docs.shape[0], dtype=jnp.int32)
-    row_docs = lax.dynamic_slice_in_dim(docs, first_row, block_rows)
-    row_labels = lax.dynamic_slice_in_dim(labels, first_row, block_rows)
-    same_doc = row_docs[:, None] == docs[None, :]
-    causal = column_places[None, :] <= row_places[:, None]
-    same_piece = (row_labels[:, None] == labels[None, :]) & (row_labels[:, None] > 0)
-    return same_doc & (causal | same_piece)
+def half_rows(x, h):
+    rows = lax.broadcasted_iota(jnp.int32, x.shape, 0)
+    keep = (rows < 64) if h == 0 else (rows >= 64)
+    return jnp.where(keep, x, jnp.zeros_like(x))
+
+def half_lanes(x, h):
+    lanes = lax.broadcasted_iota(jnp.int32, x.shape, 1)
+    keep = (lanes < 64) if h == 0 else (lanes >= 64)
+    return jnp.where(keep, x, jnp.zeros_like(x))
+
+def attend_kernel(bk, lo_ref, hi_ref, q_ref, k_ref, v_ref, a_ref, b_ref, o_ref, lse_ref, vt, ):
+    i = pl.program_id(1)
+    bq = q_ref.shape[0]
+    @pl.when(i == 0)
+    def _():
+        vt[...] = v_ref[...].T
+    qt = q_ref[...].T
+    qz = [half_rows(qt, h) for h in (0, 1)]
+    a = a_ref[...]; b = b_ref[...]
+    def body(kb, carry):
+        base = pl.multiple_of(kb * bk, bk)
+        kblk = k_ref[pl.ds(base, bk), :]
+        j = base + lax.broadcasted_iota(jnp.int32, (bk, bq), 0)
+        mask = (j >= a) & (j <= b)
+        out = []
+        for h in (0, 1):
+            m, l, acc = carry[h]
+            s = jnp.dot(kblk, qz[h], preferred_element_type=f32)
+            s = jnp.where(mask, s, MASKED)
+            mn = jnp.maximum(m, jnp.max(s, axis=0, keepdims=True))
+            p = jnp.exp(s - mn)
+            al = jnp.exp(m - mn)
+            l = al * l + jnp.sum(p, axis=0, keepdims=True)
+            acc = acc * al + jnp.dot(vt[pl.ds(64 * h, 64), pl.ds(base, bk)], p.astype(bf16), preferred_element_type=f32)
+            out.append((mn, l, acc))
+        return tuple(out)
+    init = tuple((jnp.full((1, bq), MASKED, f32), jnp.zeros((1, bq), f32), jnp.zeros((64, bq), f32)) for _ in (0, 1))
+    res = lax.fori_loop(lo_ref[i], hi_ref[i], body, init)
+    ot = jnp.concatenate([acc / l for m, l, acc in res], axis=0)
+    o_ref[...] = ot.T.astype(bf16)
+    lse_ref[...] = jnp.concatenate([m + jnp.log(l) for m, l, acc in res] + [jnp.zeros((6, bq), f32)], axis=0)
+
+def attention_fwd(q, k, v, a, b, lo, hi, bq, bk):
+    S, W = q.shape
+    n = S // bq
+    return pl.pallas_call(
+        functools.partial(attend_kernel, bk),
+        grid_spec=pltpu.PrefetchScalarGridSpec(
+            num_scalar_prefetch=2, grid=(W // 128, n),
+            in_specs=[pl.BlockSpec((bq, 128), lambda p, i, *_: (i, p)),
+                      pl.BlockSpec((S, 128), lambda p, i, *_: (0, p)),
+                      pl.BlockSpec((S, 128), lambda p, i, *_: (0, p)),
+                      pl.BlockSpec((1, bq), lambda p, i, *_: (0, i)),
+                      pl.BlockSpec((1, bq), lambda p, i, *_: (0, i))],
+            out_specs=[pl.BlockSpec((bq, 128), lambda p, i, *_: (i, p)),
+                       pl.BlockSpec((8, bq), lambda p, i, *_: (p, i))],
+            scratch_shapes=[pltpu.VMEM((128, S), bf16)]),
+        out_shape=[jax.ShapeDtypeStruct((S, W), bf16), jax.ShapeDtypeStruct((W // 16, S), f32)],
+        compiler_params=pltpu.CompilerParams(vmem_limit_bytes=40 << 20),
+    )(lo, hi, q, k, v, a, b)
+
+def attend_back_kernel(bk, lo_ref, hi_ref, q_ref, k_ref, v_ref, do_ref, o_ref, lse_ref, a_ref, b_ref, dq_ref, dk_ref, dv_ref, kt, dk_acc, dv_acc):
+    i = pl.program_id(1)
+    bq = q_ref.shape[0]
+    @pl.when(i == 0)
+    def _():
+        kt[...] = k_ref[...].T
+        dk_acc[...] = jnp.zeros_like(dk_acc)
+        dv_acc[...] = jnp.zeros_like(dv_acc)
+    q = q_ref[...]; do = do_ref[...]
+    qt = q.T; dot_ = do.T
+    qz = [half_rows(qt, h) for h in (0, 1)]
+    dz = [half_rows(dot_, h) for h in (0, 1)]
+    qcat = jnp.concatenate([half_lanes(q, 0), half_lanes(q, 1)], axis=0)
+    dcat = jnp.concatenate([half_lanes(do, 0), half_lanes(do, 1)], axis=0)
+    prod = (do.astype(f32) * o_ref[...].astype(f32)).T
+    delta = [jnp.sum(prod[:64], axis=0, keepdims=True), jnp.sum(prod[64:], axis=0, keepdims=True)]
+    lse = [lse_ref[0:1, :], lse_ref[1:2, :]]
+    a = a_ref[...]; b = b_ref[...]
+    def body(kb, carry):
+        base = pl.multiple_of(kb * bk, bk)
+        kblk = k_ref[pl.ds(base, bk), :]
+        vblk = v_ref[pl.ds(base, bk), :]
+        j = base + lax.broadcasted_iota(jnp.int32, (bk, bq), 0)
+        mask = (j >= a) & (j <= b)
+        ps, dss, out = [], [], []
+        for h in (0, 1):
+            s = jnp.dot(kblk, qz[h], preferred_element_type=f32)
+            p = jnp.exp(jnp.where(mask, s - lse[h], MASKED))
+            dp = jnp.dot(vblk, dz[h], preferred_element_type=f32)
+            ds = (p * (dp - delta[h])).astype(bf16)
+            ps.append(p.astype(bf16)); dss.append(ds)
+            out.append(carry[h] + jnp.dot(kt[pl.ds(64 * h, 64), pl.ds(base, bk)], ds, preferred_element_type=f32))
+        dv_acc[pl.ds(base, bk), :] += jnp.dot(jnp.concatenate(ps, axis=1), dcat, preferred_element_type=f32)
+        dk_acc[pl.ds(base, bk), :] += jnp.dot(jnp.concatenate(dss, axis=1), qcat, preferred_element_type=f32)
+        return tuple(out)
+    init = tuple(jnp.zeros((64, bq), f32) for _ in (0, 1))
+    dqt = lax.fori_loop(lo_ref[i], hi_ref[i], body, init)
+    dq_ref[...] = (jnp.concatenate(dqt, axis=0).T * 0.125).astype(bf16)
+    @pl.when(i == pl.num_programs(1) - 1)
+    def _():
+        dk_ref[...] = dk_acc[...].astype(bf16)
+        dv_ref[...] = dv_acc[...].astype(bf16)
+
+def attention_bwd(q, k, v, do, o, lse, a, b, lo, hi, bq, bk):
+    S, W = q.shape
+    n = S // bq
+    qs = pl.BlockSpec((bq, 128), lambda p, i, *_: (i, p))
+    ks = pl.BlockSpec((S, 128), lambda p, i, *_: (0, p))
+    rs = pl.BlockSpec((1, bq), lambda p, i, *_: (0, i))
+    return pl.pallas_call(
+        functools.partial(attend_back_kernel, bk),
+        grid_spec=pltpu.PrefetchScalarGridSpec(
+            num_scalar_prefetch=2, grid=(W // 128, n),
+            in_specs=[qs, ks, ks, qs, qs, pl.BlockSpec((8, bq), lambda p, i, *_: (p, i)), rs, rs],
+            out_specs=[qs, ks, ks],
+            scratch_shapes=[pltpu.VMEM((128, S), bf16), pltpu.VMEM((S, 128), f32), pltpu.VMEM((S, 128), f32)]),
+        out_shape=[jax.ShapeDtypeStruct((S, W), bf16)] * 3,
+        compiler_params=pltpu.CompilerParams(vmem_limit_bytes=40 << 20),
+    )(lo, hi, q, k, v, do, o, lse, a, b)
+
+def intervals(docs, starts, piece):
+    S = docs.shape[0]
+    pos = jnp.arange(S, dtype=jnp.int32)
+    first = jnp.sum((docs[None, :] < docs[:, None]).astype(jnp.int32), axis=1)
+    last = jnp.sum((docs[None, :] <= docs[:, None]).astype(jnp.int32), axis=1) - 1
+    inside = (pos[None, :] >= starts[:, None]) & (pos[None, :] < starts[:, None] + piece)
+    piece_last = jnp.max(jnp.where(inside, starts[:, None] + piece - 1, -1), axis=0)
+    end = jnp.maximum(pos, jnp.minimum(piece_last, last))
+    return first, end
+def ranges(first, end, bq, bk):
+    lo = first[::bq] // bk
+    hi = jnp.max(end.reshape(-1, bq), axis=1) // bk + 1
+    return lo, hi
 
 
 def expert_forward(rows_in, upper, upper_bias, lower):
@@ -131,38 +257,14 @@
         "sd,djc->sjc", whole_normed, input_full, preferred_element_type=jnp.float32
     )
     bias_flat = bias_full.reshape(2, local_width).astype(jnp.float32)
-    queries = (
-        ((projected[:, 0] + bias_flat[0]) * 0.125)
-        .astype(jnp.bfloat16)
-        .reshape(length, local_heads, HEAD_DIM)
-    )
-    keys = projected[:, 1].astype(jnp.bfloat16).reshape(length, local_heads, HEAD_DIM)
-    values = (
-        (projected[:, 2] + bias_flat[1]).astype(jnp.bfloat16).reshape(length, local_heads, HEAD_DIM)
-    )
-    labels = piece_labels(piece_starts[0], length)
-    block_rows = min(512, length)
-    blocks = length // block_rows
-
-    def block_scores(first_row):
-        query_block = lax.dynamic_slice_in_dim(queries, first_row, block_rows)
-        scores = jnp.einsum("qhc,khc->hqk", query_block, keys, preferred_element_type=jnp.float32)
-        allowed = block_mask(first_row, block_rows, docs, labels)
-        return (query_block, jnp.where(allowed[None], scores, MASKED))
-
-    def forward_block(block_number):
-        query_block, scores = block_scores(block_number * block_rows)
-        highest = jnp.max(scores, axis=-1, keepdims=True)
-        weights = jnp.exp(scores - highest)
-        total = jnp.sum(weights, axis=-1, keepdims=True)
-        probs_low = (weights / total).astype(jnp.bfloat16)
-        context_block = jnp.einsum(
-            "hqk,khc->qhc", probs_low, values, preferred_element_type=jnp.float32
-        )
-        return (context_block.astype(jnp.bfloat16), (highest + jnp.log(total))[..., 0])
-
-    contexts, log_totals = lax.map(forward_block, jnp.arange(blocks, dtype=jnp.int32))
-    context = contexts.reshape(length, local_width)
+    queries = ((projected[:, 0] + bias_flat[0]) * 0.125).astype(bf16)
+    keys = projected[:, 1].astype(bf16)
+    values = (projected[:, 2] + bias_flat[1]).astype(bf16)
+    first, end = intervals(docs, piece_starts[0], PIECE)
+    lows, highs = ranges(first, end, BLOCK_Q, BLOCK_K)
+    context, log_totals = attention_fwd(
+        queries, keys, values, first[None], end[None], lows, highs, BLOCK_Q, BLOCK_K
+    )
     attention_part = jnp.dot(context, output_full, preferred_element_type=jnp.float32)
     attention_rows = lax.psum_scatter(
         attention_part.astype(jnp.bfloat16), "tp", scatter_dimension=0, tiled=True
@@ -221,44 +323,11 @@
     context_back = jnp.einsum(
         "sd,cd->sc", whole_back, output_full, preferred_element_type=jnp.float32
     )
-    context_back = context_back.astype(jnp.bfloat16).reshape(length, local_heads, HEAD_DIM)
-
-    def backward_block(carry, block_number):
-        key_back, value_back = carry
-        first_row = block_number * block_rows
-        query_block, scores = block_scores(first_row)
-        probs = jnp.exp(scores - log_totals[block_number][..., None])
-        probs_low = probs.astype(jnp.bfloat16)
-        context_block = lax.dynamic_slice_in_dim(context_back, first_row, block_rows)
-        value_back = value_back + jnp.einsum(
-            "hqk,qhc->khc", probs_low, context_block, preferred_element_type=jnp.float32
-        )
-        probs_back = jnp.einsum(
-            "qhc,khc->hqk", context_block, values, preferred_element_type=jnp.float32
-        )
-        inner = jnp.sum(probs_back * probs, axis=-1, keepdims=True)
-        scores_back = (probs * (probs_back - inner)).astype(jnp.bfloat16)
-        query_back = jnp.einsum(
-            "hqk,khc->qhc", scores_back, keys, preferred_element_type=jnp.float32
-        )
-        key_back = key_back + jnp.einsum(
-            "hqk,qhc->khc", scores_back, query_block, preferred_element_type=jnp.float32
-        )
-        return ((key_back, value_back), query_back)
-
-    empty = jnp.zeros((length, local_heads, HEAD_DIM), jnp.float32)
-    (key_back, value_back), query_back = lax.scan(
-        backward_block, (empty, empty), jnp.arange(blocks, dtype=jnp.int32)
-    )
-    query_low = query_back.reshape(length, local_width).astype(jnp.bfloat16) * jnp.bfloat16(0.125)
-    projected_back = jnp.stack(
-        [
-            query_low,
-            key_back.reshape(length, local_width).astype(jnp.bfloat16),
-            value_back.reshape(length, local_width).astype(jnp.bfloat16),
-        ],
-        axis=1,
-    )
+    query_low, key_low, value_low = attention_bwd(
+        queries, keys, values, context_back.astype(bf16), context, log_totals,
+        first[None], end[None], lows, highs, BLOCK_Q, BLOCK_K,
+    )
+    projected_back = jnp.stack([query_low, key_low, value_low], axis=1)
     input_weight_back = jnp.einsum(
         "sd,sjc->djc", whole_normed, projected_back, preferred_element_type=jnp.float32
     )

time: 1060 us -> 858 us (0.81)
  matrix products: 307 us -> 138 us
  other arithmetic: 122 us -> 45.5 us
  Pallas kernels: 0 us -> 55.7 us
  waiting for transfers between devices: 306 us -> 326 us
  local copies, waits for them, and re-layouts: 49.4 us -> 32.8 us
  loops' own time: 14 us -> 0 us
    dot_general x28 -> x0, matrix products: 168 us -> none  [the longest x4 43.6 us: backward_block(): jnp.einsum('qhc,khc->hqk', context_block, values, preferred_element_type=...]
    pallas_call x0 -> x2, Pallas kernels: none -> 55.7 us  [the longest x1 32 us: attention_bwd(): pl.pallas_call(functools.partial(attend_back_kernel, bk), grid_spec=pltpu...]
    convert_element_type x6 -> x1, other arithmetic: 44.5 us -> 0.42 us  [local(): values = (projected[:, 2] + bias_flat[1]).astype(bf16)]
    and x8 -> x0, other arithmetic: 16.8 us -> none  [block_mask(): return same_doc & (causal | same_piece)]
    another operation x2 -> x0, loops' own time: 14 us -> none  [the longest x1 11.2 us: local(): lax.scan(backward_block, (empty, empty), jnp.arange(blocks, dtype=jnp.int...]
    reduce_scatter x1, waiting for transfers between devices: 0.01 us -> 11.8 us  [local(): lax.psum_scatter(input_weight_back.astype(jnp.bfloat16), 'fsdp', scatter_...]
    reduce_sum x5 -> x1, other arithmetic: 15.6 us -> 4.13 us  [intervals(): jnp.sum((docs[None, :] <= docs[:, None]).astype(jnp.int32), axis=1) - 1]
  transfers between devices with their start and end apart: 13 -> 13, of which waited for: 9 -> 10; matrix products, arithmetic and copies ran while one was open for 35% -> 19% of each run, Pallas kernels for 0% -> 4%
where the time goes in v1:
time: 858 us; the launch traced here: 845 us
  waiting for transfers between devices  326 us (38%)
  blocking collectives  220 us (26%)
  matrix products  138 us (16%)
  Pallas kernels  55.7 us (6%)
  other arithmetic  45.5 us (5%)
  local copies, waits for them, and re-layouts  32.8 us (4%)
  between operations  15.4 us (2%)
  starting transfers between devices  12 us (1%)
    reduce_scatter x2, waiting for transfers between devices, sum_shares(): lax.psum_scatter(partial_out.astype(jnp.bfloat16), 'tp', scatter_dimensio...  97.5 us
    all_to_all x1, blocking collectives, local(): lax.all_to_all(sent_rows, 'fsdp', split_axis=0, concat_axis=0, tiled=True)  51.9 us
    all_to_all x1, blocking collectives, local(): lax.all_to_all(sent_cotangent, 'fsdp', split_axis=0, concat_axis=0, tiled...  51.4 us
    reduce_scatter x1, waiting for transfers between devices, local(): lax.psum_scatter(attention_part.astype(jnp.bfloat16), 'tp', scatter_dimen...  47.7 us
    reduce_scatter x1, waiting for transfers between devices, local(): lax.psum_scatter(first_back_part.astype(jnp.bfloat16), 'tp', scatter_dime...  46.3 us
    all_to_all x2, waiting for transfers between devices, send_home(): lax.all_to_all(block, 'fsdp', split_axis=0, concat_axis=0, tiled=True)  41.2 us
    psum x1, blocking collectives, local(): lax.psum((first_gain_back, first_shift_back, second_gain_back, second_shi...  39.5 us
    all_gather x1, waiting for transfers between devices, local(): lax.all_gather(mixed_back.astype(jnp.bfloat16), 'tp', axis=0, tiled=True)  35 us
  transfers between devices with their start and end apart: 13, of which 10 were waited for; matrix products, arithmetic and copies ran while one was open for 19% of the time, Pallas kernels for 4%

profile of v1, /device:TPU:9, one launch (start us, length us, event | category | flops | bytes accessed | tf_op | source)
XLA Modules:
  0.0 845.3 jit_solution(13245869654531608935)
XLA Ops:
  14.0 5.6 all_gather.24
  24.0 22.6 %all_gather.27 = bf16[2,4,64]{1,0,2:T(2,128)(2,1)S(1)} all-gather(bf16[2,4,8]{1,0,2:T(2,128)(2,1)S(1)} %copy.55), channel_id=1, replica_groups=mesh['fsdp'=8,'tp'=4] {'fsdp'}, dimensions={2}, use_global_device_ids=true | all-gather | bytes 1152 | tf_op jit(solution)/shard_map/all_gather | solution.py:250
  47.1 26.6 %all_gather.28 = bf16[256,1024]{1,0:T(8,128)(2,1)} all-gather(bf16[256,128]{1,0:T(8,128)(2,1)S(1)} %copy-done.15), channel_id=1, replica_groups=mesh['fsdp'=8,'tp'=4] {'fsdp'}, dimensions={1}, use_global_device_ids=true | all-gather | bytes 589824 | tf_op jit(solution)/shard_map/all_gather | solution.py:249
  73.8 18.4 %all-gather.6.cloned.1.call-done = bf16[2048,1024]{1,0:T(8,128)(2,1)} async-done(((bf16[512,1024]{1,0:T(8,128)(2,1)}), bf16[2048,1024]{1,0:T(8,128)(2,1)}) %all-gather.6.cloned.1.call-update) | async-done | bytes 4194320 | tf_op jit(solution)/shard_map/all_gather | solution.py:244
  92.2 5.6 fusion.18
  98.4 23.7 %shard_map.272 = (bf16[2048,256]{1,0:T(8,128)(2,1)S(1)}, f32[16,2048]{1,0:T(8,128)S(1)}) custom-call(s32[4]{0:T(128)S(1)} %get-tuple-element.50.lo_ref, s32[4]{0:T(128)S(1)} %get-tuple-element.51.hi_ref, bf16[2048,256]{1,0:T(8,128)(2,1)S(1)} %get-tuple-element.42.q_ref, bf16[2048,256]{1,0:T(8,128)(2,1)S(1)} %fusion.53.k_ref, ...), custom_call_target="tpu_custom_call" | custom-call | tf_op jit(solution)/shard_map/pallas_call | solution.py:89
  127.3 47.7 %reduce-scatter.10.cloned.1.call-done = bf16[512,1024]{1,0:T(8,128)(2,1)} async-done(((bf16[2048,1024]{1,0:T(8,128)(2,1)}), bf16[512,1024]{1,0:T(8,128)(2,1)}) %reduce-scatter.10.cloned.1.call-update) | async-done | bytes 1048592 | tf_op jit(solution)/shard_map/reduce_scatter | solution.py:269
  179.1 5.7 scatter_custom_fusion
  184.9 51.9 %all_to_all.20 = bf16[8,2,64,1024]{3,2,1,0:T(8,128)(2,1)S(1)} all-to-all(bf16[8,2,64,1024]{3,2,1,0:T(8,128)(2,1)} %bitcast.127), channel_id=1, replica_groups=mesh['fsdp'=8,'tp'=4] {'fsdp'}, dimensions={0} | all-to-all | bytes 4194304 | tf_op jit(solution)/shard_map/all_to_all | solution.py:297
  243.1 51.4 %all_to_all.21 = bf16[8,2,64,1024]{3,2,1,0:T(8,128)(2,1)S(1)} all-to-all(bf16[8,2,64,1024]{3,2,1,0:T(8,128)(2,1)} %bitcast.128), channel_id=1, replica_groups=mesh['fsdp'=8,'tp'=4] {'fsdp'}, dimensions={0} | all-to-all | bytes 4194304 | tf_op jit(solution)/shard_map/all_to_all | solution.py:298
  297.1 16.4 %fusion.12 = f32[2,8,256,1024]{3,2,1,0:T(8,128)} fusion(bf16[8,2,256,1024]{3,2,0,1:T(8,128)(2,1)} %all-gather.10.cloned.1.call-done, bf16[2,1024,1024]{2,1,0:T(8,128)(2,1)} %param.30), kind=kOutput, calls=%fused_computation.28 | convolution fusion | flops 8589934592 | bytes 29360128 | tf_op jit(solution)/shard_map/secd,edf->secf/dot_general | solution.py:182
  313.5 17.0 %convert_bitcast_fusion.1 = bf16[8,2,256,1024]{3,2,0,1:T(8,128)(2,1)} fusion(bf16[2,1024,1024]{2,1,0:T(8,128)(2,1)S(1)} %copy-done.28, f32[2,8,256,1024]{3,2,1,0:T(8,128)} %fusion.12, f32[2,1024]{1,0:T(2,128)S(1)} %copy-done.31), kind=kOutput, calls=%fused_computation.26 | convolution fusion | flops 8636071936 | bytes 29368320 | tf_op jit(solution)/shard_map/secf,efd->secd/dot_general | solution.py:186
  331.0 26.5 %all-gather.12.cloned.1.call-done = bf16[8,2,256,1024]{3,2,0,1:T(8,128)(2,1)} async-done(((bf16[8,2,64,1024]{3,2,0,1:T(8,128)(2,1)}), bf16[8,2,256,1024]{3,2,0,1:T(8,128)(2,1)}) %all-gather.12.cloned.1.call-update) | async-done | bytes 8388624 | tf_op jit(solution)/shard_map/all_gather | solution.py:302
  357.5 27.4 %convert_reduce_fusion.1 = (f32[2,1024]{1,0:T(2,128)}, bf16[8,2,256,1024]{3,2,0,1:T(8,128)(2,1)}) fusion(f32[2,8,256,1024]{3,2,1,0:T(8,128)} %fusion.12, f32[2,1024]{1,0:T(2,128)S(1)} %copy-done.31, bf16[8,2,256,1024]{3,2,0,1:T(8,128)(2,1)} %all-gather.12.cloned.1.call-done, bf16[2,1024,1024]{2,1,0:T(8,128)(2,1)} %param.32), kind=kOutput, calls=%fused_computation.21 | convolution fusion | flops 8686401536 | bytes 37765120 | tf_op jit(solution)/shard_map/secd,efd->secf/dot_general | solution.py:195
  384.9 14.7 %convert_bitcast_fusion = bf16[8,2,256,1024]{3,2,0,1:T(8,128)(2,1)} fusion(bf16[8,2,256,1024]{3,2,0,1:T(8,128)(2,1)} %get-tuple-element.49, bf16[2,1024,1024]{2,1,0:T(8,128)(2,1)} %param.30), kind=kOutput, calls=%fused_computation.25 | convolution fusion | flops 8594128896 | bytes 20971520 | tf_op jit(solution)/shard_map/secf,edf->secd/dot_general | solution.py:202
  399.7 31.8 %reduce-scatter.12.cloned.1.call-done = bf16[8,2,64,1024]{3,2,0,1:T(8,128)(2,1)} async-done(((bf16[8,2,256,1024]{3,2,0,1:T(8,128)(2,1)}), bf16[8,2,64,1024]{3,2,0,1:T(8,128)(2,1)}) %reduce-scatter.12.cloned.1.call-update) | async-done | bytes 2097168 | tf_op jit(solution)/shard_map/reduce_scatter | solution.py:209
  435.1 5.5 all-to-all-start.1
  440.6 65.7 %reduce-scatter.14.cloned.1.call-done = bf16[8,2,64,1024]{3,2,0,1:T(8,128)(2,1)} async-done(((bf16[8,2,256,1024]{3,2,0,1:T(8,128)(2,1)}), bf16[8,2,64,1024]{3,2,0,1:T(8,128)(2,1)}) %reduce-scatter.14.cloned.1.call-update) | async-done | bytes 2097168 | tf_op jit(solution)/shard_map/reduce_scatter | solution.py:209
  509.5 5.5 all-to-all-start.3
  515.0 5.3 gather_fusion
  520.3 41.2 %all-to-all-done.3 = bf16[8,2,64,1024]{3,2,1,0:T(8,128)(2,1)} async-done(((bf16[8,2,64,1024]{3,2,1,0:T(8,128)(2,1)}), bf16[8,2,64,1024]{3,2,1,0:T(8,128)(2,1)}, u32[]{:S(2)}, u32[]{:S(2)}) %all-to-all-start.3) | async-done | bytes 2097184 | tf_op jit(solution)/shard_map/all_to_all | solution.py:215
  561.5 5.3 gather_fusion.1
  576.0 35.0 %all-gather.14.cloned.1.call-done = bf16[2048,1024]{1,0:T(8,128)(2,1)} async-done(((bf16[512,1024]{1,0:T(8,128)(2,1)}), bf16[2048,1024]{1,0:T(8,128)(2,1)}) %all-gather.14.cloned.1.call-update) | async-done | bytes 4194320 | tf_op jit(solution)/shard_map/all_gather | solution.py:319
  621.6 32.0 %shard_map.273 = (bf16[2048,256]{1,0:T(8,128)(2,1)S(1)}, bf16[2048,256]{1,0:T(8,128)(2,1)S(1)}, bf16[2048,256]{1,0:T(8,128)(2,1)S(1)}) custom-call(s32[4]{0:T(128)S(1)} %get-tuple-element.50.lo_ref, s32[4]{0:T(128)S(1)} %get-tuple-element.51.hi_ref, bf16[2048,256]{1,0:T(8,128)(2,1)S(1)} %get-tuple-element.42.q_ref, bf16[2048,256]{1,0:T(8,128)(2,1)S(1)} %fusion.53.k_ref, ...), custom_call_target="tpu_custom_call" | custom-call | tf_op jit(solution)/shard_map/pallas_call | solution.py:154
  660.0 7.0 bitcast_convert_fusion
  668.9 5.8 convert_reduce_fusion
  674.7 15.9 %convolution_bitcast_fusion.1 = f32[2,1024,1024]{2,1,0:T(8,128)} fusion(bf16[8,2,256,1024]{3,2,0,1:T(8,128)(2,1)} %all-gather.10.cloned.1.call-done, bf16[8,2,256,1024]{3,2,0,1:T(8,128)(2,1)} %get-tuple-element.49), kind=kOutput, calls=%fused_computation.39 | convolution fusion | flops 8589934592 | bytes 25165824 | tf_op jit(solution)/shard_map/secd,secf->edf/dot_general | solution.py:200
  690.7 17.4 %convolution_bitcast_fusion = f32[2,1024,1024]{2,1,0:T(8,128)} fusion(bf16[8,2,256,1024]{3,2,0,1:T(8,128)(2,1)S(1)} %bitcast.126, f32[2,8,256,1024]{3,2,1,0:T(8,128)} %fusion.12, f32[2,1024]{1,0:T(2,128)S(1)} %copy-done.31), kind=kOutput, calls=%fused_computation.38 | convolution fusion | flops 8631877632 | bytes 33562624 | tf_op jit(solution)/shard_map/secf,secd->efd/dot_general | solution.py:191
  708.8 22.4 %all-reduce = bf16[2,4,64]{2,1,0:T(4,128)(2,1)S(1)} all-reduce(bf16[2,4,64]{2,1,0:T(4,128)(2,1)S(1)} %pad_maximum_fusion.3), channel_id=7, replica_groups=mesh['fsdp'=8,'tp'=4] {'fsdp'}, use_global_device_ids=true, to_apply=%region_26.27.clone | all-reduce | flops 512 | bytes 2048
  733.5 11.8 %reduce-scatter.18.cloned.1.call-done = bf16[128,3,256]{2,0,1:T(8,128)(2,1)} async-done(((bf16[1024,3,256]{2,0,1:T(8,128)(2,1)}), bf16[128,3,256]{2,0,1:T(8,128)(2,1)}) %reduce-scatter.18.cloned.1.call-update) | async-done | bytes 196624 | tf_op jit(solution)/shard_map/reduce_scatter | solution.py:350
  747.1 46.3 %reduce-scatter.16.cloned.1.call-done = bf16[512,1024]{1,0:T(8,128)(2,1)} async-done(((bf16[2048,1024]{1,0:T(8,128)(2,1)}), bf16[512,1024]{1,0:T(8,128)(2,1)}) %reduce-scatter.16.cloned.1.call-update) | async-done | bytes 1048592 | tf_op jit(solution)/shard_map/reduce_scatter | solution.py:343
  795.6 39.5 %all-reduce.1 = (f32[1024]{0:T(1024)}, f32[1024]{0:T(1024)}, f32[1024]{0:T(1024)}, f32[1024]{0:T(1024)}, f32[1024]{0:T(1024)}) all-reduce(f32[1024]{0:T(1024)S(1)} %get-tuple-element.26, f32[1024]{0:T(1024)S(1)} %get-tuple-element.31, f32[1024]{0:T(1024)S(1)} %get-tuple-element.39, ...), channel_id=1, replica_groups=mesh['fsdp'=8,'tp'=4] {'fsdp','tp'}, use_global_device_ids=true, to_apply=%region_20.21 | all-reduce | flops 5120 | bytes 40960 | tf_op jit(solution)/shard_map/psum | solution.py:366
  (156 shorter events, 75.2 us)
Async XLA Ops:
  7.2 16.6 %copy-start.27 = (s32[1,2]{1,0:T(1,128)S(1)}, s32[1,2]{1,0:T(1,128)}, u32[]{:S(2)}) copy-start(s32[1,2]{1,0:T(1,128)} %param.21) | copy-start | bytes 28
  7.2 39.9 %copy-start.15 = (bf16[256,128]{1,0:T(8,128)(2,1)S(1)}, bf16[256,128]{1,0:T(8,128)(2,1)}, u32[]{:S(2)}) copy-start(bf16[256,128]{1,0:T(8,128)(2,1)} %param.26) | copy-start | bytes 196612
  7.2 66.6 %all-gather.8.cloned.1.call-start = ((), (), s32[]{:S(2)}) async-start(), calls=%async_computation.11 | async-start | bytes 1769472 | tf_op jit(solution)/shard_map/all_gather | solution.py:248
  8.0 84.3 %all-gather.6.cloned.1.call-start = ((), (), s32[]{:S(2)}) async-start(), calls=%async_computation.10 | async-start | bytes 5242880 | tf_op jit(solution)/shard_map/all_gather | solution.py:244
  13.8 161.2 %reduce-scatter.10.cloned.1.call-start = ((), (), s32[]{:S(2)}) async-start(), calls=%async_computation.12 | async-start | bytes 5242880 | tf_op jit(solution)/shard_map/reduce_scatter | solution.py:269
  98.4 24.7 %copy-start.13 = (bf16[256,1024]{1,0:T(8,128)(2,1)S(1)}, bf16[256,1024]{1,0:T(8,128)(2,1)}, u32[]{:S(2)}) copy-start(bf16[256,1024]{1,0:T(8,128)(2,1)} %all_gather.28) | copy-start | bytes 1572868
  126.4 48.6 %copy-start.14 = (f32[1024]{0:T(1024)S(1)}, f32[1024]{0:T(1024)}, u32[]{:S(2)}) copy-start(f32[1024]{0:T(1024)} %param.27) | copy-start | bytes 12292
  126.4 52.7 %copy-start.18 = (f32[1024]{0:T(1024)S(1)}, f32[1024]{0:T(1024)}, u32[]{:S(2)}) copy-start(f32[1024]{0:T(1024)} %param.28) | copy-start | bytes 12292
  126.4 52.7 %copy-start.24 = (f32[1024]{0:T(1024)S(1)}, f32[1024]{0:T(1024)}, u32[]{:S(2)}) copy-start(f32[1024]{0:T(1024)} %param.29) | copy-start | bytes 12292
  126.4 170.7 %all-gather.10.cloned.1.call-start = ((), (), s32[]{:S(2)}) async-start(), calls=%async_computation.13 | async-start | bytes 10485760 | tf_op jit(solution)/shard_map/all_gather | solution.py:301
  238.3 119.2 %all-gather.12.cloned.1.call-start = ((), (), s32[]{:S(2)}) async-start(), calls=%async_computation.15 | async-start | bytes 10485760 | tf_op jit(solution)/shard_map/all_gather | solution.py:302
  296.0 17.4 %copy-start.31 = (f32[2,1024]{1,0:T(2,128)S(1)}, f32[2,1024]{1,0:T(2,128)}, u32[]{:S(2)}) copy-start(f32[2,1024]{1,0:T(2,128)} %param.31) | copy-start | bytes 24580
  296.0 135.4 %reduce-scatter.12.cloned.1.call-start = ((), (), s32[]{:S(2)}) async-start(), calls=%async_computation.14 | async-start | bytes 10485760 | tf_op jit(solution)/shard_map/reduce_scatter | solution.py:209
  297.1 16.4 %copy-start.28 = (bf16[2,1024,1024]{2,1,0:T(8,128)(2,1)S(1)}, bf16[2,1024,1024]{2,1,0:T(8,128)(2,1)}, u32[]{:S(2)}) copy-start(bf16[2,1024,1024]{2,1,0:T(8,128)(2,1)} %param.32) | copy-start | bytes 12582916
  330.5 175.8 %reduce-scatter.14.cloned.1.call-start = ((), (), s32[]{:S(2)}) async-start(), calls=%async_computation.16 | async-start | bytes 10485760 | tf_op jit(solution)/shard_map/reduce_scatter | solution.py:209
  399.6 31.8 %copy-start.23 = (f32[2,1024]{1,0:T(2,128)S(1)}, f32[2,1024]{1,0:T(2,128)}, u32[]{:S(2)}) copy-start(f32[2,1024]{1,0:T(2,128)} %param.33) | copy-start | bytes 24580
  435.1 74.4 %all-to-all-start.1 = ((bf16[8,2,64,1024]{3,2,1,0:T(8,128)(2,1)}), bf16[8,2,64,1024]{3,2,1,0:T(8,128)(2,1)}, u32[]{:S(2)}, u32[]{:S(2)}) async-start(bf16[8,2,64,1024]{3,2,1,0:T(8,128)(2,1)} %copy.59), calls=%async_computation.3 | async-start | bytes 4194304 | tf_op jit(solution)/shard_map/all_to_all | solution.py:215
  509.5 52.0 %all-to-all-start.3 = ((bf16[8,2,64,1024]{3,2,1,0:T(8,128)(2,1)}), bf16[8,2,64,1024]{3,2,1,0:T(8,128)(2,1)}, u32[]{:S(2)}, u32[]{:S(2)}) async-start(bf16[8,2,64,1024]{3,2,1,0:T(8,128)(2,1)} %copy.61), calls=%async_computation.6 | async-start | bytes 4194304 | tf_op jit(solution)/shard_map/all_to_all | solution.py:215
  515.0 96.0 %all-gather.14.cloned.1.call-start = ((), (), s32[]{:S(2)}) async-start(), calls=%async_computation.17 | async-start | bytes 5242880 | tf_op jit(solution)/shard_map/all_gather | solution.py:319
  575.9 156.0 %reduce-scatter.20.cloned.1.call-start = ((), (), s32[]{:S(2)}) async-start(), calls=%async_computation.20 | async-start | bytes 589824
  617.6 127.7 %reduce-scatter.18.cloned.1.call-start = ((), (), s32[]{:S(2)}) async-start(), calls=%async_computation.19 | async-start | bytes 1769472 | tf_op jit(solution)/shard_map/reduce_scatter | solution.py:350
  621.6 33.7 %copy-start.29 = (bf16[2048,1024]{1,0:T(8,128)(2,1)S(1)}, bf16[2048,1024]{1,0:T(8,128)(2,1)}, u32[]{:S(2)}) copy-start(bf16[2048,1024]{1,0:T(8,128)(2,1)} %all-gather.6.cloned.1.call-done) | copy-start | bytes 12582916
  660.0 133.3 %reduce-scatter.16.cloned.1.call-start = ((), (), s32[]{:S(2)}) async-start(), calls=%async_computation.18 | async-start | bytes 5242880 | tf_op jit(solution)/shard_map/reduce_scatter | solution.py:343
  668.9 21.7 %slice-start = ((s8[8388608]{0:T(1024)(128)(4,1)}), s8[4194304]{0:T(1024)(128)(4,1)S(1)}, s32[]{:S(2)}) async-start(s8[8388608]{0:T(1024)(128)(4,1)} %bitcast.125), calls=%async_computation.21 | async-start | bytes 8388608
  674.7 15.9 %slice-start.1 = ((s8[8388608]{0:T(1024)(128)(4,1)}), s8[4194304]{0:T(1024)(128)(4,1)S(1)}, s32[]{:S(2)}) async-start(s8[8388608]{0:T(1024)(128)(4,1)} %bitcast.125), calls=%async_computation.22 | async-start | bytes 8388608
  690.7 17.4 %copy-start.5 = (bf16[2048,256]{1,0:T(8,128)(2,1)S(1)}, bf16[2048,256]{1,0:T(8,128)(2,1)}, u32[]{:S(2)}) copy-start(bf16[2048,256]{1,0:T(8,128)(2,1)} %copy-done.4) | copy-start | bytes 3145732
  690.7 17.7 %copy-start.3 = (bf16[2048,256]{1,0:T(8,128)(2,1)S(1)}, bf16[2048,256]{1,0:T(8,128)(2,1)}, u32[]{:S(2)}) copy-start(bf16[2048,256]{1,0:T(8,128)(2,1)} %copy-done.2) | copy-start | bytes 3145732
  690.7 102.7 %copy-start.17 = (f32[512]{0:T(512)S(1)}, f32[512]{0:T(512)}, u32[]{:S(2)}) copy-start(f32[512]{0:T(512)} %copy-done.16) | copy-start | bytes 6148
  690.7 102.6 %copy-start.19 = (f32[1024]{0:T(1024)S(1)}, f32[1024]{0:T(1024)}, u32[]{:S(2)}) copy-start(f32[1024]{0:T(1024)} %param.22) | copy-start | bytes 12292
  690.7 102.6 %copy-start.21 = (f32[512]{0:T(512)S(1)}, f32[512]{0:T(512)}, u32[]{:S(2)}) copy-start(f32[512]{0:T(512)} %copy-done.20) | copy-start | bytes 6148
  708.1 85.3 %copy-start.8 = (bf16[512,1024]{1,0:T(8,128)(2,1)S(1)}, bf16[512,1024]{1,0:T(8,128)(2,1)}, u32[]{:S(2)}) copy-start(bf16[512,1024]{1,0:T(8,128)(2,1)} %param.17) | copy-start | bytes 3145732
  708.7 126.4 %copy-start.11 = (f32[512,1024]{1,0:T(8,128)S(1)}, f32[512,1024]{1,0:T(8,128)}, u32[]{:S(2)}) copy-start(f32[512,1024]{1,0:T(8,128)} %copy-done.10) | copy-start | bytes 6291460
  (16 other events, 57.8 us)
Sparse Core Ops, SparseCore 0:
  10.2 45.1 all-gather.7
  57.6 34.6 all-gather.5
  126.5 48.4 reduce-scatter.9
  238.4 58.6 all-gather.9
  299.2 58.2 all-gather.11
  360.1 71.3 reduce-scatter.11
  434.6 71.7 reduce-scatter.13
  576.0 34.8 all-gather.13
  617.7 59.4 reduce-scatter.19
  680.5 64.7 reduce-scatter.17
  748.0 45.2 reduce-scatter.15

commit v2 on v1

v2 whole, which is shorter than its diff:
```python
import functools

import jax
import jax.numpy as jnp
from jax import lax
from jax.experimental import pallas as pl
from jax.experimental.pallas import tpu as pltpu
from jax.sharding import PartitionSpec as P

f32 = jnp.float32
bf16 = jnp.bfloat16
i32 = jnp.int32

HEAD_DIM = 64
PIECE = 256
DOCS = 4
TP = 4
BLOCK_K = 256
EXTRA = 16
EPSILON = 1e-05
MASKED = -1e30
VMEM = 60 << 20

NN = (((1,), (0,)), ((), ()))
NT = (((1,), (1,)), ((), ()))
TN = (((0,), (0,)), ((), ()))


def mxu(a, b, dims=NN):
    return lax.dot_general(a, b, dims, preferred_element_type=f32)


def cost():
    return pl.CostEstimate(flops=1, bytes_accessed=1, transcendentals=0)


def whole_spec(x):
    return pl.BlockSpec(x.shape, lambda *_: (0,) * x.ndim)


def smem_spec():
    return pl.BlockSpec(memory_space=pltpu.SMEM)


def kernel_name(kernel):
    return getattr(kernel, "func", kernel).__name__


def plain_call(kernel, ins, outs, scratch=(), scalars=()):
    return pl.pallas_call(
        kernel,
        name=kernel_name(kernel),
        grid=(1,),
        in_specs=[smem_spec() for _ in scalars] + [whole_spec(x) for x in ins],
        out_specs=[whole_spec(x) for x in outs],
        out_shape=list(outs),
        scratch_shapes=list(scratch),
        compiler_params=pltpu.CompilerParams(vmem_limit_bytes=VMEM),
        cost_estimate=cost(),
    )(*scalars, *ins)


def struct(shape, dtype):
    return jax.ShapeDtypeStruct(shape, dtype)


def send_tp(x, turn):
    return lax.ppermute(x, "tp", [(i, i ^ turn) for i in range(TP)])


def send_fsdp(x, turn):
    n = lax.axis_size("fsdp")
    return lax.ppermute(x, "fsdp", [(i, i ^ turn) for i in range(n)])


def after(x, *firsts):
    return lax.optimization_barrier((x, firsts))[0]


def sum_kernel(*refs):
    total = refs[0][...].astype(f32)
    for ref in refs[1:-1]:
        total = total + ref[...].astype(f32)
    refs[-1][...] = total.astype(refs[-1].dtype)


def added(*parts, dtype=bf16):
    return plain_call(sum_kernel, parts, [struct(parts[0].shape, dtype)])[0]


def turned_sum_kernel(*refs):
    total = refs[0][...].astype(f32)
    for ref in refs[1:-1]:
        total = total + ref[...].astype(f32)
    refs[-1][...] = total.T


def two_parts(x):
    high = x.astype(bf16)
    return jnp.concatenate([high, (x - high.astype(f32)).astype(bf16)], axis=0)


def one_part(x):
    x = x.astype(f32)
    return x[: x.shape[0] // 2] + x[x.shape[0] // 2 :]


def first_fold_kernel(own, vector, got, kept, vectors, parts):
    rows = own.shape[0]
    kept[...] = own[...].astype(f32) + got[:rows, :].astype(f32)
    vectors[...] = vector[...] + one_part(got[rows:, :])
    parts[...] = two_parts(vectors[...])


def fold_kernel(own, got, parts, out):
    rows = own.shape[0]
    out[:rows, :] = (own[...].astype(f32) + got[...].astype(f32)).astype(bf16)
    out[rows:, :] = parts[...]


def last_fold_kernel(kept, vector, *refs):
    out, vectors = refs[-2:]
    rows, width = kept.shape[0], out.shape[2]
    total = kept[...]
    sums = vector[...]
    for ref in refs[:-2]:
        total = total + ref[:rows, :].astype(f32)
        sums = sums + one_part(ref[rows:, :])
    for j in range(out.shape[1]):
        out[:, j, :] = total[:, j * width : (j + 1) * width]
    vectors[...] = sums


def normed(values):
    centered = values - jnp.mean(values, axis=-1, keepdims=True)
    inverse = lax.rsqrt(jnp.mean(centered * centered, axis=-1, keepdims=True) + EPSILON)
    return centered * inverse, inverse


def norm_back(incoming, unit, inverse, gain):
    scaled = incoming * gain
    return inverse * (
        scaled
        - jnp.mean(scaled, axis=-1, keepdims=True)
        - unit * jnp.mean(scaled * unit, axis=-1, keepdims=True)
    )


def first_kernel(x, gain, shift, docs, w_in, w_out, bias, out, packed):
    rows = x.shape[0]
    unit, _ = normed(x[...].astype(f32))
    out[:rows, :] = (unit * gain[...] + shift[...]).astype(bf16)
    out[rows:, :] = jnp.zeros_like(out[rows:, :])
    out[rows : rows + EXTRA, :rows] = jnp.broadcast_to(
        docs[...].astype(f32), (EXTRA, rows)
    ).astype(bf16)
    shard, width = w_in.shape[0], w_in.shape[2]
    for j in range(3):
        packed[:shard, j * width : (j + 1) * width] = w_in[:, j, :]
    packed[:shard, 3 * width :] = w_out[...].T
    packed[shard:, :] = jnp.zeros_like(packed[shard:, :])
    packed[shard:, :width] = bias[...]


def slots_kernel(cap, place, ids, cot, slots, sent):
    rows = ids.shape[0]
    column = ids[...].astype(f32)
    across = jnp.broadcast_to(column, (rows, 128)).T[:1]
    before = lax.broadcasted_iota(i32, (rows, rows), 0) < lax.broadcasted_iota(i32, (rows, rows), 1)
    rank = jnp.sum(jnp.where(before & (column == across), 1.0, 0.0), axis=0, keepdims=True)
    rank = rank.astype(i32)
    expert = across.astype(i32)
    mine = (expert & 1) == (place[1] & 1)
    own = (expert >> 1) * cap + rank
    slots[...] = jnp.broadcast_to(jnp.where(mine, own, -1), slots.shape)
    sent[:rows, :] = cot[...]
    sent[rows:, :] = jnp.zeros_like(sent[rows:, :])
    meta = [jnp.where(mine, -1, v).astype(f32) for v in (expert >> 1, rank)]
    meta += [jnp.zeros((EXTRA - 2, rows), f32)]
    sent[rows:, :rows] = jnp.concatenate(meta, axis=0).astype(bf16)


def other_slots_kernel(cap, sent, slots, out):
    rows = slots.shape[1]
    meta = sent[rows:, :rows].astype(f32)
    group, rank = meta[0:1].astype(i32), meta[1:2].astype(i32)
    named = group >= 0
    own = jnp.where(named, group * cap + rank, -1)
    slots[...] = jnp.broadcast_to(own, slots.shape)
    spots = lax.broadcasted_iota(i32, (out.shape[0], rows), 0)
    out[...] = mxu(jnp.where(spots == own, 1.0, 0.0).astype(bf16), sent[:rows, :]).astype(bf16)


def project_kernel(n, rows, place, *refs):
    xs, ws = refs[:TP], refs[TP : TP + n]
    q, k, v, w_in, w_out = refs[TP + n :]
    width = q.shape[1]
    bias = jnp.zeros((8, width), f32)
    lane = lax.rem(lax.broadcasted_iota(i32, (8, width), 1), HEAD_DIM) // (HEAD_DIM // n)
    for turn in range(n):
        base = pl.multiple_of((place[0] ^ turn) * rows, rows)
        w_in[pl.ds(base, rows), :] = ws[turn][:rows, : 3 * width]
        w_out[pl.ds(base, rows), :] = ws[turn][:rows, 3 * width :]
        part = ws[turn][rows:, :width].astype(f32)[:8]
        bias = jnp.where(lane == (place[0] ^ turn), part, bias)
    block = q.shape[0] // TP
    for r in range(TP):
        x = xs[r][:block, :]
        here = pl.ds(r * block, block)
        q[here, :] = ((mxu(x, w_in[:, :width]) + bias[0:1, :]) * 0.125).astype(bf16)
        k[here, :] = mxu(x, w_in[:, width : 2 * width]).astype(bf16)
        v[here, :] = (mxu(x, w_in[:, 2 * width :]) + bias[1:2, :]).astype(bf16)


def middle_kernel(*refs):
    ctxs, ws = refs[:TP], refs[TP : 2 * TP]
    residual, bias, gain, shift, mixed, second = refs[-6:]
    total = residual[...].astype(f32) + bias[...]
    for r in range(TP):
        total = total + mxu(ctxs[r][...], ws[r][...], NT)
    mixed[...] = total
    unit, _ = normed(total)
    second[...] = (unit * gain[...] + shift[...]).astype(bf16)


def turn_kernel(*refs):
    ws = refs[:TP]
    own, other, mixed, cot, gain = refs[TP : TP + 5]
    back, low, sums = refs[TP + 5 : TP + 8]
    outs = refs[TP + 8 :]
    unit, inverse = normed(mixed[...])
    second_back = own[...].astype(f32) + other[...].astype(f32)
    total = cot[...].astype(f32) + norm_back(second_back, unit, inverse, gain[...])
    back[...] = total
    low[...] = total.astype(bf16)
    sums[...] = jnp.concatenate(
        [
            jnp.sum(second_back * unit, axis=0, keepdims=True),
            jnp.sum(second_back, axis=0, keepdims=True),
            jnp.sum(total, axis=0, keepdims=True),
            jnp.zeros((5, total.shape[1]), f32),
        ],
        axis=0,
    )
    for r in range(TP):
        outs[r][...] = mxu(low[...], ws[r][...]).astype(bf16)


def output_weight_kernel(n, rows, place, *refs):
    ctxs, low, kept, away, total = refs[:TP], refs[TP], refs[TP + 1], refs[TP + 2], refs[TP + 3]
    size = total.shape[0]
    for r in range(TP):
        total[...] = mxu(low[...], ctxs[r][...], TN)
        out = away if r & 1 else kept
        for at, turn in enumerate(list(range(0, n, 2)) + list(range(1, n, 2))):
            base = pl.multiple_of((place[0] ^ turn) * rows, rows)
            to = (r // 2) * size + at * rows
            out[to : to + rows, :] = total[pl.ds(base, rows), :].astype(bf16)


def pair_sum_kernel(a, b, here, there):
    size = here.shape[0]
    for at, out in enumerate((here, there)):
        rows = slice(at * size, (at + 1) * size)
        out[...] = (a[rows, :].astype(f32) + b[rows, :].astype(f32)).astype(bf16)


def input_back_kernel(count, turns, *refs):
    backs, w_in, outs = refs[:count], refs[count], refs[count + 1 :]
    pairs = count // 3
    width = w_in.shape[1] // 3
    block = outs[0].shape[0]
    for at, r in enumerate(turns):
        here = pl.ds(r * block, block)
        total = None
        for j in range(3):
            back = jnp.concatenate([backs[3 * p + j][here, :] for p in range(pairs)], axis=1)
            part = mxu(back, w_in[:, j * width : (j + 1) * width], NT)
            total = part if total is None else total + part
        outs[at][...] = total.astype(bf16)


def lane_sums(x):
    total = jnp.sum(x, axis=1, keepdims=True)
    return jnp.broadcast_to(total, (x.shape[0], 128)).T[:8]


def input_weight_kernel(n, rows, count, place, *refs):
    xs, backs, w_in, sums2 = refs[:TP], refs[TP : TP + count], refs[TP + count], refs[TP + count + 1]
    parts, vectors, small, total = refs[TP + count + 2 : -3], *refs[-3:]
    pairs = count // 3
    width = w_in.shape[1] // 3
    block = backs[0].shape[0] // TP
    ones = jnp.ones((8, block), bf16)
    for j in range(3):
        part = jnp.zeros((total.shape[0], width), f32)
        column = jnp.zeros((8, width), f32)
        for r in range(TP):
            here = pl.ds(r * block, block)
            back = jnp.concatenate([backs[3 * p + j][here, :] for p in range(pairs)], axis=1)
            part += mxu(xs[r][:block, :], back, TN)
            column += mxu(ones, back)
        total[:, j * width : (j + 1) * width] = part
        small[8 * j : 8 * j + 8, :] = column
    for turn in range(n):
        base = pl.multiple_of((place[0] ^ turn) * rows, rows)
        parts[turn][:rows, :] = total[pl.ds(base, rows), :].astype(bf16)
    w = w_in[...].astype(f32)
    column = jnp.concatenate([small[8 * j : 8 * j + 1, :] for j in range(3)], axis=1)
    lines = [lane_sums(total[...] * w)[:1], lane_sums(w * column)[:1]]
    lines += [sums2[r : r + 1, :] for r in range(3)]
    for r, line in enumerate(lines):
        vectors[r : r + 1, :] = line[:, : 3 * width]
    rests = [line[:, 3 * width :] for line in lines]
    rests += [small[0:1, :], small[16:17, :], jnp.zeros((1, 2 * width), f32)]
    rests = jnp.concatenate(rests, axis=1)
    for r in range(3):
        vectors[5 + r : 6 + r, :] = rests[:, 3 * width * r : 3 * width * (r + 1)]
    parts[1][rows:, :] = two_parts(vectors[...])


def last_kernel(residual, gain, own, other, mixed_back, out):
    unit, inverse = normed(residual[...].astype(f32))
    first_back = own[...].astype(f32) + other[...].astype(f32)
    out[...] = mixed_back[...] + norm_back(first_back, unit, inverse, gain[...])


def half_rows(x, h):
    rows = lax.broadcasted_iota(i32, x.shape, 0)
    keep = (rows < HEAD_DIM) if h == 0 else (rows >= HEAD_DIM)
    return jnp.where(keep, x, jnp.zeros_like(x))


def half_lanes(x, h):
    lanes = lax.broadcasted_iota(i32, x.shape, 1)
    keep = (lanes < HEAD_DIM) if h == 0 else (lanes >= HEAD_DIM)
    return jnp.where(keep, x, jnp.zeros_like(x))


def key_base(kb, block, t):
    per = block // BLOCK_K
    return pl.multiple_of(((kb // per) ^ t) * block + lax.rem(kb, per) * BLOCK_K, BLOCK_K)


def attend_kernel(t_ref, q_ref, k_ref, v_ref, a_ref, b_ref, *rest):
    outs, lse_ref, vt = rest[-TP - 2 : -2], rest[-2], rest[-1]
    i = pl.program_id(0)
    bq = q_ref.shape[0]
    bk = BLOCK_K

    @pl.when(i == 0)
    def _():
        vt[...] = v_ref[...].T

    qt = q_ref[...].T
    qz = [half_rows(qt, h) for h in (0, 1)]
    a = a_ref[...]
    b = b_ref[...]

    def body(kb, carry):
        base = key_base(kb, bq, t_ref[0])
        kblk = k_ref[pl.ds(base, bk), :]
        j = kb * bk + lax.broadcasted_iota(i32, (bk, bq), 0)
        mask = (j >= a) & (j <= b)
        out = []
        for h in (0, 1):
            m, l, acc = carry[h]
            s = jnp.where(mask, mxu(kblk, qz[h]), MASKED)
            mn = jnp.maximum(m, jnp.max(s, axis=0, keepdims=True))
            p = jnp.exp(s - mn)
            al = jnp.exp(m - mn)
            l = al * l + jnp.sum(p, axis=0, keepdims=True)
            acc = acc * al + mxu(
                vt[pl.ds(HEAD_DIM * h, HEAD_DIM), pl.ds(base, bk)], p.astype(bf16)
            )
            out.append((mn, l, acc))
        return tuple(out)

    init = tuple(
        (jnp.full((1, bq), MASKED, f32), jnp.zeros((1, bq), f32), jnp.zeros((HEAD_DIM, bq), f32))
        for _ in (0, 1)
    )
    res = lax.fori_loop(jnp.min(a) // bk, jnp.max(b) // bk + 1, body, init)
    ot = jnp.concatenate([acc / l for m, l, acc in res], axis=0)
    o = ot.T.astype(bf16)
    for r in range(TP):

        @pl.when(i == r)
        def _(r=r):
            outs[r][...] = o

    lse_ref[...] = jnp.concatenate(
        [m + jnp.log(l) for m, l, acc in res] + [jnp.zeros((6, bq), f32)], axis=0
    )


def attention_fwd(pair, q, k, v, a, b, t, before):
    S, W = q.shape
    bq = S // TP
    whole = pl.BlockSpec((S, 128), lambda i, *_: (0, pair))
    row = pl.BlockSpec((1, bq), lambda i, *_: (0, i))
    return pl.pallas_call(
        attend_kernel,
        name="attend",
        grid_spec=pltpu.PrefetchScalarGridSpec(
            num_scalar_prefetch=1,
            grid=(TP,),
            in_specs=[pl.BlockSpec((bq, 128), lambda i, *_: (i, pair)), whole, whole, row, row]
            + [pl.BlockSpec(memory_space=pl.ANY)] * len(before),
            out_specs=[pl.BlockSpec((bq, 128), lambda i, *_: (0, pair))] * TP
            + [pl.BlockSpec((8, bq), lambda i, *_: (0, i))],
            scratch_shapes=[pltpu.VMEM((128, S), bf16)],
        ),
        out_shape=[struct((bq, W), bf16)] * TP + [struct((8, S), f32)],
        input_output_aliases={6 + r: r for r in range(len(before))},
        compiler_params=pltpu.CompilerParams(vmem_limit_bytes=VMEM),
        cost_estimate=cost(),
    )(t, q, k, v, a, b, *before)


def attend_back_kernel(t_ref, q_ref, k_ref, v_ref, *rest):
    dos, os = rest[:TP], rest[TP : 2 * TP]
    lse_ref, a_ref, b_ref, dq_ref, dk_ref, dv_ref, kt, dk_acc, dv_acc, do_s, o_s = rest[2 * TP :]
    i = pl.program_id(0)
    bq = q_ref.shape[0]
    bk = BLOCK_K

    @pl.when(i == 0)
    def _():
        kt[...] = k_ref[...].T
        dk_acc[...] = jnp.zeros_like(dk_acc)
        dv_acc[...] = jnp.zeros_like(dv_acc)

    for r in range(TP):

        @pl.when(i == r)
        def _(r=r):
            do_s[...] = dos[r][...]
            o_s[...] = os[r][...]

    q = q_ref[...]
    do = do_s[...]
    qt = q.T
    dot_ = do.T
    qz = [half_rows(qt, h) for h in (0, 1)]
    dz = [half_rows(dot_, h) for h in (0, 1)]
    qcat = jnp.concatenate([half_lanes(q, 0), half_lanes(q, 1)], axis=0)
    dcat = jnp.concatenate([half_lanes(do, 0), half_lanes(do, 1)], axis=0)
    prod = (do.astype(f32) * o_s[...].astype(f32)).T
    delta = [
        jnp.sum(prod[:HEAD_DIM], axis=0, keepdims=True),
        jnp.sum(prod[HEAD_DIM:], axis=0, keepdims=True),
    ]
    lse = [lse_ref[0:1, :], lse_ref[1:2, :]]
    a = a_ref[...]
    b = b_ref[...]

    def body(kb, carry):
        base = key_base(kb, bq, t_ref[0])
        here = pl.ds(base, bk)
        kblk = k_ref[here, :]
        vblk = v_ref[here, :]
        j = kb * bk + lax.broadcasted_iota(i32, (bk, bq), 0)
        mask = (j >= a) & (j <= b)
        ps, dss, out = [], [], []
        for h in (0, 1):
            p = jnp.exp(jnp.where(mask, mxu(kblk, qz[h]) - lse[h], MASKED))
            ds = (p * (mxu(vblk, dz[h]) - delta[h])).astype(bf16)
            ps.append(p.astype(bf16))
            dss.append(ds)
            out.append(carry[h] + mxu(kt[pl.ds(HEAD_DIM * h, HEAD_DIM), here], ds))
        dv_acc[here, :] += mxu(jnp.concatenate(ps, axis=1), dcat)
        dk_acc[here, :] += mxu(jnp.concatenate(dss, axis=1), qcat)
        return tuple(out)

    init = tuple(jnp.zeros((HEAD_DIM, bq), f32) for _ in (0, 1))
    dqt = lax.fori_loop(jnp.min(a) // bk, jnp.max(b) // bk + 1, body, init)
    dq_ref[...] = (jnp.concatenate(dqt, axis=0).T * 0.125).astype(bf16)

    @pl.when(i == TP - 1)
    def _():
        dk_ref[...] = dk_acc[...].astype(bf16)
        dv_ref[...] = dv_acc[...].astype(bf16)


def attention_bwd(pair, q, k, v, dos, os, lse, a, b, t):
    S = q.shape[0]
    bq = S // TP
    context = pl.BlockSpec((bq, 128), lambda i, *_: (0, pair))
    whole = pl.BlockSpec((S, 128), lambda i, *_: (0, pair))
    out = pl.BlockSpec((S, 128), lambda i, *_: (0, 0))
    row = pl.BlockSpec((1, bq), lambda i, *_: (0, i))
    return pl.pallas_call(
        attend_back_kernel,
        name="attend_back",
        grid_spec=pltpu.PrefetchScalarGridSpec(
            num_scalar_prefetch=1,
            grid=(TP,),
            in_specs=[pl.BlockSpec((bq, 128), lambda i, *_: (i, pair)), whole, whole]
            + [context] * (2 * TP)
            + [pl.BlockSpec((8, bq), lambda i, *_: (0, i)), row, row],
            out_specs=[pl.BlockSpec((bq, 128), lambda i, *_: (i, 0)), out, out],
            scratch_shapes=[
                pltpu.VMEM((128, S), bf16),
                pltpu.VMEM((S, 128), f32),
                pltpu.VMEM((S, 128), f32),
                pltpu.VMEM((bq, 128), bf16),
                pltpu.VMEM((bq, 128), bf16),
            ],
        ),
        out_shape=[struct((S, 128), bf16)] * 3,
        compiler_params=pltpu.CompilerParams(vmem_limit_bytes=VMEM),
        cost_estimate=cost(),
    )(t, q, k, v, *dos, *os, lse, a, b)


def intervals_kernel(place, starts, *refs):
    first, end = refs[TP:]
    rows = first.shape[1] // TP
    docs = [ref[0:1, :rows].astype(f32) for ref in refs[:TP]]
    bounds = [jnp.zeros((1, 1), f32)]
    for number in range(DOCS):
        here = sum(jnp.sum(jnp.where(d == number, 1.0, 0.0), axis=1, keepdims=True) for d in docs)
        bounds.append(bounds[-1] + here)
    for r in range(TP):
        low = jnp.zeros((1, rows), f32)
        last = jnp.zeros((1, rows), f32)
        for number in range(DOCS):
            here = docs[r] == number
            low = jnp.where(here, bounds[number], low)
            last = jnp.where(here, bounds[number + 1] - 1.0, last)
        spot = (place[1] ^ r) * rows + lax.broadcasted_iota(i32, (1, rows), 1)
        piece_last = jnp.full((1, rows), -1, i32)
        for p in range(2):
            inside = (spot >= starts[0, p]) & (spot < starts[0, p] + PIECE)
            piece_last = jnp.where(inside, starts[0, p] + PIECE - 1, piece_last)
        first[:, r * rows : (r + 1) * rows] = low.astype(i32)
        end[:, r * rows : (r + 1) * rows] = jnp.maximum(
            spot, jnp.minimum(piece_last, last.astype(i32))
        )


def intervals(here, starts, xs, rows):
    tail = pl.BlockSpec((EXTRA, xs[0].shape[1]), lambda i: (rows // EXTRA, 0))
    out = struct((1, TP * rows), i32)
    return pl.pallas_call(
        intervals_kernel,
        name="intervals",
        grid=(1,),
        in_specs=[smem_spec(), smem_spec()] + [tail] * TP,
        out_specs=[whole_spec(out)] * 2,
        out_shape=[out] * 2,
        cost_estimate=cost(),
    )(here, starts, *xs)


def place_kernel(x, s, out):
    spots = lax.broadcasted_iota(i32, (out.shape[0], s.shape[1]), 0)
    pick = jnp.where(spots == s[0:1, :], 1.0, 0.0).astype(bf16)
    out[...] = mxu(pick, x[...]).astype(bf16)


def collect_kernel(s_own, s_other, own_rows, other_rows, own, other):
    slots = lax.broadcasted_iota(i32, (own_rows.shape[0], own.shape[0]), 0)
    for s, rows, out in ((s_own, own_rows, own), (s_other, other_rows, other)):
        pick = jnp.where(slots == s[0:1, :], 1.0, 0.0).astype(bf16)
        out[...] = mxu(pick, rows[...], TN).astype(bf16)


def collect(s_own, s_other, own_rows, other_rows):
    rows, width = s_own.shape[1], own_rows.shape[1]
    return plain_call(
        collect_kernel,
        [s_own, s_other, own_rows, other_rows],
        [struct((rows, width), bf16)] * 2,
    )


def act_back_kernel(lo, near, far, down_a, down_b, out_near, out_far, sums):
    hidden = down_a.shape[0]
    half = pl.num_programs(0) // 2
    for at, (x, out) in enumerate(((near, out_near), (far, out_far))):

        @pl.when(pl.program_id(0) // half == at)
        def _(x=x, out=out):
            act_back_tile(hidden, x, down_a, down_b, out, sums)


def act_back_tile(hidden, x, down_a, down_b, out, sums):
    for j, down in enumerate((down_a, down_b)):
        out[:, j * hidden : (j + 1) * hidden] = mxu(x[...], down[...], NT).astype(bf16)
    total = mxu(jnp.ones((8, x.shape[0]), bf16), x[...])

    @pl.when(pl.program_id(0) == 0)
    def _():
        sums[...] = jnp.zeros_like(sums)

    sums[...] += total


def expert_kernel(lo, x, act_back, up_a, up_b, bias_a, bias_b, act, pre_back, x_back):
    width = up_a.shape[1]
    total = None
    for j, (up, bias) in enumerate(((up_a, bias_a), (up_b, bias_b))):
        here = slice(j * width, (j + 1) * width)
        pre = mxu(x[...], up[...]) + bias[...]
        square = pre * pre
        tan = jnp.tanh(0.7978845608028654 * pre * (1.0 + 0.044715 * square))
        half = 0.5 + 0.5 * tan
        act[:, here] = (pre * half).astype(bf16)
        slope = half + (0.5 * pre) * (1.0 - tan * tan) * (
            0.7978845608028654 + 0.1070322243 * square
        )
        low = (act_back[:, here].astype(f32) * slope).astype(bf16)
        pre_back[:, here] = low
        part = mxu(low, up[...], NT)
        total = part if total is None else total + part
    x_back[...] = total.astype(bf16)


def expert_out_kernel(lo, act_0, act_1, down_a, down_b, out):
    hidden = down_a.shape[0]
    half = pl.num_programs(0) // 2
    for at, act in enumerate((act_0, act_1)):

        @pl.when(pl.program_id(0) // half == at)
        def _(act=act):
            total = mxu(act[:, :hidden], down_a[...]) + mxu(act[:, hidden:], down_b[...])
            out[...] = total.astype(bf16)


def out_sum_kernel(cap, near, far, bias, out):
    half = near.shape[0] // 2
    for at in range(half // cap):
        for core in range(2):
            here = slice(core * half + at * cap, core * half + (at + 1) * cap)
            to = (2 * at + core) * cap
            total = near[here, :].astype(f32) + far[here, :].astype(f32) + bias[...]
            out[to : to + cap, :] = total.astype(bf16)


def collect_both_kernel(cap, s_own, s_other, both, own, other):
    slots = lax.broadcasted_iota(i32, (both.shape[0] // 2, own.shape[0]), 0)
    for core, (s, out) in enumerate(((s_own, own), (s_other, other))):
        pick = jnp.where(slots == s[0:1, :], 1.0, 0.0).astype(bf16)
        rows = jnp.concatenate(
            [both[at : at + cap, :] for at in range(core * cap, both.shape[0], 2 * cap)], axis=0
        )
        out[...] = mxu(pick, rows, TN).astype(bf16)


def up_outer_kernel(count, lo, *refs):
    left = jnp.concatenate([r[...] for r in refs[:count]], axis=0)
    right = jnp.concatenate([r[...] for r in refs[count:-2]], axis=0)
    out, sums = refs[-2:]
    out[...] = mxu(left, right, TN).astype(out.dtype)
    sums[...] = mxu(jnp.ones((8, right.shape[0]), bf16), right)


def down_outer_kernel(count, lo, *refs):
    left = jnp.concatenate([r[...] for r in refs[:count]], axis=0)
    right = jnp.concatenate([r[...] for r in refs[count:-1]], axis=0)
    refs[-1][...] = mxu(left, right, TN).astype(refs[-1].dtype)


def halves_kernel(lo, up, down, out):
    out[0] = up[...]
    out[1] = down[...]


def fill_kernel(lo, kept, other, out):
    out[...] = other[...].astype(f32)


class Expert:
    def __init__(self, lo, width, hidden):
        self.lo = jnp.reshape(lo, (1,)).astype(i32)
        self.width, self.hidden = width, hidden
        self.tile = 256

    def hold(self, up, up_bias, up_bias_other, down, other):
        self.up, self.down, self.other = up, down, other
        self.up_bias, self.up_bias_other = up_bias[:, None, :], up_bias_other

    def call(self, kernel, grid, in_specs, out_specs, out_shape, args, alias=None, scratch=()):
        return pl.pallas_call(
            kernel,
            name=kernel_name(kernel),
            grid_spec=pltpu.PrefetchScalarGridSpec(
                num_scalar_prefetch=1,
                grid=grid,
                in_specs=in_specs,
                out_specs=out_specs,
                scratch_shapes=list(scratch),
            ),
            out_shape=out_shape,
            input_output_aliases=alias or {},
            compiler_params=pltpu.CompilerParams(vmem_limit_bytes=VMEM),
            cost_estimate=cost(),
        )(self.lo, *args)

    def away(self, at):
        return pl.BlockSpec((None,) + self.other.shape[1:], lambda i, lo: (at, 0, 0))

    def own(self, x):
        return pl.BlockSpec((None,) + x.shape[1:], lambda i, lo: (lo[0], 0, 0))

    def row(self, columns):
        return pl.BlockSpec((self.tile, columns), lambda i, lo: (i, 0))

    def two(self, columns, steps):
        return [
            pl.BlockSpec((self.tile, columns), lambda i, lo: (jnp.minimum(i, steps - 1), 0)),
            pl.BlockSpec((self.tile, columns), lambda i, lo: (jnp.maximum(i - steps, 0), 0)),
        ]

    def act_back(self, near, far):
        rows = near.shape[0]
        steps = rows // self.tile
        return self.call(
            act_back_kernel,
            (2 * steps,),
            self.two(self.width, steps) + [self.own(self.down), self.away(1)],
            self.two(2 * self.hidden, steps)
            + [pl.BlockSpec((8, self.width), lambda i, lo: (0, 0))],
            [struct((rows, 2 * self.hidden), bf16)] * 2 + [struct((8, self.width), f32)],
            [near, far, self.down, self.other],
        )

    def rows(self, x, act_back):
        rows = x.shape[0]
        wide = self.row(2 * self.hidden)
        return self.call(
            expert_kernel,
            (rows // self.tile,),
            [
                self.row(self.width),
                wide,
                self.own(self.up),
                self.away(0),
                self.own(self.up_bias),
                whole_spec(self.up_bias_other),
            ],
            [wide, wide, self.row(self.width)],
            [struct((rows, 2 * self.hidden), bf16)] * 2 + [struct((rows, self.width), bf16)],
            [x, act_back, self.up, self.other, self.up_bias, self.up_bias_other],
        )

    def out(self, act_0, act_1):
        rows = act_0.shape[0]
        steps = rows // self.tile
        return self.call(
            expert_out_kernel,
            (2 * steps,),
            self.two(2 * self.hidden, steps) + [self.own(self.down), self.away(1)],
            self.row(self.width),
            struct((2 * rows, self.width), bf16),
            [act_0, act_1, self.down, self.other],
        )

    def outer_specs(self, own):
        size, tile = self.width, 512
        if own:
            out = pl.BlockSpec((None, tile, size), lambda i, lo: (lo[0], i, 0))
            return out, struct((2, size, size), f32)
        return pl.BlockSpec((tile, size), lambda i, lo: (i, 0)), struct((size, size), bf16)

    def up_outer(self, xs, backs, at, own):
        size, count = self.width, len(xs)
        out, shape = self.outer_specs(own)
        return self.call(
            functools.partial(up_outer_kernel, count),
            (size // 512,),
            [pl.BlockSpec((xs[0].shape[0], 512), lambda i, lo: (0, i))] * count
            + [pl.BlockSpec((backs[0].shape[0], size), lambda i, lo: (0, at))] * len(backs),
            [out, pl.BlockSpec((8, size), lambda i, lo: (0, 0))],
            [shape, struct((8, size), f32)],
            list(xs) + list(backs),
        )

    def down_outer(self, acts, cots, at, own):
        rows, size, count = acts[0].shape[0], self.width, len(acts)
        out, shape = self.outer_specs(own)
        return self.call(
            functools.partial(down_outer_kernel, count),
            (size // 512,),
            [pl.BlockSpec((rows, 512), lambda i, lo: (0, at * (size // 512) + i))] * count
            + [whole_spec(c) for c in cots],
            out,
            shape,
            list(acts) + list(cots),
        )

    def halves(self, up, down):
        size = up.shape[1]
        part = pl.BlockSpec((None, size // 4, size), lambda i, lo: (1 - lo[0], i, 0))
        return self.call(
            halves_kernel,
            (4,),
            [part, part],
            pl.BlockSpec((2, size // 4, size), lambda i, lo: (0, i, 0)),
            struct((2, size, size), bf16),
            [up, down],
        )

    def fill(self, kept, other):
        size = other.shape[0]
        return self.call(
            fill_kernel,
            (4,),
            [
                pl.BlockSpec(memory_space=pl.ANY),
                pl.BlockSpec((size // 4, size), lambda i, lo: (i, 0)),
            ],
            pl.BlockSpec((None, size // 4, size), lambda i, lo: (1 - lo[0], i, 0)),
            struct(kept.shape, f32),
            [kept, other],
            alias={1: 0},
        )


def ordered(lo, own, other):
    return jnp.where(lo == 0, jnp.stack([own, other]), jnp.stack([other, own]))


def local(
    residual_in,
    out_cotangent,
    expert_index,
    document_index,
    piece_starts,
    first_norm_gain,
    first_norm_shift,
    input_weight,
    input_bias,
    output_weight,
    output_bias,
    second_norm_gain,
    second_norm_shift,
    expert_up,
    expert_up_bias,
    expert_down,
    expert_down_bias,
):
    rows, width = residual_in.shape
    n = lax.axis_size("fsdp")
    g = lax.axis_index("fsdp")
    t = lax.axis_index("tp")
    lo = t & 1
    place = jnp.reshape(g, (1,)).astype(i32)
    turn = jnp.reshape(t, (1,)).astype(i32)
    row = lambda v: v.reshape(1, -1)
    head_width = input_weight.shape[2]
    shard = input_weight.shape[0]
    cap = rows * 2 // (2 * n)
    evens = list(range(0, n, 2))

    expert = Expert(lo, width, expert_up.shape[2])

    share = jnp.pad(
        jnp.tile(input_bias, (1, 1, n)).reshape(2, head_width), ((0, EXTRA - 2), (0, 0))
    )
    x0, packed = plain_call(
        first_kernel,
        [
            residual_in,
            row(first_norm_gain),
            row(first_norm_shift),
            document_index,
            input_weight,
            output_weight,
            share,
        ],
        [struct((rows + EXTRA, width), bf16), struct((shard + EXTRA, 4 * head_width), bf16)],
    )
    x2 = send_tp(x0, 2)
    weights = {0: packed}
    for k in evens[1:]:
        weights[k] = send_fsdp(packed, k)
    weights[1] = send_fsdp(packed, 1)
    arrived = [weights[k] for k in evens[1:] + [1]]
    for k in evens[1:]:
        weights[k ^ 1] = send_fsdp(after(weights[k], arrived), 1)
    x1 = send_tp(after(x0, arrived), 1)
    x3 = send_tp(after(x2, arrived), 1)
    xs = [x0, x1, x2, x3]
    halves_sent = expert.halves(*after((expert_up, expert_down), x1))

    here = jnp.concatenate([place, turn])
    length = TP * rows
    first, end = intervals(here, piece_starts, xs, rows)
    s_own, cot_sent = plain_call(
        functools.partial(slots_kernel, cap),
        [after(expert_index, x1), out_cotangent],
        [struct((8, rows), i32), struct((rows + EXTRA, width), bf16)],
        scalars=[here],
    )

    def exchange(x):
        return lax.all_to_all(x, "fsdp", split_axis=0, concat_axis=0, tiled=True)

    slotted = struct((n * cap, width), bf16)
    cot_sent_own = plain_call(place_kernel, [out_cotangent, s_own], [slotted])[0]
    queries, keys, values, w_in, w_out0 = plain_call(
        functools.partial(project_kernel, n, shard),
        list(after(tuple(xs), cot_sent_own, halves_sent)) + [weights[k] for k in range(n)],
        [struct((length, head_width), bf16)] * 3
        + [struct((width, 3 * head_width), bf16), struct((width, head_width), bf16)],
        scalars=[place],
    )
    cot_other = send_tp(after(cot_sent, queries), 1)
    s_other, cot_sent_other = plain_call(
        functools.partial(other_slots_kernel, cap),
        [cot_other],
        [struct((8, rows), i32), slotted],
    )
    near_own = exchange(cot_sent_own)

    halves_other = send_tp(after(halves_sent, queries), 1)
    down_bias = lax.dynamic_index_in_dim(expert_down_bias, lo, keepdims=True)

    w_out2 = send_tp(w_out0, 2)
    w_out1 = send_tp(w_out0, 1)
    pairs = head_width // 128
    contexts, totals = [], []
    firsts = [queries, (cot_other, near_own)]
    cot_pieces = []
    for p in range(pairs):
        *contexts, total = attention_fwd(
            p,
            after(queries, firsts[min(p, 1)], totals),
            keys,
            values,
            first,
            end,
            turn,
            contexts,
        )
        if p == 0:
            near_other = exchange(after(cot_sent_other, near_own, total))
            far_own = send_tp(after(near_own, total, w_out1, w_out2, halves_other), 2)
            cot_pieces = [near_own, far_own, near_other, send_tp(near_other, 2)]
        totals.append(total)
    w_outs = [w_out0, w_out1, w_out2, send_tp(after(w_out2, total), 1)]
    ctxs = [contexts[0]] + [send_tp(contexts[r], r) for r in range(1, TP)]
    expert.hold(expert_up, expert_up_bias, None, expert_down, halves_other)
    act_backs, cot_sums = [None] * 4, [None] * 2
    act_backs[0], act_backs[1], cot_sums[0] = expert.act_back(*cot_pieces[:2])
    mixed, second = plain_call(
        middle_kernel,
        ctxs
        + w_outs
        + [
            after(residual_in, act_backs[0]),
            row(output_bias),
            row(second_norm_gain),
            row(second_norm_shift),
        ],
        [struct((rows, width), f32), struct((rows, width), bf16)],
    )

    bias_sent = lax.dynamic_index_in_dim(after(expert_up_bias, second), 1 - lo, keepdims=True)
    expert.hold(expert_up, expert_up_bias, send_tp(bias_sent, 1), expert_down, halves_other)
    act_backs[2], act_backs[3], cot_sums[1] = expert.act_back(*cot_pieces[2:])
    cot_sum = added(*cot_sums, dtype=f32)[:1]
    sent_own = plain_call(place_kernel, [second, s_own], [slotted])[0]
    second_other = send_tp(second, 1)
    sent_other = plain_call(
        place_kernel, [second_other, s_other], [slotted]
    )[0]
    rows_own = exchange(after(sent_own, near_other))
    rows_other = exchange(after(sent_other, rows_own, cot_pieces[3]))
    pieces = [rows_own, send_tp(rows_own, 2), rows_other]
    acts, pre_backs, x_backs = [], [], []
    for at in range(4):
        act, pre_back, x_back = expert.rows(after(pieces[at], x_backs, act_backs[3]), act_backs[at])
        if at == 0:
            pieces.append(send_tp(after(rows_other, x_back), 2))
        acts.append(act)
        pre_backs.append(pre_back)
        x_backs.append(x_back)

    got_own = send_tp(x_backs[1], 2)
    got_other = send_tp(x_backs[3], 2)
    back_sent_own = added(x_backs[0], after(got_own, x_backs[3]))
    back_home_own = exchange(back_sent_own)
    out_far = expert.out(*after((acts[1], acts[3]), back_sent_own))
    up_away, up_sum_away = expert.up_outer(pieces, after(tuple(pre_backs), out_far), 1, False)
    back_sent_other = added(x_backs[2], after(got_other, up_away))
    back_home_other = exchange(after(back_sent_other, back_home_own))
    out_got = send_tp(after(out_far, got_other), 2)
    late = after(tuple(acts), back_sent_other)
    down_away = expert.down_outer(late, cot_pieces, 1, False)
    out_near = expert.out(*after((acts[0], acts[2]), down_away))
    up_own, up_sum = expert.up_outer(pieces, after(tuple(pre_backs), out_near), 0, True)
    up_got, down_got = send_tp(up_away, 1), send_tp(down_away, 1)
    sent = send_tp(jnp.concatenate([up_sum_away[:1], cot_sum], axis=0), 1)
    back_own, back_away = collect(
        s_own, s_other, back_home_own, after(back_home_other, up_own, up_got, down_got, out_got, sent)
    )
    back_other = send_tp(back_away, 1)

    mixed_back, mixed_low, sums2, *ctx_backs = plain_call(
        turn_kernel,
        w_outs + [back_own, back_other, mixed, out_cotangent, row(second_norm_gain)],
        [
            struct((rows, width), f32),
            struct((rows, width), bf16),
            struct((8, width), f32),
        ]
        + [struct((rows, head_width), bf16)] * TP,
    )

    wo_kept, wo_away = plain_call(
        functools.partial(output_weight_kernel, n, shard),
        ctxs + [mixed_low],
        [struct((2 * width, head_width), bf16)] * 2,
        scratch=[pltpu.VMEM((width, head_width), f32)],
        scalars=[place],
    )
    up_bias_back = ordered(lo, up_sum[0], sent[0])
    down_bias_back = ordered(lo, cot_sum[0], sent[1])

    dos = [ctx_backs[0]] + [send_tp(ctx_backs[r], r) for r in range(1, TP)]
    wo_got = send_tp(wo_away, 1)
    out_sent = plain_call(
        functools.partial(out_sum_kernel, cap),
        [out_near, after(out_got, dos[0]), down_bias],
        [struct((2 * n * cap, width), bf16)],
    )[0]
    out_home = exchange(out_sent)
    projected_backs = []
    firsts = [(wo_away, out_sent), None]
    for p in range(pairs):
        back = attention_bwd(
            p,
            after(queries, firsts[min(p, 1)], projected_backs),
            keys,
            values,
            dos,
            contexts,
            totals[p],
            first,
            end,
            turn,
        )
        projected_backs += back
        if p == 0:
            wo_sum, wo_there = plain_call(
                pair_sum_kernel,
                [wo_kept, after(wo_got, back)],
                [struct((width, head_width), bf16)] * 2,
            )
            wo_got = send_tp(wo_there, 2)
            firsts[1] = wo_sum
    wo = added(wo_sum, after(wo_got, projected_backs))

    def input_back(turns, first):
        return plain_call(
            functools.partial(input_back_kernel, 3 * pairs, turns),
            projected_backs + [after(w_in, first)],
            [struct((rows, width), bf16)] * 2,
        )

    middle = n // 2 * shard
    wo_kept = added(wo[:middle], send_fsdp(wo[middle:], 1))
    wo_parts = [wo_kept[:shard]] + [
        send_fsdp(wo_kept[(at + 1) * shard : (at + 2) * shard], k)
        for at, k in enumerate(evens[1:])
    ]
    output_weight_back = plain_call(
        turned_sum_kernel, wo_parts, [struct((head_width, shard), f32)]
    )[0]

    *parts, vector = plain_call(
        functools.partial(input_weight_kernel, n, shard, 3 * pairs),
        xs + projected_backs + [w_in, sums2],
        [
            struct((shard + (EXTRA if k == 1 else 0), 3 * head_width), bf16)
            for k in range(n)
        ]
        + [struct((8, 3 * head_width), f32)],
        scratch=[
            pltpu.VMEM((24, head_width), f32),
            pltpu.VMEM((width, 3 * head_width), f32),
        ],
        scalars=[place],
    )
    part3, part2 = input_back((3, 2), (parts[0], wo))
    got3 = send_tp(part3, 1)
    part1, part0 = input_back((1, 0), part3)
    sum2 = added(part2, after(got3, part0))
    got2 = send_tp(sum2, 2)
    sum0 = added(part0, send_tp(part1, 1))
    got = {k: send_fsdp(parts[k + 1], 1) for k in evens}
    kept, vector, vector_parts = plain_call(
        first_fold_kernel,
        [parts[0], vector, got[0]],
        [
            struct((shard, 3 * head_width), f32),
            struct((8, 3 * head_width), f32),
            struct((EXTRA, 3 * head_width), bf16),
        ],
    )
    folds = [
        plain_call(
            fold_kernel,
            [parts[k], got[k], vector_parts],
            [struct((shard + EXTRA, 3 * head_width), bf16)],
        )[0]
        for k in evens[1:]
    ]
    wi_kept = (kept, folds)
    wi_total, vector = plain_call(
        last_fold_kernel,
        [kept, vector] + [send_fsdp(fold, k) for fold, k in zip(folds, evens[1:])],
        [struct((shard, 3, head_width), f32), struct((8, 3 * head_width), f32)],
    )

    out_own, out_away = plain_call(
        functools.partial(collect_both_kernel, cap),
        [s_own, s_other, after(out_home, wi_kept)],
        [struct((rows, width), bf16)] * 2,
    )
    out_other = send_tp(out_away, 1)
    block_output = added(mixed, out_own, out_other)

    down_own = expert.down_outer(after(tuple(acts), wi_kept), cot_pieces, 0, True)
    up_back = expert.fill(up_own, up_got)
    down_back = expert.fill(down_own, down_got)
    tails = vector[5:].reshape(-1)
    bias_sum = tails[5 * head_width : 7 * head_width]
    bias_sum = bias_sum.reshape(2, head_width // HEAD_DIM, n, HEAD_DIM // n)
    input_bias_back = lax.dynamic_index_in_dim(bias_sum, g, axis=2, keepdims=False)
    vector = after(vector, up_back, down_back, block_output, output_weight_back)
    vector = added(vector, send_tp(vector, 1), dtype=f32)
    vector = added(vector, send_tp(vector, 2), dtype=f32)
    tails = vector[5:].reshape(-1)[: 5 * head_width].reshape(5, head_width)
    vectors = jnp.concatenate([vector[:5], tails], axis=1)
    back_residual = plain_call(
        last_kernel,
        [residual_in, row(first_norm_gain), sum0, got2, after(mixed_back, vectors)],
        [struct((rows, width), f32)],
    )[0]

    first_gain_back = (vectors[0] - first_norm_shift * vectors[1]) / first_norm_gain
    return (
        block_output,
        back_residual,
        first_gain_back,
        vectors[1],
        wi_total,
        input_bias_back,
        output_weight_back,
        vectors[4],
        vectors[2],
        vectors[3],
        up_back,
        up_bias_back,
        down_back,
        down_bias_back,
    )


def solution(mesh):
    in_specs = (
        P(("fsdp", "tp"), None),
        P(("fsdp", "tp"), None),
        P(("fsdp", "tp"), None),
        P("fsdp", "tp"),
        P("fsdp", None),
        P(),
        P(),
        P("fsdp", None, "tp"),
        P(None, "tp", "fsdp"),
        P("tp", "fsdp"),
        P(),
        P(),
        P(),
        P("fsdp", None, "tp"),
        P("fsdp", "tp"),
        P("fsdp", "tp", None),
        P("fsdp", None),
    )
    out_specs = (
        P(("fsdp", "tp"), None),
        P(("fsdp", "tp"), None),
        P(),
        P(),
        P("fsdp", None, "tp"),
        P(None, "tp", "fsdp"),
        P("tp", "fsdp"),
        P(),
        P(),
        P(),
        P("fsdp", None, "tp"),
        P("fsdp", "tp"),
        P("fsdp", "tp", None),
        P("fsdp", None),
    )
    return jax.shard_map(local, mesh=mesh, in_specs=in_specs, out_specs=out_specs, check_vma=False)
```

time: 858 us -> 586 us (0.68)
  Pallas kernels: 55.7 us -> 318 us
  blocking collectives: 220 us -> 0 us
  waiting for transfers between devices: 326 us -> 116 us
  matrix products: 138 us -> 0 us
  starting transfers between devices: 12 us -> 104 us
  other arithmetic: 45.5 us -> 4.04 us
  between operations: 15.4 us -> 1.53 us
    pallas_call x2 -> x54, Pallas kernels: 55.7 us -> 318 us  [the longest x15 128 us: call(): pl.pallas_call(kernel, name=kernel_name(kernel), grid_spec=pltpu.Prefetch...]
    reduce_scatter x5 -> x0, waiting for transfers between devices: 203 us -> none  [the longest x2 97.5 us: sum_shares(): lax.psum_scatter(partial_out.astype(jnp.bfloat16), 'tp', scatter_dimensio...]
    dot_general x12 -> x0, matrix products: 138 us -> none  [the longest x1 27.4 us: expert_backward(): jnp.einsum('secd,efd->secf', cotangent_rows, lower, preferred_element_typ...]
    ppermute x0 -> x53, waiting for transfers between devices: none -> 112 us  [the longest x35 64.3 us: send_tp(): return lax.ppermute(x, 'tp', [(i, i ^ turn) for i in range(TP)])]
    all_to_all x2 -> x0, blocking collectives: 103 us -> none  [the longest x1 51.9 us: local(): lax.all_to_all(sent_rows, 'fsdp', split_axis=0, concat_axis=0, tiled=True)]
    all_gather x5 -> x0, waiting for transfers between devices: 80.9 us -> none  [the longest x1 35 us: local(): lax.all_gather(mixed_back.astype(jnp.bfloat16), 'tp', axis=0, tiled=True)]
    ppermute x0 -> x53, starting transfers between devices: none -> 63.2 us  [the longest x35 39.2 us: send_tp(): return lax.ppermute(x, 'tp', [(i, i ^ turn) for i in range(TP)])]
    all_gather x3 -> x0, blocking collectives: 54.9 us -> none  [the longest x1 26.6 us: local(): lax.all_gather(output_weight, 'fsdp', axis=1, tiled=True)]
  transfers between devices with their start and end apart: 13 -> 60, of which waited for: 10 -> 29; matrix products, arithmetic and copies ran while one was open for 19% -> 2% of each run, Pallas kernels for 4% -> 50%
where the time goes in v2:
time: 586 us; the launch traced here: 574 us
  Pallas kernels  318 us (54%)
  waiting for transfers between devices  116 us (20%)
  starting transfers between devices  104 us (18%)
  local copies, waits for them, and re-layouts  31.3 us (5%)
    pallas_call x15, Pallas kernels, call(): pl.pallas_call(kernel, name=kernel_name(kernel), grid_spec=pltpu.Prefetch...  128 us
    pallas_call x34, Pallas kernels, plain_call(): pl.pallas_call(kernel, name=kernel_name(kernel), grid=(1,), in_specs=[sme...  115 us
    ppermute x35, waiting for transfers between devices, send_tp(): return lax.ppermute(x, 'tp', [(i, i ^ turn) for i in range(TP)])  64.3 us
    ppermute x18, waiting for transfers between devices, send_fsdp(): return lax.ppermute(x, 'fsdp', [(i, i ^ turn) for i in range(n)])  47.4 us
    pallas_call x2, Pallas kernels, attention_bwd(): pl.pallas_call(attend_back_kernel, name='attend_back', grid_spec=pltpu.Pr...  40.8 us
    all_to_all x7, starting transfers between devices, exchange(): return lax.all_to_all(x, 'fsdp', split_axis=0, concat_axis=0, tiled=True)  40.3 us
    ppermute x35, starting transfers between devices, send_tp(): return lax.ppermute(x, 'tp', [(i, i ^ turn) for i in range(TP)])  39.2 us
    pallas_call x2, Pallas kernels, attention_fwd(): pl.pallas_call(attend_kernel, name='attend', grid_spec=pltpu.PrefetchScal...  31.7 us
  transfers between devices with their start and end apart: 60, of which 29 were waited for; matrix products, arithmetic and copies ran while one was open for 2% of the time, Pallas kernels for 50%

profile of v2, /device:TPU:9, one launch (start us, length us, event | category | flops | bytes accessed | tf_op | source)
XLA Modules:
  0.0 574.5 jit_solution(1998116476444207121)
XLA Ops:
  16.2 14.4 %collective-permute-done.2.refs_10_ = bf16[144,1024]{1,0:T(8,128)(2,1)} collective-permute-done((bf16[144,1024]{1,0:T(8,128)(2,1)}, bf16[144,1024]{1,0:T(8,128)(2,1)}, u32[]{:S(2)}, u32[]{:S(2)}) %collective-permute-start.2) | collective-permute-done | bytes 294944 | tf_op jit(solution)/shard_map/ppermute | solution.py:73
  52.5 6.1 %collective-permute-done.9.refs_11_ = bf16[144,1024]{1,0:T(8,128)(2,1)} collective-permute-done((bf16[144,1024]{1,0:T(8,128)(2,1)}, bf16[144,1024]{1,0:T(8,128)(2,1)}, u32[]{:S(2)}, u32[]{:S(2)}) %collective-permute-start.9) | collective-permute-done | bytes 294944 | tf_op jit(solution)/shard_map/ppermute | solution.py:73
  58.6 7.7 %project_kernel.1 = (bf16[2048,256]{1,0:T(8,128)(2,1)}, bf16[2048,256]{1,0:T(8,128)(2,1)}, bf16[2048,256]{1,0:T(8,128)(2,1)}, bf16[1024,768]{1,0:T(8,128)(2,1)}, bf16[1024,256]{1,0:T(8,128)(2,1)}) custom-call(s32[1]{0:T(128)} %bitcast.1.place, bf16[528,1024]{1,0:T(8,128)(2,1)} %get-tuple-element.172.refs_0_, bf16[528,1024]{1,0:T(8,128)(2,1)} %copy-done.6, ...), custom_call_target="tpu_custom_call" | custom-call | flops 1 | bytes 1 | tf_op jit(solution)/shard_map/project_kernel/pallas_call | solution.py:50
  67.6 5.6 all-to-all-start
  75.3 15.9 %attend.2 = (bf16[512,256]{1,0:T(8,128)(2,1)}, bf16[512,256]{1,0:T(8,128)(2,1)}, bf16[512,256]{1,0:T(8,128)(2,1)}, bf16[512,256]{1,0:T(8,128)(2,1)}, f32[8,2048]{1,0:T(8,128)}) custom-call(s32[1]{0:T(128)} %bitcast.t_ref, bf16[2048,256]{1,0:T(8,128)(2,1)} %get-tuple-element.274.q_ref, bf16[2048,256]{1,0:T(8,128)(2,1)} %get-tuple-element.183.k_ref, ...), custom_call_target="tpu_custom_call" | custom-call | flops 1 | bytes 1 | tf_op jit(solution)/shard_map/attend/pallas_call | solution.py:402
  97.3 5.7 %all-to-all-start.1 = ((bf16[8,64,1024]{2,1,0:T(8,128)(2,1)}), bf16[8,64,1024]{2,1,0:T(8,128)(2,1)S(1)}, u32[]{:S(2)}, u32[]{:S(2)}) async-start(bf16[8,64,1024]{2,1,0:T(8,128)(2,1)} %bitcast.54), calls=%async_computation.1 | async-start | bytes 2097152 | tf_op jit(solution)/shard_map/all_to_all | solution.py:900
  104.6 10.9 %collective-permute-done.15.refs_6_.refs_2_ = bf16[1024,256]{1,0:T(8,128)(2,1)S(1)} collective-permute-done((bf16[1024,256]{1,0:T(8,128)(2,1)S(1)}, bf16[1024,256]{1,0:T(8,128)(2,1)S(1)}, u32[]{:S(2)}, u32[]{:S(2)}) %collective-permute-start.15) | collective-permute-done | bytes 524320 | tf_op jit(solution)/shard_map/ppermute | solution.py:68
  116.5 15.9 %attend.3 = (bf16[512,256]{1,0:T(8,128)(2,1)}, bf16[512,256]{1,0:T(8,128)(2,1)}, bf16[512,256]{1,0:T(8,128)(2,1)}, bf16[512,256]{1,0:T(8,128)(2,1)}, f32[8,2048]{1,0:T(8,128)}) custom-call(s32[1]{0:T(128)} %bitcast.t_ref, bf16[2048,256]{1,0:T(8,128)(2,1)} %get-tuple-element.274.q_ref, ...), custom_call_target="tpu_custom_call", output_to_operand_aliasing={{0}: (6, {}), {1}: (7, {}), {2}: (8, {}), {3}: (9, {})} | custom-call | flops 1 | bytes 1 | tf_op jit(solution)/shard_map/attend/pallas_call | solution.py:402
  140.0 9.3 %act_back_kernel.2 = (bf16[512,2048]{1,0:T(8,128)(2,1)}, bf16[512,2048]{1,0:T(8,128)(2,1)}, f32[8,1024]{1,0:T(8,128)}) custom-call(s32[1]{0:T(128)} %bitcast.4.lo, bf16[512,1024]{1,0:T(8,128)(2,1)} %bitcast.40, bf16[512,1024]{1,0:T(8,128)(2,1)} %copy-done.10, bf16[2,1024,1024]{2,1,0:T(8,128)(2,1)} %down_a.7, ...), custom_call_target="tpu_custom_call" | custom-call | flops 1 | bytes 1 | tf_op jit(solution)/shard_map/act_back_kernel/pallas_call | solution.py:686
  175.1 19.2 %collective-permute-done.19.far.refs_7_ = bf16[512,1024]{1,0:T(8,128)(2,1)S(1)} collective-permute-done((bf16[512,1024]{1,0:T(8,128)(2,1)S(1)}, bf16[512,1024]{1,0:T(8,128)(2,1)S(1)}, u32[]{:S(2)}, u32[]{:S(2)}) %collective-permute-start.19) | collective-permute-done | bytes 1048608 | tf_op jit(solution)/shard_map/ppermute | solution.py:68
  195.3 5.7 all-to-all-start.3
  203.6 9.3 %act_back_kernel.3 = (bf16[512,2048]{1,0:T(8,128)(2,1)}, bf16[512,2048]{1,0:T(8,128)(2,1)}, f32[8,1024]{1,0:T(8,128)}) custom-call(s32[1]{0:T(128)} %bitcast.4.lo, bf16[512,1024]{1,0:T(8,128)(2,1)} %bitcast.44, bf16[512,1024]{1,0:T(8,128)(2,1)} %copy-done.11, bf16[2,1024,1024]{2,1,0:T(8,128)(2,1)} %down_a.7, ...), custom_call_target="tpu_custom_call" | custom-call | flops 1 | bytes 1 | tf_op jit(solution)/shard_map/act_back_kernel/pallas_call | solution.py:686
  213.6 10.3 %expert_kernel.4 = (bf16[512,2048]{1,0:T(8,128)(2,1)}, bf16[512,2048]{1,0:T(8,128)(2,1)}, bf16[512,1024]{1,0:T(8,128)(2,1)}) custom-call(s32[1]{0:T(128)} %bitcast.4.lo, bf16[512,1024]{1,0:T(8,128)(2,1)} %bitcast.32, bf16[512,2048]{1,0:T(8,128)(2,1)} %get-tuple-element.202.act_back, bf16[2,1024,1024]{2,1,0:T(8,128)(2,1)} %up_a.7, ...), custom_call_target="tpu_custom_call" | custom-call | flops 1 | bytes 1 | tf_op jit(solution)/shard_map/expert_kernel/pallas_call | solution.py:686
  225.4 10.4 %expert_kernel.5 = (bf16[512,2048]{1,0:T(8,128)(2,1)}, bf16[512,2048]{1,0:T(8,128)(2,1)}, bf16[512,1024]{1,0:T(8,128)(2,1)}) custom-call(s32[1]{0:T(128)} %bitcast.4.lo, bf16[512,1024]{1,0:T(8,128)(2,1)} %copy-done.8, bf16[512,2048]{1,0:T(8,128)(2,1)} %get-tuple-element.217.act_back, bf16[2,1024,1024]{2,1,0:T(8,128)(2,1)} %up_a.7, ...), custom_call_target="tpu_custom_call" | custom-call | flops 1 | bytes 1 | tf_op jit(solution)/shard_map/expert_kernel/pallas_call | solution.py:686
  236.5 10.3 %expert_kernel.6 = (bf16[512,2048]{1,0:T(8,128)(2,1)}, bf16[512,2048]{1,0:T(8,128)(2,1)}, bf16[512,1024]{1,0:T(8,128)(2,1)}) custom-call(s32[1]{0:T(128)} %bitcast.4.lo, bf16[512,1024]{1,0:T(8,128)(2,1)} %bitcast.36, bf16[512,2048]{1,0:T(8,128)(2,1)} %get-tuple-element.220.act_back, bf16[2,1024,1024]{2,1,0:T(8,128)(2,1)} %up_a.7, ...), custom_call_target="tpu_custom_call" | custom-call | flops 1 | bytes 1 | tf_op jit(solution)/shard_map/expert_kernel/pallas_call | solution.py:686
  247.8 10.7 %expert_kernel.7 = (bf16[512,2048]{1,0:T(8,128)(2,1)}, bf16[512,2048]{1,0:T(8,128)(2,1)}, bf16[512,1024]{1,0:T(8,128)(2,1)}) custom-call(s32[1]{0:T(128)} %bitcast.4.lo, bf16[512,1024]{1,0:T(8,128)(2,1)} %copy-done.9, bf16[512,2048]{1,0:T(8,128)(2,1)} %get-tuple-element.210.act_back, bf16[2,1024,1024]{2,1,0:T(8,128)(2,1)} %up_a.7, ...), custom_call_target="tpu_custom_call" | custom-call | flops 1 | bytes 1 | tf_op jit(solution)/shard_map/expert_kernel/pallas_call | solution.py:686
  258.6 10.8 %collective-permute-done.25.refs_1_ = bf16[512,1024]{1,0:T(8,128)(2,1)S(1)} collective-permute-done((bf16[512,1024]{1,0:T(8,128)(2,1)}, bf16[512,1024]{1,0:T(8,128)(2,1)S(1)}, u32[]{:S(2)}, u32[]{:S(2)}) %collective-permute-start.25) | collective-permute-done | bytes 1048608 | tf_op jit(solution)/shard_map/ppermute | solution.py:68
  273.1 6.8 %all-to-all-start.4 = ((bf16[8,64,1024]{2,1,0:T(8,128)(2,1)}), bf16[8,64,1024]{2,1,0:T(8,128)(2,1)S(1)}, u32[]{:S(2)}, u32[]{:S(2)}) async-start(bf16[8,64,1024]{2,1,0:T(8,128)(2,1)} %bitcast.49), calls=%async_computation.4 | async-start | bytes 2097152 | tf_op jit(solution)/shard_map/all_to_all | solution.py:900
  280.1 8.9 %expert_out_kernel.2 = bf16[1024,1024]{1,0:T(8,128)(2,1)} custom-call(s32[1]{0:T(128)} %bitcast.4.lo, bf16[512,2048]{1,0:T(8,128)(2,1)} %get-tuple-element.307.act_0.refs_1_, bf16[512,2048]{1,0:T(8,128)(2,1)} %get-tuple-element.309.act_1.refs_3_, bf16[2,1024,1024]{2,1,0:T(8,128)(2,1)} %down_a.7, bf16[2,1024,1024]{2,1,0:T(8,128)(2,1)} %collective-permute-done.17.down_b.up_b), custom_call_target="tpu_custom_call" | custom-call | flops 1 | bytes 1 | tf_op jit(solution)/shard_map/expert_out_kernel/pallas_call | solution.py:686
  289.1 9.3 %up_outer_kernel.2 = (bf16[1024,1024]{1,0:T(8,128)(2,1)}, f32[8,1024]{1,0:T(8,128)}) custom-call(s32[1]{0:T(128)} %bitcast.4.lo, bf16[512,1024]{1,0:T(8,128)(2,1)} %bitcast.33, bf16[512,1024]{1,0:T(8,128)(2,1)} %copy-done.8, bf16[512,1024]{1,0:T(8,128)(2,1)} %bitcast.37, bf16[512,1024]{1,0:T(8,128)(2,1)} %copy-done.9, ...), custom_call_target="tpu_custom_call" | custom-call | flops 1 | bytes 1 | tf_op jit(solution)/shard_map/up_outer_kernel/pallas_call | solution.py:686
  305.9 8.7 %down_outer_kernel.2 = bf16[1024,1024]{1,0:T(8,128)(2,1)} custom-call(s32[1]{0:T(128)} %bitcast.4.lo, bf16[512,2048]{1,0:T(8,128)(2,1)} %get-tuple-element.306.refs_0_.act_0, bf16[512,2048]{1,0:T(8,128)(2,1)} %get-tuple-element.307.act_0.refs_1_, bf16[512,2048]{1,0:T(8,128)(2,1)} %get-tuple-element.308.refs_2_.act_1, ...), custom_call_target="tpu_custom_call" | custom-call | flops 1 | bytes 1 | tf_op jit(solution)/shard_map/down_outer_kernel/pallas_call | solution.py:686
  318.1 5.6 all-to-all-start.5
  327.3 9.0 %expert_out_kernel.3.near = bf16[1024,1024]{1,0:T(8,128)(2,1)} custom-call(s32[1]{0:T(128)} %bitcast.4.lo, bf16[512,2048]{1,0:T(8,128)(2,1)} %get-tuple-element.306.refs_0_.act_0, bf16[512,2048]{1,0:T(8,128)(2,1)} %get-tuple-element.308.refs_2_.act_1, bf16[2,1024,1024]{2,1,0:T(8,128)(2,1)} %down_a.7, bf16[2,1024,1024]{2,1,0:T(8,128)(2,1)} %collective-permute-done.17.down_b.up_b), custom_call_target="tpu_custom_call" | custom-call | flops 1 | bytes 1 | tf_op jit(solution)/shard_map/expert_out_kernel/pallas_call | solution.py:686
  336.3 9.5 %up_outer_kernel.3 = (f32[2,1024,1024]{2,1,0:T(8,128)}, f32[8,1024]{1,0:T(8,128)}) custom-call(s32[1]{0:T(128)} %bitcast.4.lo, bf16[512,1024]{1,0:T(8,128)(2,1)} %bitcast.34, bf16[512,1024]{1,0:T(8,128)(2,1)} %copy-done.8, bf16[512,1024]{1,0:T(8,128)(2,1)} %bitcast.38, bf16[512,1024]{1,0:T(8,128)(2,1)} %copy-done.9, ...), custom_call_target="tpu_custom_call" | custom-call | flops 1 | bytes 1 | tf_op jit(solution)/shard_map/up_outer_kernel/pallas_call | solution.py:686
  358.8 6.9 %turn_kernel.1 = (f32[512,1024]{1,0:T(8,128)}, bf16[512,1024]{1,0:T(8,128)(2,1)}, f32[8,1024]{1,0:T(8,128)}, bf16[512,256]{1,0:T(8,128)(2,1)}, bf16[512,256]{1,0...) custom-call(bf16[1024,256]{1,0:T(8,128)(2,1)} %get-tuple-element.197.refs_4_.refs_0_, ...), custom_call_target="tpu_custom_call" | custom-call | flops 1 | bytes 1 | tf_op jit(solution)/shard_map/turn_kernel/pallas_call | solution.py:50
  388.2 6.6 %collective-permute-done.33.rest_3_ = bf16[512,256]{1,0:T(8,128)(2,1)S(1)} collective-permute-done((bf16[512,256]{1,0:T(8,128)(2,1)}, bf16[512,256]{1,0:T(8,128)(2,1)S(1)}, u32[]{:S(2)}, u32[]{:S(2)}) %collective-permute-start.33) | collective-permute-done | bytes 262176 | tf_op jit(solution)/shard_map/ppermute | solution.py:68
  395.5 20.3 %attend_back.2 = (bf16[2048,128]{1,0:T(8,128)(2,1)}, bf16[2048,128]{1,0:T(8,128)(2,1)}, bf16[2048,128]{1,0:T(8,128)(2,1)}) custom-call(s32[1]{0:T(128)} %bitcast.t_ref, bf16[2048,256]{1,0:T(8,128)(2,1)} %get-tuple-element.274.q_ref, bf16[2048,256]{1,0:T(8,128)(2,1)} %get-tuple-element.183.k_ref, bf16[2048,256]{1,0:T(8,128)(2,1)} %get-tuple-element.184.v_ref, ...), custom_call_target="tpu_custom_call" | custom-call | flops 1 | bytes 1 | tf_op jit(solution)/shard_map/attend_back/pallas_call | solution.py:493
  420.4 20.5 %attend_back.3 = (bf16[2048,128]{1,0:T(8,128)(2,1)}, bf16[2048,128]{1,0:T(8,128)(2,1)}, bf16[2048,128]{1,0:T(8,128)(2,1)}) custom-call(s32[1]{0:T(128)} %bitcast.t_ref, bf16[2048,256]{1,0:T(8,128)(2,1)} %get-tuple-element.274.q_ref, bf16[2048,256]{1,0:T(8,128)(2,1)} %get-tuple-element.183.k_ref, bf16[2048,256]{1,0:T(8,128)(2,1)} %get-tuple-element.184.v_ref, ...), custom_call_target="tpu_custom_call" | custom-call | flops 1 | bytes 1 | tf_op jit(solution)/shard_map/attend_back/pallas_call | solution.py:493
  441.0 9.0 %input_weight_kernel.1 = (bf16[128,768]{1,0:T(8,128)(2,1)}, bf16[144,768]{1,0:T(8,128)(2,1)}, bf16[128,768]{1,0:T(8,128)(2,1)}, bf16[128,768]{1,0:T(8,128)(2,1)}...) custom-call(s32[1]{0:T(128)} %bitcast.1.place, ...), custom_call_target="tpu_custom_call" | custom-call | flops 1 | bytes 1 | tf_op jit(solution)/shard_map/input_weight_kernel/pallas_call | solution.py:50
  507.9 7.9 %collective-permute-start.50 = (bf16[128,256]{1,0:T(8,128)(2,1)S(1)}, bf16[128,256]{1,0:T(8,128)(2,1)S(1)}, u32[]{:S(2)}, u32[]{:S(2)}) collective-permute-start(bf16[128,256]{1,0:T(8,128)(2,1)S(1)} %get-tuple-element.344), channel_id=1, source_target_pairs={{0,24},{4,28},{8,16},{12,20},{16,8},{20,12},{24,0},{28,4},{1,25},{... | collective-permute-start | bytes 196616 | tf_op jit(solution)/shard_map/ppermute | solution.py:73
  515.9 6.2 %collective-permute-done.46.refs_2_ = bf16[144,768]{1,0:T(8,128)(2,1)S(1)} collective-permute-done((bf16[144,768]{1,0:T(8,128)(2,1)S(1)}, bf16[144,768]{1,0:T(8,128)(2,1)S(1)}, u32[]{:S(2)}, u32[]{:S(2)}) %collective-permute-start.46) | collective-permute-done | bytes 221216 | tf_op jit(solution)/shard_map/ppermute | solution.py:73
  525.3 9.3 %down_outer_kernel.3.kept = f32[2,1024,1024]{2,1,0:T(8,128)} custom-call(s32[1]{0:T(128)} %bitcast.4.lo, bf16[512,2048]{1,0:T(8,128)(2,1)} %get-tuple-element.306.refs_0_.act_0, bf16[512,2048]{1,0:T(8,128)(2,1)} %get-tuple-element.307.act_0.refs_1_, bf16[512,2048]{1,0:T(8,128)(2,1)} %get-tuple-element.308.refs_2_.act_1, ...), custom_call_target="tpu_custom_call" | custom-call | flops 1 | bytes 1 | tf_op jit(solution)/shard_map/down_outer_kernel/pallas_call | solution.py:686
  (282 shorter events, 250.2 us)
Async XLA Ops:
  7.2 30.3 %collective-permute-start.5 = (bf16[528,1024]{1,0:T(8,128)(2,1)}, bf16[528,1024]{1,0:T(8,128)(2,1)S(1)}, u32[]{:S(2)}, u32[]{:S(2)}) collective-permute-start(bf16[528,1024]{1,0:T(8,128)(2,1)} %get-tuple-element.172.refs_0_), channel_id=1, source_target_pairs={{0,2},{1,3},{2,0},{3,1},{4,6},{5,7},{6,4},{7,5},{8,10},{9,11},{10,... | collective-permute-start | bytes 3244040 | tf_op jit(solution)/shard_map/ppermute | solution.py:68
  9.6 20.9 %collective-permute-start.2 = (bf16[144,1024]{1,0:T(8,128)(2,1)}, bf16[144,1024]{1,0:T(8,128)(2,1)}, u32[]{:S(2)}, u32[]{:S(2)}) collective-permute-start(bf16[144,1024]{1,0:T(8,128)(2,1)} %get-tuple-element.165.refs_4_), channel_id=1, source_target_pairs={{0,24},{4,28},{8,16},{12,20},{16,8},{20,12},{24,0},{28,4},{1,25},{... | collective-permute-start | bytes 884744 | tf_op jit(solution)/shard_map/ppermute | solution.py:73
  10.9 24.3 %collective-permute-start.1 = (bf16[144,1024]{1,0:T(8,128)(2,1)}, bf16[144,1024]{1,0:T(8,128)(2,1)}, u32[]{:S(2)}, u32[]{:S(2)}) collective-permute-start(bf16[144,1024]{1,0:T(8,128)(2,1)} %get-tuple-element.165.refs_4_), channel_id=1, source_target_pairs={{0,16},{4,20},{8,24},{12,28},{16,0},{20,4},{24,8},{28,12},{1,17},{... | collective-permute-start | bytes 884744 | tf_op jit(solution)/shard_map/ppermute | solution.py:73
  11.9 23.3 %collective-permute-start = (bf16[144,1024]{1,0:T(8,128)(2,1)}, bf16[144,1024]{1,0:T(8,128)(2,1)}, u32[]{:S(2)}, u32[]{:S(2)}) collective-permute-start(bf16[144,1024]{1,0:T(8,128)(2,1)} %get-tuple-element.165.refs_4_), channel_id=1, source_target_pairs={{0,8},{4,12},{8,0},{12,4},{16,24},{20,28},{24,16},{28,20},{1,9},{5... | collective-permute-start | bytes 884744 | tf_op jit(solution)/shard_map/ppermute | solution.py:73
  39.0 19.6 %collective-permute-start.9 = (bf16[144,1024]{1,0:T(8,128)(2,1)}, bf16[144,1024]{1,0:T(8,128)(2,1)}, u32[]{:S(2)}, u32[]{:S(2)}) collective-permute-start(bf16[144,1024]{1,0:T(8,128)(2,1)} %collective-permute-done.2.refs_10_), channel_id=1, source_target_pairs={{0,4},{4,0},{8,12},{12,8},{16,20},{20,16},{24,28},{28,24},{1,5},{5... | collective-permute-start | bytes 884744 | tf_op jit(solution)/shard_map/ppermute | solution.py:73
  66.3 50.0 %collective-permute-start.17 = (bf16[2,1024,1024]{2,1,0:T(8,128)(2,1)}, bf16[2,1024,1024]{2,1,0:T(8,128)(2,1)}, u32[]{:S(2)}, u32[]{:S(2)}) collective-permute-start(bf16[2,1024,1024]{2,1,0:T(8,128)(2,1)} %halves_kernel.1), channel_id=1, source_target_pairs={{0,1},{1,0},{2,3},{3,2},{4,5},{5,4},{6,7},{7,6},{8,9},{9,8},{10,11... | collective-permute-start | bytes 12582920 | tf_op jit(solution)/shard_map/ppermute | solution.py:68
  67.6 29.7 %all-to-all-start = ((bf16[8,64,1024]{2,1,0:T(8,128)(2,1)}), bf16[8,64,1024]{2,1,0:T(8,128)(2,1)S(1)}, u32[]{:S(2)}, u32[]{:S(2)}) async-start(bf16[8,64,1024]{2,1,0:T(8,128)(2,1)} %bitcast.5), calls=%async_computation | async-start | bytes 2097152 | tf_op jit(solution)/shard_map/all_to_all | solution.py:900
  97.3 63.5 %all-to-all-start.1 = ((bf16[8,64,1024]{2,1,0:T(8,128)(2,1)}), bf16[8,64,1024]{2,1,0:T(8,128)(2,1)S(1)}, u32[]{:S(2)}, u32[]{:S(2)}) async-start(bf16[8,64,1024]{2,1,0:T(8,128)(2,1)} %bitcast.54), calls=%async_computation.1 | async-start | bytes 2097152 | tf_op jit(solution)/shard_map/all_to_all | solution.py:900
  116.3 22.7 %collective-permute-start.18 = (bf16[512,1024]{1,0:T(8,128)(2,1)S(1)}, bf16[512,1024]{1,0:T(8,128)(2,1)S(1)}, u32[]{:S(2)}, u32[]{:S(2)}) collective-permute-start(bf16[512,1024]{1,0:T(8,128)(2,1)S(1)} %bitcast.39), channel_id=1, source_target_pairs={{0,2},{1,3},{2,0},{3,1},{4,6},{5,7},{6,4},{7,5},{8,10},{9,11},{10,... | collective-permute-start | bytes 3145736 | tf_op jit(solution)/shard_map/ppermute | solution.py:68
  132.4 20.1 %collective-permute-start.16 = (bf16[1024,256]{1,0:T(8,128)(2,1)S(1)}, bf16[1024,256]{1,0:T(8,128)(2,1)}, u32[]{:S(2)}, u32[]{:S(2)}) collective-permute-start(bf16[1024,256]{1,0:T(8,128)(2,1)S(1)} %collective-permute-done.15.refs_6_.refs_2_), channel_id=1, source_target_pairs={{0,1},{1,0},{2,3},{3,2},{4,5},{5,4},{6,7},{7,6},{8,9},{9,8},{10,11... | collective-permute-start | bytes 1572872 | tf_op jit(solution)/shard_map/ppermute | solution.py:68
  160.7 33.6 %all-to-all-start.2 = ((bf16[8,64,1024]{2,1,0:T(8,128)(2,1)}), bf16[8,64,1024]{2,1,0:T(8,128)(2,1)S(1)}, u32[]{:S(2)}, u32[]{:S(2)}) async-start(bf16[8,64,1024]{2,1,0:T(8,128)(2,1)} %bitcast.53), calls=%async_computation.2 | async-start | bytes 2097152 | tf_op jit(solution)/shard_map/all_to_all | solution.py:900
  169.6 24.8 %collective-permute-start.19 = (bf16[512,1024]{1,0:T(8,128)(2,1)S(1)}, bf16[512,1024]{1,0:T(8,128)(2,1)S(1)}, u32[]{:S(2)}, u32[]{:S(2)}) collective-permute-start(bf16[512,1024]{1,0:T(8,128)(2,1)S(1)} %bitcast.43), channel_id=1, source_target_pairs={{0,2},{1,3},{2,0},{3,1},{4,6},{5,7},{6,4},{7,5},{8,10},{9,11},{10,... | collective-permute-start | bytes 3145736 | tf_op jit(solution)/shard_map/ppermute | solution.py:68
  195.3 29.1 %all-to-all-start.3 = ((bf16[8,64,1024]{2,1,0:T(8,128)(2,1)}), bf16[8,64,1024]{2,1,0:T(8,128)(2,1)S(1)}, u32[]{:S(2)}, u32[]{:S(2)}) async-start(bf16[8,64,1024]{2,1,0:T(8,128)(2,1)} %bitcast.52), calls=%async_computation.3 | async-start | bytes 2097152 | tf_op jit(solution)/shard_map/all_to_all | solution.py:900
  201.0 23.4 %collective-permute-start.22 = (bf16[512,1024]{1,0:T(8,128)(2,1)S(1)}, bf16[512,1024]{1,0:T(8,128)(2,1)S(1)}, u32[]{:S(2)}, u32[]{:S(2)}) collective-permute-start(bf16[512,1024]{1,0:T(8,128)(2,1)S(1)} %bitcast.31), channel_id=1, source_target_pairs={{0,2},{1,3},{2,0},{3,1},{4,6},{5,7},{6,4},{7,5},{8,10},{9,11},{10,... | collective-permute-start | bytes 3145736 | tf_op jit(solution)/shard_map/ppermute | solution.py:68
  224.4 22.4 %collective-permute-start.23 = (bf16[512,1024]{1,0:T(8,128)(2,1)S(1)}, bf16[512,1024]{1,0:T(8,128)(2,1)S(1)}, u32[]{:S(2)}, u32[]{:S(2)}) collective-permute-start(bf16[512,1024]{1,0:T(8,128)(2,1)S(1)} %bitcast.35), channel_id=1, source_target_pairs={{0,2},{1,3},{2,0},{3,1},{4,6},{5,7},{6,4},{7,5},{8,10},{9,11},{10,... | collective-permute-start | bytes 3145736 | tf_op jit(solution)/shard_map/ppermute | solution.py:68
  235.8 33.6 %collective-permute-start.25 = (bf16[512,1024]{1,0:T(8,128)(2,1)}, bf16[512,1024]{1,0:T(8,128)(2,1)S(1)}, u32[]{:S(2)}, u32[]{:S(2)}) collective-permute-start(bf16[512,1024]{1,0:T(8,128)(2,1)} %get-tuple-element.218), channel_id=1, source_target_pairs={{0,2},{1,3},{2,0},{3,1},{4,6},{5,7},{6,4},{7,5},{8,10},{9,11},{10,... | collective-permute-start | bytes 3145736 | tf_op jit(solution)/shard_map/ppermute | solution.py:68
  273.1 45.0 %all-to-all-start.4 = ((bf16[8,64,1024]{2,1,0:T(8,128)(2,1)}), bf16[8,64,1024]{2,1,0:T(8,128)(2,1)S(1)}, u32[]{:S(2)}, u32[]{:S(2)}) async-start(bf16[8,64,1024]{2,1,0:T(8,128)(2,1)} %bitcast.49), calls=%async_computation.4 | async-start | bytes 2097152 | tf_op jit(solution)/shard_map/all_to_all | solution.py:900
  279.9 22.0 %collective-permute-start.24 = (bf16[512,1024]{1,0:T(8,128)(2,1)S(1)}, bf16[512,1024]{1,0:T(8,128)(2,1)S(1)}, u32[]{:S(2)}, u32[]{:S(2)}) collective-permute-start(bf16[512,1024]{1,0:T(8,128)(2,1)S(1)} %copy-done.54), channel_id=1, source_target_pairs={{0,2},{1,3},{2,0},{3,1},{4,6},{5,7},{6,4},{7,5},{8,10},{9,11},{10,... | collective-permute-start | bytes 3145736 | tf_op jit(solution)/shard_map/ppermute | solution.py:68
  298.4 47.4 %collective-permute-start.27 = (bf16[1024,1024]{1,0:T(8,128)(2,1)}, bf16[1024,1024]{1,0:T(8,128)(2,1)}, u32[]{:S(2)}, u32[]{:S(2)}) collective-permute-start(bf16[1024,1024]{1,0:T(8,128)(2,1)} %get-tuple-element.239), channel_id=1, source_target_pairs={{0,1},{1,0},{2,3},{3,2},{4,5},{5,4},{6,7},{7,6},{8,9},{9,8},{10,11... | collective-permute-start | bytes 6291464 | tf_op jit(solution)/shard_map/ppermute | solution.py:68
  301.9 44.2 %collective-permute-start.26 = (bf16[1024,1024]{1,0:T(8,128)(2,1)}, bf16[1024,1024]{1,0:T(8,128)(2,1)}, u32[]{:S(2)}, u32[]{:S(2)}) collective-permute-start(bf16[1024,1024]{1,0:T(8,128)(2,1)} %expert_out_kernel.2), channel_id=1, source_target_pairs={{0,2},{1,3},{2,0},{3,1},{4,6},{5,7},{6,4},{7,5},{8,10},{9,11},{10,... | collective-permute-start | bytes 6291464 | tf_op jit(solution)/shard_map/ppermute | solution.py:68
  314.6 31.5 %collective-permute-start.28 = (bf16[1024,1024]{1,0:T(8,128)(2,1)}, bf16[1024,1024]{1,0:T(8,128)(2,1)}, u32[]{:S(2)}, u32[]{:S(2)}) collective-permute-start(bf16[1024,1024]{1,0:T(8,128)(2,1)} %down_outer_kernel.2), channel_id=1, source_target_pairs={{0,1},{1,0},{2,3},{3,2},{4,5},{5,4},{6,7},{7,6},{8,9},{9,8},{10,11... | collective-permute-start | bytes 6291464 | tf_op jit(solution)/shard_map/ppermute | solution.py:68
  318.1 29.6 %all-to-all-start.5 = ((bf16[8,64,1024]{2,1,0:T(8,128)(2,1)}), bf16[8,64,1024]{2,1,0:T(8,128)(2,1)S(1)}, u32[]{:S(2)}, u32[]{:S(2)}) async-start(bf16[8,64,1024]{2,1,0:T(8,128)(2,1)} %bitcast.18), calls=%async_computation.5 | async-start | bytes 2097152 | tf_op jit(solution)/shard_map/all_to_all | solution.py:900
  326.7 19.2 %collective-permute-start.29 = (f32[2,1024]{1,0:T(2,128)S(1)}, f32[2,1024]{1,0:T(2,128)S(1)}, u32[]{:S(2)}, u32[]{:S(2)}) collective-permute-start(f32[2,1024]{1,0:T(2,128)S(1)} %pad_maximum_fusion.2), channel_id=1, source_target_pairs={{0,1},{1,0},{2,3},{3,2},{4,5},{5,4},{6,7},{7,6},{8,9},{9,8},{10,11... | collective-permute-start | bytes 24584 | tf_op jit(solution)/shard_map/ppermute | solution.py:68
  369.8 112.3 %all-to-all-start.6 = ((bf16[8,128,1024]{2,1,0:T(8,128)(2,1)}), bf16[8,128,1024]{2,1,0:T(8,128)(2,1)S(1)}, u32[]{:S(2)}, u32[]{:S(2)}) async-start(bf16[8,128,1024]{2,1,0:T(8,128)(2,1)} %bitcast.48), calls=%async_computation.6 | async-start | bytes 4194304 | tf_op jit(solution)/shard_map/all_to_all | solution.py:900
  379.7 36.1 %collective-permute-start.34 = (bf16[2048,256]{1,0:T(8,128)(2,1)}, bf16[2048,256]{1,0:T(8,128)(2,1)S(1)}, u32[]{:S(2)}, u32[]{:S(2)}) collective-permute-start(bf16[2048,256]{1,0:T(8,128)(2,1)} %get-tuple-element.263), channel_id=1, source_target_pairs={{0,1},{1,0},{2,3},{3,2},{4,5},{5,4},{6,7},{7,6},{8,9},{9,8},{10,11... | collective-permute-start | bytes 3145736 | tf_op jit(solution)/shard_map/ppermute | solution.py:68
  419.5 30.5 %collective-permute-start.40 = (bf16[1024,256]{1,0:T(8,128)(2,1)}, bf16[1024,256]{1,0:T(8,128)(2,1)S(1)}, u32[]{:S(2)}, u32[]{:S(2)}) collective-permute-start(bf16[1024,256]{1,0:T(8,128)(2,1)} %get-tuple-element.294), channel_id=1, source_target_pairs={{0,2},{1,3},{2,0},{3,1},{4,6},{5,7},{6,4},{7,5},{8,10},{9,11},{10,... | collective-permute-start | bytes 1572872 | tf_op jit(solution)/shard_map/ppermute | solution.py:68
  458.3 37.8 %collective-permute-start.42 = (bf16[512,1024]{1,0:T(8,128)(2,1)}, bf16[512,1024]{1,0:T(8,128)(2,1)}, u32[]{:S(2)}, u32[]{:S(2)}) collective-permute-start(bf16[512,1024]{1,0:T(8,128)(2,1)} %get-tuple-element.297), channel_id=1, source_target_pairs={{0,1},{1,0},{2,3},{3,2},{4,5},{5,4},{6,7},{7,6},{8,9},{9,8},{10,11... | collective-permute-start | bytes 3145736 | tf_op jit(solution)/shard_map/ppermute | solution.py:68
  487.4 61.1 %collective-permute-start.39 = (bf16[512,1024]{1,0:T(8,128)(2,1)}, bf16[512,1024]{1,0:T(8,128)(2,1)}, u32[]{:S(2)}, u32[]{:S(2)}) collective-permute-start(bf16[512,1024]{1,0:T(8,128)(2,1)} %get-tuple-element.293), channel_id=1, source_target_pairs={{0,1},{1,0},{2,3},{3,2},{4,5},{5,4},{6,7},{7,6},{8,9},{9,8},{10,11... | collective-permute-start | bytes 3145736 | tf_op jit(solution)/shard_map/ppermute | solution.py:68
  495.8 63.2 %collective-permute-start.41 = (bf16[512,1024]{1,0:T(8,128)(2,1)}, bf16[512,1024]{1,0:T(8,128)(2,1)S(1)}, u32[]{:S(2)}, u32[]{:S(2)}) collective-permute-start(bf16[512,1024]{1,0:T(8,128)(2,1)} %get-tuple-element.300), channel_id=1, source_target_pairs={{0,1},{1,0},{2,3},{3,2},{4,5},{5,4},{6,7},{7,6},{8,9},{9,8},{10,11... | collective-permute-start | bytes 3145736 | tf_op jit(solution)/shard_map/ppermute | solution.py:68
  498.8 63.9 %collective-permute-start.43 = (bf16[512,1024]{1,0:T(8,128)(2,1)}, bf16[512,1024]{1,0:T(8,128)(2,1)S(1)}, u32[]{:S(2)}, u32[]{:S(2)}) collective-permute-start(bf16[512,1024]{1,0:T(8,128)(2,1)} %sum_kernel.16), channel_id=1, source_target_pairs={{0,2},{1,3},{2,0},{3,1},{4,6},{5,7},{6,4},{7,5},{8,10},{9,11},{10,... | collective-permute-start | bytes 3145736 | tf_op jit(solution)/shard_map/ppermute | solution.py:68
  522.0 24.0 %collective-permute-start.49 = (bf16[128,256]{1,0:T(8,128)(2,1)S(1)}, bf16[128,256]{1,0:T(8,128)(2,1)S(1)}, u32[]{:S(2)}, u32[]{:S(2)}) collective-permute-start(bf16[128,256]{1,0:T(8,128)(2,1)S(1)} %get-tuple-element.345), channel_id=1, source_target_pairs={{0,16},{4,20},{8,24},{12,28},{16,0},{20,4},{24,8},{28,12},{1,17},{... | collective-permute-start | bytes 196616 | tf_op jit(solution)/shard_map/ppermute | solution.py:73
  523.4 22.6 %collective-permute-start.48 = (bf16[128,256]{1,0:T(8,128)(2,1)S(1)}, bf16[128,256]{1,0:T(8,128)(2,1)S(1)}, u32[]{:S(2)}, u32[]{:S(2)}) collective-permute-start(bf16[128,256]{1,0:T(8,128)(2,1)S(1)} %get-tuple-element.346), channel_id=1, source_target_pairs={{0,8},{4,12},{8,0},{12,4},{16,24},{20,28},{24,16},{28,20},{1,9},{5... | collective-permute-start | bytes 196616 | tf_op jit(solution)/shard_map/ppermute | solution.py:73
  (84 other events, 1098.5 us)

commit v3 on v2

--- a/solution.py
+++ b/solution.py
@@ -30,8 +30,28 @@
     return lax.dot_general(a, b, dims, preferred_element_type=f32)
 
 
-def cost():
-    return pl.CostEstimate(flops=1, bytes_accessed=1, transcendentals=0)
+TIMES = {
+    "attend": 15,
+    "middle_kernel": 5,
+    "place_kernel": 3,
+    "attend_back": 19,
+    "project_kernel": 7,
+    "halves_kernel": 5,
+    "act_back_kernel": 9,
+    "expert_kernel": 10,
+    "expert_out_kernel": 9,
+    "up_outer_kernel": 9,
+    "down_outer_kernel": 9,
+    "output_weight_kernel": 4,
+    "out_sum_kernel": 4,
+    "input_weight_kernel": 9,
+    "input_back_kernel": 5,
+}
+
+
+def cost(name, part=1.0):
+    flops = int(part * TIMES.get(name, 0) * 1.1e9) + 1
+    return pl.CostEstimate(flops=flops, bytes_accessed=1, transcendentals=0)
 
 
 def whole_spec(x):
@@ -56,7 +76,7 @@
         out_shape=list(outs),
         scratch_shapes=list(scratch),
         compiler_params=pltpu.CompilerParams(vmem_limit_bytes=VMEM),
-        cost_estimate=cost(),
+        cost_estimate=cost(kernel_name(kernel)),
     )(*scalars, *ins)
 
 
@@ -88,11 +108,12 @@
     return plain_call(sum_kernel, parts, [struct(parts[0].shape, dtype)])[0]
 
 
-def turned_sum_kernel(*refs):
-    total = refs[0][...].astype(f32)
-    for ref in refs[1:-1]:
-        total = total + ref[...].astype(f32)
-    refs[-1][...] = total.T
+def turned_sum_kernel(blocks, out):
+    rows = out.shape[1]
+    total = blocks[:rows, :].astype(f32)
+    for at in range(rows, blocks.shape[0], rows):
+        total = total + blocks[at : at + rows, :].astype(f32)
+    out[...] = total.T
 
 
 def two_parts(x):
@@ -105,29 +126,28 @@
     return x[: x.shape[0] // 2] + x[x.shape[0] // 2 :]
 
 
-def first_fold_kernel(own, vector, got, kept, vectors, parts):
-    rows = own.shape[0]
-    kept[...] = own[...].astype(f32) + got[:rows, :].astype(f32)
-    vectors[...] = vector[...] + one_part(got[rows:, :])
-    parts[...] = two_parts(vectors[...])
-
-
-def fold_kernel(own, got, parts, out):
-    rows = own.shape[0]
-    out[:rows, :] = (own[...].astype(f32) + got[...].astype(f32)).astype(bf16)
-    out[rows:, :] = parts[...]
+def fold_kernel(own, vector, got, kept, vectors, *outs):
+    rows = kept.shape[0]
+    size = own.shape[0]
+    kept[...] = own[:rows, :].astype(f32) + got[:rows, :].astype(f32)
+    vectors[...] = vector[...] + one_part(got[size:, :])
+    parts = two_parts(vectors[...])
+    for at, out in enumerate(outs):
+        here = slice((at + 1) * rows, (at + 2) * rows)
+        out[:rows, :] = (own[here, :].astype(f32) + got[here, :].astype(f32)).astype(bf16)
+        out[rows:, :] = parts
 
 
 def last_fold_kernel(kept, vector, *refs):
     out, vectors = refs[-2:]
-    rows, width = kept.shape[0], out.shape[2]
+    rows, width = out.shape[1:]
     total = kept[...]
     sums = vector[...]
     for ref in refs[:-2]:
         total = total + ref[:rows, :].astype(f32)
         sums = sums + one_part(ref[rows:, :])
-    for j in range(out.shape[1]):
-        out[:, j, :] = total[:, j * width : (j + 1) * width]
+    for j in range(out.shape[0]):
+        out[j] = total[:, j * width : (j + 1) * width]
     vectors[...] = sums
 
 
@@ -146,7 +166,7 @@
     )
 
 
-def first_kernel(x, gain, shift, docs, w_in, w_out, bias, out, packed):
+def first_kernel(x, gain, shift, docs, w_in, w_out, bias, out, packed, copies):
     rows = x.shape[0]
     unit, _ = normed(x[...].astype(f32))
     out[:rows, :] = (unit * gain[...] + shift[...]).astype(bf16)
@@ -154,10 +174,12 @@
     out[rows : rows + EXTRA, :rows] = jnp.broadcast_to(
         docs[...].astype(f32), (EXTRA, rows)
     ).astype(bf16)
-    shard, width = w_in.shape[0], w_in.shape[2]
+    shard, width = w_in.shape[1:]
     for j in range(3):
-        packed[:shard, j * width : (j + 1) * width] = w_in[:, j, :]
-    packed[:shard, 3 * width :] = w_out[...].T
+        packed[:shard, j * width : (j + 1) * width] = w_in[j]
+    turned = w_out[...].T
+    for at in range(0, copies.shape[0], shard):
+        copies[at : at + shard, :] = turned
     packed[shard:, :] = jnp.zeros_like(packed[shard:, :])
     packed[shard:, :width] = bias[...]
 
@@ -193,14 +215,13 @@
 
 def project_kernel(n, rows, place, *refs):
     xs, ws = refs[:TP], refs[TP : TP + n]
-    q, k, v, w_in, w_out = refs[TP + n :]
+    q, k, v, w_in = refs[TP + n :]
     width = q.shape[1]
     bias = jnp.zeros((8, width), f32)
     lane = lax.rem(lax.broadcasted_iota(i32, (8, width), 1), HEAD_DIM) // (HEAD_DIM // n)
     for turn in range(n):
         base = pl.multiple_of((place[0] ^ turn) * rows, rows)
-        w_in[pl.ds(base, rows), :] = ws[turn][:rows, : 3 * width]
-        w_out[pl.ds(base, rows), :] = ws[turn][:rows, 3 * width :]
+        w_in[pl.ds(base, rows), :] = ws[turn][:rows, :]
         part = ws[turn][rows:, :width].astype(f32)[:8]
         bias = jnp.where(lane == (place[0] ^ turn), part, bias)
     block = q.shape[0] // TP
@@ -214,13 +235,16 @@
 
 def middle_kernel(*refs):
     ctxs, ws = refs[:TP], refs[TP : 2 * TP]
-    residual, bias, gain, shift, mixed, second = refs[-6:]
+    residual, bias, gain, shift, mixed, second, upper, lower = refs[-8:]
     total = residual[...].astype(f32) + bias[...]
     for r in range(TP):
         total = total + mxu(ctxs[r][...], ws[r][...], NT)
     mixed[...] = total
     unit, _ = normed(total)
     second[...] = (unit * gain[...] + shift[...]).astype(bf16)
+    half = upper.shape[0]
+    upper[...] = second[:half, :]
+    lower[...] = second[half:, :]
 
 
 def turn_kernel(*refs):
@@ -246,16 +270,13 @@
         outs[r][...] = mxu(low[...], ws[r][...]).astype(bf16)
 
 
-def output_weight_kernel(n, rows, place, *refs):
-    ctxs, low, kept, away, total = refs[:TP], refs[TP], refs[TP + 1], refs[TP + 2], refs[TP + 3]
-    size = total.shape[0]
+def output_weight_kernel(*refs):
+    ctxs, low, kept, away = refs[:TP], refs[TP], refs[TP + 1], refs[TP + 2]
+    size = low.shape[1]
     for r in range(TP):
-        total[...] = mxu(low[...], ctxs[r][...], TN)
         out = away if r & 1 else kept
-        for at, turn in enumerate(list(range(0, n, 2)) + list(range(1, n, 2))):
-            base = pl.multiple_of((place[0] ^ turn) * rows, rows)
-            to = (r // 2) * size + at * rows
-            out[to : to + rows, :] = total[pl.ds(base, rows), :].astype(bf16)
+        to = (r // 2) * size
+        out[to : to + size, :] = mxu(low[...], ctxs[r][...], TN).astype(bf16)
 
 
 def pair_sum_kernel(a, b, here, there):
@@ -287,7 +308,7 @@
 
 def input_weight_kernel(n, rows, count, place, *refs):
     xs, backs, w_in, sums2 = refs[:TP], refs[TP : TP + count], refs[TP + count], refs[TP + count + 1]
-    parts, vectors, small, total = refs[TP + count + 2 : -3], *refs[-3:]
+    keep, away, vectors, small, total = refs[TP + count + 2 :]
     pairs = count // 3
     width = w_in.shape[1] // 3
     block = backs[0].shape[0] // TP
@@ -304,7 +325,9 @@
         small[8 * j : 8 * j + 8, :] = column
     for turn in range(n):
         base = pl.multiple_of((place[0] ^ turn) * rows, rows)
-        parts[turn][:rows, :] = total[pl.ds(base, rows), :].astype(bf16)
+        dest = away if turn % 2 else keep
+        to = turn // 2 * rows
+        dest[to : to + rows, :] = total[pl.ds(base, rows), :].astype(bf16)
     w = w_in[...].astype(f32)
     column = jnp.concatenate([small[8 * j : 8 * j + 1, :] for j in range(3)], axis=1)
     lines = [lane_sums(total[...] * w)[:1], lane_sums(w * column)[:1]]
@@ -316,7 +339,7 @@
     rests = jnp.concatenate(rests, axis=1)
     for r in range(3):
         vectors[5 + r : 6 + r, :] = rests[:, 3 * width * r : 3 * width * (r + 1)]
-    parts[1][rows:, :] = two_parts(vectors[...])
+    away[n // 2 * rows :, :] = two_parts(vectors[...])
 
 
 def last_kernel(residual, gain, own, other, mixed_back, out):
@@ -414,7 +437,7 @@
         out_shape=[struct((bq, W), bf16)] * TP + [struct((8, S), f32)],
         input_output_aliases={6 + r: r for r in range(len(before))},
         compiler_params=pltpu.CompilerParams(vmem_limit_bytes=VMEM),
-        cost_estimate=cost(),
+        cost_estimate=cost("attend"),
     )(t, q, k, v, a, b, *before)
 
 
@@ -510,7 +533,7 @@
         ),
         out_shape=[struct((S, 128), bf16)] * 3,
         compiler_params=pltpu.CompilerParams(vmem_limit_bytes=VMEM),
-        cost_estimate=cost(),
+        cost_estimate=cost("attend_back"),
     )(t, q, k, v, *dos, *os, lse, a, b)
 
 
@@ -550,8 +573,16 @@
         in_specs=[smem_spec(), smem_spec()] + [tail] * TP,
         out_specs=[whole_spec(out)] * 2,
         out_shape=[out] * 2,
-        cost_estimate=cost(),
+        cost_estimate=cost("intervals"),
     )(here, starts, *xs)
+
+
+def place_halves_kernel(upper, lower, s, out):
+    spots = lax.broadcasted_iota(i32, (out.shape[0], s.shape[1]), 0)
+    pick = jnp.where(spots == s[0:1, :], 1.0, 0.0).astype(bf16)
+    half = upper.shape[0]
+    total = mxu(pick[:, :half], upper[...]) + mxu(pick[:, half:], lower[...])
+    out[...] = total.astype(bf16)
 
 
 def place_kernel(x, s, out):
@@ -668,8 +699,9 @@
     out[1] = down[...]
 
 
-def fill_kernel(lo, kept, other, out):
-    out[...] = other[...].astype(f32)
+def fill_kernel(lo, up, down, up_other, down_other, up_out, down_out):
+    up_out[...] = up_other[...].astype(f32)
+    down_out[...] = down_other[...].astype(f32)
 
 
 class Expert:
@@ -682,7 +714,7 @@
         self.up, self.down, self.other = up, down, other
         self.up_bias, self.up_bias_other = up_bias[:, None, :], up_bias_other
 
-    def call(self, kernel, grid, in_specs, out_specs, out_shape, args, alias=None, scratch=()):
+    def call(self, kernel, grid, in_specs, out_specs, out_shape, args, alias=None, scratch=(), part=1.0):
         return pl.pallas_call(
             kernel,
             name=kernel_name(kernel),
@@ -696,7 +728,7 @@
             out_shape=out_shape,
             input_output_aliases=alias or {},
             compiler_params=pltpu.CompilerParams(vmem_limit_bytes=VMEM),
-            cost_estimate=cost(),
+            cost_estimate=cost(kernel_name(kernel), part),
         )(self.lo, *args)
 
     def away(self, at):
@@ -746,7 +778,7 @@
             [x, act_back, self.up, self.other, self.up_bias, self.up_bias_other],
         )
 
-    def out(self, act_0, act_1):
+    def out(self, act_0, act_1, part=1.0):
         rows = act_0.shape[0]
         steps = rows // self.tile
         return self.call(
@@ -756,6 +788,7 @@
             self.row(self.width),
             struct((2 * rows, self.width), bf16),
             [act_0, act_1, self.down, self.other],
+            part=part,
         )
 
     def outer_specs(self, own):
@@ -765,7 +798,7 @@
             return out, struct((2, size, size), f32)
         return pl.BlockSpec((tile, size), lambda i, lo: (i, 0)), struct((size, size), bf16)
 
-    def up_outer(self, xs, backs, at, own):
+    def up_outer(self, xs, backs, at, own, part=1.0):
         size, count = self.width, len(xs)
         out, shape = self.outer_specs(own)
         return self.call(
@@ -776,9 +809,10 @@
             [out, pl.BlockSpec((8, size), lambda i, lo: (0, 0))],
             [shape, struct((8, size), f32)],
             list(xs) + list(backs),
+            part=part,
         )
 
-    def down_outer(self, acts, cots, at, own):
+    def down_outer(self, acts, cots, at, own, part=1.0):
         rows, size, count = acts[0].shape[0], self.width, len(acts)
         out, shape = self.outer_specs(own)
         return self.call(
@@ -789,6 +823,7 @@
             out,
             shape,
             list(acts) + list(cots),
+            part=part,
         )
 
     def halves(self, up, down):
@@ -803,19 +838,18 @@
             [up, down],
         )
 
-    def fill(self, kept, other):
-        size = other.shape[0]
+    def fill(self, up, down, up_other, down_other):
+        size = up_other.shape[0]
+        part = pl.BlockSpec((size // 4, size), lambda i, lo: (i, 0))
+        out = pl.BlockSpec((None, size // 4, size), lambda i, lo: (1 - lo[0], i, 0))
         return self.call(
             fill_kernel,
             (4,),
-            [
-                pl.BlockSpec(memory_space=pl.ANY),
-                pl.BlockSpec((size // 4, size), lambda i, lo: (i, 0)),
-            ],
-            pl.BlockSpec((None, size // 4, size), lambda i, lo: (1 - lo[0], i, 0)),
-            struct(kept.shape, f32),
-            [kept, other],
-            alias={1: 0},
+            [pl.BlockSpec(memory_space=pl.ANY)] * 2 + [part, part],
+            [out, out],
+            [struct(up.shape, f32), struct(down.shape, f32)],
+            [up, down, up_other, down_other],
+            alias={1: 0, 2: 1},
         )
 
 
@@ -857,21 +891,28 @@
 
     expert = Expert(lo, width, expert_up.shape[2])
 
+    def exchange(x):
+        return lax.all_to_all(x, "fsdp", split_axis=0, concat_axis=0, tiled=True)
+
     share = jnp.pad(
         jnp.tile(input_bias, (1, 1, n)).reshape(2, head_width), ((0, EXTRA - 2), (0, 0))
     )
-    x0, packed = plain_call(
+    x0, packed, copies = plain_call(
         first_kernel,
         [
             residual_in,
             row(first_norm_gain),
             row(first_norm_shift),
             document_index,
-            input_weight,
+            jnp.transpose(input_weight, (1, 0, 2)),
             output_weight,
             share,
         ],
-        [struct((rows + EXTRA, width), bf16), struct((shard + EXTRA, 4 * head_width), bf16)],
+        [
+            struct((rows + EXTRA, width), bf16),
+            struct((shard + EXTRA, 3 * head_width), bf16),
+            struct((n * shard, head_width), bf16),
+        ],
     )
     x2 = send_tp(x0, 2)
     weights = {0: packed}
@@ -884,7 +925,6 @@
     x1 = send_tp(after(x0, arrived), 1)
     x3 = send_tp(after(x2, arrived), 1)
     xs = [x0, x1, x2, x3]
-    halves_sent = expert.halves(*after((expert_up, expert_down), x1))
 
     here = jnp.concatenate([place, turn])
     length = TP * rows
@@ -896,16 +936,12 @@
         scalars=[here],
     )
 
-    def exchange(x):
-        return lax.all_to_all(x, "fsdp", split_axis=0, concat_axis=0, tiled=True)
-
     slotted = struct((n * cap, width), bf16)
     cot_sent_own = plain_call(place_kernel, [out_cotangent, s_own], [slotted])[0]
-    queries, keys, values, w_in, w_out0 = plain_call(
+    queries, keys, values, w_in = plain_call(
         functools.partial(project_kernel, n, shard),
-        list(after(tuple(xs), cot_sent_own, halves_sent)) + [weights[k] for k in range(n)],
-        [struct((length, head_width), bf16)] * 3
-        + [struct((width, 3 * head_width), bf16), struct((width, head_width), bf16)],
+        list(after(tuple(xs), cot_sent_own)) + [weights[k] for k in range(n)],
+        [struct((length, head_width), bf16)] * 3 + [struct((width, 3 * head_width), bf16)],
         scalars=[place],
     )
     cot_other = send_tp(after(cot_sent, queries), 1)
@@ -915,6 +951,8 @@
         [struct((8, rows), i32), slotted],
     )
     near_own = exchange(cot_sent_own)
+    halves_sent = expert.halves(*after((expert_up, expert_down), queries))
+    w_out0 = exchange(after(copies, near_own))
 
     halves_other = send_tp(after(halves_sent, queries), 1)
     down_bias = lax.dynamic_index_in_dim(expert_down_bias, lo, keepdims=True)
@@ -923,7 +961,7 @@
     w_out1 = send_tp(w_out0, 1)
     pairs = head_width // 128
     contexts, totals = [], []
-    firsts = [queries, (cot_other, near_own)]
+    firsts = [(near_own, halves_sent), (cot_other, w_out0)]
     cot_pieces = []
     for p in range(pairs):
         *contexts, total = attention_fwd(
@@ -937,8 +975,8 @@
             contexts,
         )
         if p == 0:
-            near_other = exchange(after(cot_sent_other, near_own, total))
-            far_own = send_tp(after(near_own, total, w_out1, w_out2, halves_other), 2)
+            near_other = exchange(after(cot_sent_other, w_out0, total))
+            far_own = send_tp(near_own, 2)
             cot_pieces = [near_own, far_own, near_other, send_tp(near_other, 2)]
         totals.append(total)
     w_outs = [w_out0, w_out1, w_out2, send_tp(after(w_out2, total), 1)]
@@ -946,7 +984,7 @@
     expert.hold(expert_up, expert_up_bias, None, expert_down, halves_other)
     act_backs, cot_sums = [None] * 4, [None] * 2
     act_backs[0], act_backs[1], cot_sums[0] = expert.act_back(*cot_pieces[:2])
-    mixed, second = plain_call(
+    mixed, second, upper, lower = plain_call(
         middle_kernel,
         ctxs
         + w_outs
@@ -956,7 +994,8 @@
             row(second_norm_gain),
             row(second_norm_shift),
         ],
-        [struct((rows, width), f32), struct((rows, width), bf16)],
+        [struct((rows, width), f32), struct((rows, width), bf16)]
+        + [struct((rows // 2, width), bf16)] * 2,
     )
 
     bias_sent = lax.dynamic_index_in_dim(after(expert_up_bias, second), 1 - lo, keepdims=True)
@@ -964,9 +1003,8 @@
     act_backs[2], act_backs[3], cot_sums[1] = expert.act_back(*cot_pieces[2:])
     cot_sum = added(*cot_sums, dtype=f32)[:1]
     sent_own = plain_call(place_kernel, [second, s_own], [slotted])[0]
-    second_other = send_tp(second, 1)
     sent_other = plain_call(
-        place_kernel, [second_other, s_other], [slotted]
+        place_halves_kernel, [send_tp(upper, 1), send_tp(lower, 1), s_other], [slotted]
     )[0]
     rows_own = exchange(after(sent_own, near_other))
     rows_other = exchange(after(sent_other, rows_own, cot_pieces[3]))
@@ -982,7 +1020,8 @@
 
     got_own = send_tp(x_backs[1], 2)
     got_other = send_tp(x_backs[3], 2)
-    back_sent_own = added(x_backs[0], after(got_own, x_backs[3]))
+    down_own = expert.down_outer(after(tuple(acts), x_backs[3]), cot_pieces, 0, True)
+    back_sent_own = added(x_backs[0], after(got_own, down_own))
     back_home_own = exchange(back_sent_own)
     out_far = expert.out(*after((acts[1], acts[3]), back_sent_own))
     up_away, up_sum_away = expert.up_outer(pieces, after(tuple(pre_backs), out_far), 1, False)
@@ -991,12 +1030,12 @@
     out_got = send_tp(after(out_far, got_other), 2)
     late = after(tuple(acts), back_sent_other)
     down_away = expert.down_outer(late, cot_pieces, 1, False)
-    out_near = expert.out(*after((acts[0], acts[2]), down_away))
-    up_own, up_sum = expert.up_outer(pieces, after(tuple(pre_backs), out_near), 0, True)
+    out_near = expert.out(*after((acts[0], acts[2]), down_away), part=0.3)
+    up_own, up_sum = expert.up_outer(pieces, after(tuple(pre_backs), out_near), 0, True, part=0.3)
     up_got, down_got = send_tp(up_away, 1), send_tp(down_away, 1)
     sent = send_tp(jnp.concatenate([up_sum_away[:1], cot_sum], axis=0), 1)
     back_own, back_away = collect(
-        s_own, s_other, back_home_own, after(back_home_other, up_own, up_got, down_got, out_got, sent)
+        s_own, s_other, back_home_own, after(back_home_other, up_own, out_got, sent)
     )
     back_other = send_tp(back_away, 1)
 
@@ -1012,17 +1051,20 @@
     )
 
     wo_kept, wo_away = plain_call(
-        functools.partial(output_weight_kernel, n, shard),
+        output_weight_kernel,
         ctxs + [mixed_low],
         [struct((2 * width, head_width), bf16)] * 2,
-        scratch=[pltpu.VMEM((width, head_width), f32)],
-        scalars=[place],
     )
     up_bias_back = ordered(lo, up_sum[0], sent[0])
     down_bias_back = ordered(lo, cot_sum[0], sent[1])
 
     dos = [ctx_backs[0]] + [send_tp(ctx_backs[r], r) for r in range(1, TP)]
-    wo_got = send_tp(wo_away, 1)
+    wo_sum, wo_there = plain_call(
+        pair_sum_kernel,
+        [wo_kept, send_tp(wo_away, 1)],
+        [struct((width, head_width), bf16)] * 2,
+    )
+    wo_got = send_tp(wo_there, 2)
     out_sent = plain_call(
         functools.partial(out_sum_kernel, cap),
         [out_near, after(out_got, dos[0]), down_bias],
@@ -1030,7 +1072,7 @@
     )[0]
     out_home = exchange(out_sent)
     projected_backs = []
-    firsts = [(wo_away, out_sent), None]
+    firsts = [(wo_sum, out_sent), None]
     for p in range(pairs):
         back = attention_bwd(
             p,
@@ -1046,14 +1088,8 @@
         )
         projected_backs += back
         if p == 0:
-            wo_sum, wo_there = plain_call(
-                pair_sum_kernel,
-                [wo_kept, after(wo_got, back)],
-                [struct((width, head_width), bf16)] * 2,
-            )
-            wo_got = send_tp(wo_there, 2)
-            firsts[1] = wo_sum
-    wo = added(wo_sum, after(wo_got, projected_backs))
+            wo = added(wo_sum, after(wo_got, back))
+            firsts[1] = (wo, up_got, down_got)
 
     def input_back(turns, first):
         return plain_call(
@@ -1062,22 +1098,14 @@
             [struct((rows, width), bf16)] * 2,
         )
 
-    middle = n // 2 * shard
-    wo_kept = added(wo[:middle], send_fsdp(wo[middle:], 1))
-    wo_parts = [wo_kept[:shard]] + [
-        send_fsdp(wo_kept[(at + 1) * shard : (at + 2) * shard], k)
-        for at, k in enumerate(evens[1:])
-    ]
-    output_weight_back = plain_call(
-        turned_sum_kernel, wo_parts, [struct((head_width, shard), f32)]
-    )[0]
-
-    *parts, vector = plain_call(
+    part3, part2 = input_back((3, 2), projected_backs[0])
+    got3 = send_tp(part3, 1)
+    keep, away, vector = plain_call(
         functools.partial(input_weight_kernel, n, shard, 3 * pairs),
-        xs + projected_backs + [w_in, sums2],
+        xs + projected_backs + [after(w_in, part3), sums2],
         [
-            struct((shard + (EXTRA if k == 1 else 0), 3 * head_width), bf16)
-            for k in range(n)
+            struct((n // 2 * shard, 3 * head_width), bf16),
+            struct((n // 2 * shard + EXTRA, 3 * head_width), bf16),
         ]
         + [struct((8, 3 * head_width), f32)],
         scratch=[
@@ -1086,70 +1114,60 @@
         ],
         scalars=[place],
     )
-    part3, part2 = input_back((3, 2), (parts[0], wo))
-    got3 = send_tp(part3, 1)
-    part1, part0 = input_back((1, 0), part3)
-    sum2 = added(part2, after(got3, part0))
+    got = send_fsdp(away, 1)
+    part1, part0 = input_back((1, 0), keep)
+    sum2 = added(part2, after(got3, keep))
     got2 = send_tp(sum2, 2)
     sum0 = added(part0, send_tp(part1, 1))
-    got = {k: send_fsdp(parts[k + 1], 1) for k in evens}
-    kept, vector, vector_parts = plain_call(
-        first_fold_kernel,
-        [parts[0], vector, got[0]],
-        [
-            struct((shard, 3 * head_width), f32),
-            struct((8, 3 * head_width), f32),
-            struct((EXTRA, 3 * head_width), bf16),
-        ],
-    )
-    folds = [
-        plain_call(
-            fold_kernel,
-            [parts[k], got[k], vector_parts],
-            [struct((shard + EXTRA, 3 * head_width), bf16)],
-        )[0]
-        for k in evens[1:]
-    ]
+    out_own, out_away = plain_call(
+        functools.partial(collect_both_kernel, cap),
+        [s_own, s_other, after(out_home, part0)],
+        [struct((rows, width), bf16)] * 2,
+    )
+    out_other = send_tp(out_away, 1)
+
+    kept, vector, *folds = plain_call(
+        fold_kernel,
+        [keep, vector, after(got, out_own, sum2)],
+        [struct((shard, 3 * head_width), f32), struct((8, 3 * head_width), f32)]
+        + [struct((shard + EXTRA, 3 * head_width), bf16)] * (n // 2 - 1),
+    )
     wi_kept = (kept, folds)
+    wo_home = exchange(after(wo, out_own))
+    output_weight_back = plain_call(
+        turned_sum_kernel, [wo_home], [struct((head_width, shard), f32)]
+    )[0]
     wi_total, vector = plain_call(
         last_fold_kernel,
         [kept, vector] + [send_fsdp(fold, k) for fold, k in zip(folds, evens[1:])],
-        [struct((shard, 3, head_width), f32), struct((8, 3 * head_width), f32)],
-    )
-
-    out_own, out_away = plain_call(
-        functools.partial(collect_both_kernel, cap),
-        [s_own, s_other, after(out_home, wi_kept)],
-        [struct((rows, width), bf16)] * 2,
-    )
-    out_other = send_tp(out_away, 1)
-    block_output = added(mixed, out_own, out_other)
-
-    down_own = expert.down_outer(after(tuple(acts), wi_kept), cot_pieces, 0, True)
-    up_back = expert.fill(up_own, up_got)
-    down_back = expert.fill(down_own, down_got)
+        [struct((3, shard, head_width), f32), struct((8, 3 * head_width), f32)],
+    )
+
+    up_back, down_back = expert.fill(after(up_own, wi_kept), down_own, up_got, down_got)
+    block_output = added(mixed, after(out_own, up_back), out_other)
+
+    back_residual = plain_call(
+        last_kernel,
+        [residual_in, row(first_norm_gain), sum0, got2, mixed_back],
+        [struct((rows, width), f32)],
+    )[0]
+
     tails = vector[5:].reshape(-1)
     bias_sum = tails[5 * head_width : 7 * head_width]
     bias_sum = bias_sum.reshape(2, head_width // HEAD_DIM, n, HEAD_DIM // n)
     input_bias_back = lax.dynamic_index_in_dim(bias_sum, g, axis=2, keepdims=False)
-    vector = after(vector, up_back, down_back, block_output, output_weight_back)
-    vector = added(vector, send_tp(vector, 1), dtype=f32)
-    vector = added(vector, send_tp(vector, 2), dtype=f32)
+    vector = after(vector, up_back, back_residual)
+    vector = added(after(vector, block_output), send_tp(vector, 1), dtype=f32)
+    vector = added(after(vector, output_weight_back), send_tp(vector, 2), dtype=f32)
     tails = vector[5:].reshape(-1)[: 5 * head_width].reshape(5, head_width)
     vectors = jnp.concatenate([vector[:5], tails], axis=1)
-    back_residual = plain_call(
-        last_kernel,
-        [residual_in, row(first_norm_gain), sum0, got2, after(mixed_back, vectors)],
-        [struct((rows, width), f32)],
-    )[0]
-
     first_gain_back = (vectors[0] - first_norm_shift * vectors[1]) / first_norm_gain
     return (
         block_output,
         back_residual,
         first_gain_back,
         vectors[1],
-        wi_total,
+        jnp.transpose(wi_total, (1, 0, 2)),
         input_bias_back,
         output_weight_back,
         vectors[4],

time: 586 us -> 515 us (0.88)
  waiting for transfers between devices: 116 us -> 61.7 us
  local copies, waits for them, and re-layouts: 31.3 us -> 22.1 us
    ppermute x35 -> x36, waiting for transfers between devices: 64.3 us -> 12 us  [send_tp(): return lax.ppermute(x, 'tp', [(i, i ^ turn) for i in range(TP)])]
    ppermute x18 -> x11, waiting for transfers between devices: 47.4 us -> 26.3 us  [send_fsdp(): return lax.ppermute(x, 'fsdp', [(i, i ^ turn) for i in range(n)])]
    all_to_all x7 -> x9, waiting for transfers between devices: 4.71 us -> 23.4 us  [exchange(): return lax.all_to_all(x, 'fsdp', split_axis=0, concat_axis=0, tiled=True)]
    all_to_all x7 -> x9, starting transfers between devices: 40.3 us -> 54.4 us  [exchange(): return lax.all_to_all(x, 'fsdp', split_axis=0, concat_axis=0, tiled=True)]
    ppermute x35 -> x36, starting transfers between devices: 39.2 us -> 30.2 us  [send_tp(): return lax.ppermute(x, 'tp', [(i, i ^ turn) for i in range(TP)])]
    ppermute x18 -> x11, starting transfers between devices: 24 us -> 15.5 us  [send_fsdp(): return lax.ppermute(x, 'fsdp', [(i, i ^ turn) for i in range(n)])]
    unnamed x114 -> x92, local copies, waits for them, and re-layouts: 21.1 us -> 13.4 us
    pallas_call x34 -> x30, Pallas kernels: 115 us -> 109 us  [plain_call(): pl.pallas_call(kernel, name=kernel_name(kernel), grid=(1,), in_specs=[sme...]
  transfers between devices with their start and end apart: 60 -> 56, of which waited for: 29 -> 17; matrix products, arithmetic and copies ran while one was open for 2% -> 2% of each run, Pallas kernels for 50% -> 59%
where the time goes in v3:
time: 515 us; the launch traced here: 506 us
  Pallas kernels  317 us (62%)
  starting transfers between devices  100 us (19%)
  waiting for transfers between devices  61.7 us (12%)
  local copies, waits for them, and re-layouts  22.1 us (4%)
    pallas_call x14, Pallas kernels, call(): pl.pallas_call(kernel, name=kernel_name(kernel), grid_spec=pltpu.Prefetch...  126 us
    pallas_call x30, Pallas kernels, plain_call(): pl.pallas_call(kernel, name=kernel_name(kernel), grid=(1,), in_specs=[sme...  109 us
    all_to_all x9, starting transfers between devices, exchange(): return lax.all_to_all(x, 'fsdp', split_axis=0, concat_axis=0, tiled=True)  54.4 us
    pallas_call x2, Pallas kernels, attention_bwd(): pl.pallas_call(attend_back_kernel, name='attend_back', grid_spec=pltpu.Pr...  44.9 us
    pallas_call x2, Pallas kernels, attention_fwd(): pl.pallas_call(attend_kernel, name='attend', grid_spec=pltpu.PrefetchScal...  35.2 us
    ppermute x36, starting transfers between devices, send_tp(): return lax.ppermute(x, 'tp', [(i, i ^ turn) for i in range(TP)])  30.2 us
    ppermute x11, waiting for transfers between devices, send_fsdp(): return lax.ppermute(x, 'fsdp', [(i, i ^ turn) for i in range(n)])  26.3 us
    all_to_all x9, waiting for transfers between devices, exchange(): return lax.all_to_all(x, 'fsdp', split_axis=0, concat_axis=0, tiled=True)  23.4 us
  transfers between devices with their start and end apart: 56, of which 17 were waited for; matrix products, arithmetic and copies ran while one was open for 2% of the time, Pallas kernels for 59%

profile of v3, /device:TPU:9, one launch (start us, length us, event | category | flops | bytes accessed | tf_op | source)
XLA Modules:
  0.0 506.0 jit_solution(18236066270793143889)
XLA Ops:
  12.8 11.1 %collective-permute-done.2.refs_10_ = bf16[144,768]{1,0:T(8,128)(2,1)S(1)} collective-permute-done((bf16[144,768]{1,0:T(8,128)(2,1)}, bf16[144,768]{1,0:T(8,128)(2,1)S(1)}, u32[]{:S(2)}, u32[]{:S(2)}) %collective-permute-start.2) | collective-permute-done | bytes 221216 | tf_op jit(solution)/shard_map/ppermute | solution.py:93
  49.0 7.6 %project_kernel.1 = (bf16[2048,256]{1,0:T(8,128)(2,1)}, bf16[2048,256]{1,0:T(8,128)(2,1)}, bf16[2048,256]{1,0:T(8,128)(2,1)}, bf16[1024,768]{1,0:T(8,128)(2,1)}) custom-call(s32[1]{0:T(128)} %bitcast.1.place, bf16[528,1024]{1,0:T(8,128)(2,1)} %get-tuple-element.175.refs_0_, bf16[528,1024]{1,0:T(8,128)(2,1)} %copy-done.10, bf16[528,1024]{1,0:T(8,128)(2,1)} %copy-done.9, ...), custom_call_target="tpu_custom_call" | custom-call | flops 7700000256 | bytes 1 | tf_op jit(solution)/shard_map/project_kernel/pallas_call | solution.py:70
  63.9 5.9 %all-to-all-done = bf16[8,64,1024]{2,1,0:T(8,128)(2,1)} async-done(((bf16[8,64,1024]{2,1,0:T(8,128)(2,1)}), bf16[8,64,1024]{2,1,0:T(8,128)(2,1)}, u32[]{:S(2)}, u32[]{:S(2)}) %all-to-all-start) | async-done | bytes 1048608 | tf_op jit(solution)/shard_map/all_to_all | solution.py:895
  71.0 6.9 %all-to-all-start.1 = ((bf16[8,128,256]{2,1,0:T(8,128)(2,1)}), bf16[8,128,256]{2,1,0:T(8,128)(2,1)S(1)}, u32[]{:S(2)}, u32[]{:S(2)}) async-start(bf16[8,128,256]{2,1,0:T(8,128)(2,1)} %bitcast.7), calls=%async_computation.1 | async-start | bytes 1048576 | tf_op jit(solution)/shard_map/all_to_all | solution.py:895
  77.9 17.6 %attend.2 = (bf16[512,256]{1,0:T(8,128)(2,1)}, bf16[512,256]{1,0:T(8,128)(2,1)}, bf16[512,256]{1,0:T(8,128)(2,1)}, bf16[512,256]{1,0:T(8,128)(2,1)}, f32[8,2048]{1,0:T(8,128)}) custom-call(s32[1]{0:T(128)} %bitcast.t_ref, bf16[2048,256]{1,0:T(8,128)(2,1)} %get-tuple-element.286.q_ref, bf16[2048,256]{1,0:T(8,128)(2,1)} %get-tuple-element.190.k_ref, ...), custom_call_target="tpu_custom_call" | custom-call | flops 16499999744 | bytes 1 | tf_op jit(solution)/shard_map/attend/pallas_call | solution.py:425
  101.3 5.6 %all-to-all-start.2 = ((bf16[8,64,1024]{2,1,0:T(8,128)(2,1)}), bf16[8,64,1024]{2,1,0:T(8,128)(2,1)S(1)}, u32[]{:S(2)}, u32[]{:S(2)}) async-start(bf16[8,64,1024]{2,1,0:T(8,128)(2,1)} %bitcast.61), calls=%async_computation.2 | async-start | bytes 2097152 | tf_op jit(solution)/shard_map/all_to_all | solution.py:895
  106.9 17.6 %attend.3 = (bf16[512,256]{1,0:T(8,128)(2,1)}, bf16[512,256]{1,0:T(8,128)(2,1)}, bf16[512,256]{1,0:T(8,128)(2,1)}, bf16[512,256]{1,0:T(8,128)(2,1)}, f32[8,2048]{1,0:T(8,128)}) custom-call(s32[1]{0:T(128)} %bitcast.t_ref, bf16[2048,256]{1,0:T(8,128)(2,1)} %get-tuple-element.286.q_ref, ...), custom_call_target="tpu_custom_call", output_to_operand_aliasing={{0}: (6, {}), {1}: (7, {}), {2}: (8, {}), {3}: (9, {})} | custom-call | flops 16499999744 | bytes 1 | tf_op jit(solution)/shard_map/attend/pallas_call | solution.py:425
  127.0 9.3 %act_back_kernel.2 = (bf16[512,2048]{1,0:T(8,128)(2,1)}, bf16[512,2048]{1,0:T(8,128)(2,1)}, f32[8,1024]{1,0:T(8,128)}) custom-call(s32[1]{0:T(128)} %bitcast.9.lo, bf16[512,1024]{1,0:T(8,128)(2,1)} %bitcast.6.near.refs_4_, bf16[512,1024]{1,0:T(8,128)(2,1)} %collective-permute-done.17.far.refs_5_, bf16[2,1024,1024]{2,1,0:T(8,128)(2,1)} %down_a.7, ...), custom_call_target="tpu_custom_call" | custom-call | flops 9900000256 | bytes 1 | tf_op jit(solution)/shard_map/act_back_kernel/pallas_call | solution.py:718
  140.1 5.6 %middle_kernel.1 = (f32[512,1024]{1,0:T(8,128)}, bf16[512,1024]{1,0:T(8,128)(2,1)}, bf16[256,1024]{1,0:T(8,128)(2,1)}, bf16[256,1024]{1,0:T(8,128)(2,1)}) custom-call(bf16[512,256]{1,0:T(8,128)(2,1)} %get-tuple-element.200.refs_0_.rest_4_, bf16[512,256]{1,0:T(8,128)(2,1)} %copy-done.36, bf16[512,256]{1,0:T(8,128)(2,1)} %copy-done.37, ...), custom_call_target="tpu_custom_call" | custom-call | flops 5500000256 | bytes 1 | tf_op jit(solution)/shard_map/middle_kernel/pallas_call | solution.py:70
  162.5 15.1 %all-to-all-done.3 = bf16[8,64,1024]{2,1,0:T(8,128)(2,1)S(1)} async-done(((bf16[8,64,1024]{2,1,0:T(8,128)(2,1)}), bf16[8,64,1024]{2,1,0:T(8,128)(2,1)S(1)}, u32[]{:S(2)}, u32[]{:S(2)}) %all-to-all-start.3) | async-done | bytes 1048608 | tf_op jit(solution)/shard_map/all_to_all | solution.py:895
  178.8 6.2 %all-to-all-start.4 = ((bf16[8,64,1024]{2,1,0:T(8,128)(2,1)}), bf16[8,64,1024]{2,1,0:T(8,128)(2,1)S(1)}, u32[]{:S(2)}, u32[]{:S(2)}) async-start(bf16[8,64,1024]{2,1,0:T(8,128)(2,1)} %bitcast.50), calls=%async_computation.4 | async-start | bytes 2097152 | tf_op jit(solution)/shard_map/all_to_all | solution.py:895
  185.1 9.4 %act_back_kernel.3 = (bf16[512,2048]{1,0:T(8,128)(2,1)}, bf16[512,2048]{1,0:T(8,128)(2,1)}, f32[8,1024]{1,0:T(8,128)}) custom-call(s32[1]{0:T(128)} %bitcast.9.lo, bf16[512,1024]{1,0:T(8,128)(2,1)} %bitcast.58, bf16[512,1024]{1,0:T(8,128)(2,1)} %collective-permute-done.19.far.refs_7_, bf16[2,1024,1024]{2,1,0:T(8,128)(2,1)} %down_a.7, ...), custom_call_target="tpu_custom_call" | custom-call | flops 9900000256 | bytes 1 | tf_op jit(solution)/shard_map/act_back_kernel/pallas_call | solution.py:718
  195.1 10.3 %expert_kernel.4 = (bf16[512,2048]{1,0:T(8,128)(2,1)}, bf16[512,2048]{1,0:T(8,128)(2,1)}, bf16[512,1024]{1,0:T(8,128)(2,1)}) custom-call(s32[1]{0:T(128)} %bitcast.9.lo, bf16[512,1024]{1,0:T(8,128)(2,1)} %bitcast.39, bf16[512,2048]{1,0:T(8,128)(2,1)} %get-tuple-element.207.act_back, bf16[2,1024,1024]{2,1,0:T(8,128)(2,1)} %up_a.7, ...), custom_call_target="tpu_custom_call" | custom-call | flops 11000000512 | bytes 1 | tf_op jit(solution)/shard_map/expert_kernel/pallas_call | solution.py:718
  207.9 10.7 %expert_kernel.5 = (bf16[512,2048]{1,0:T(8,128)(2,1)}, bf16[512,2048]{1,0:T(8,128)(2,1)}, bf16[512,1024]{1,0:T(8,128)(2,1)}) custom-call(s32[1]{0:T(128)} %bitcast.9.lo, bf16[512,1024]{1,0:T(8,128)(2,1)} %copy-done.11, bf16[512,2048]{1,0:T(8,128)(2,1)} %get-tuple-element.224.act_back, bf16[2,1024,1024]{2,1,0:T(8,128)(2,1)} %up_a.7, ...), custom_call_target="tpu_custom_call" | custom-call | flops 11000000512 | bytes 1 | tf_op jit(solution)/shard_map/expert_kernel/pallas_call | solution.py:718
  219.8 10.3 %expert_kernel.6 = (bf16[512,2048]{1,0:T(8,128)(2,1)}, bf16[512,2048]{1,0:T(8,128)(2,1)}, bf16[512,1024]{1,0:T(8,128)(2,1)}) custom-call(s32[1]{0:T(128)} %bitcast.9.lo, bf16[512,1024]{1,0:T(8,128)(2,1)} %bitcast.43, bf16[512,2048]{1,0:T(8,128)(2,1)} %get-tuple-element.227.act_back, bf16[2,1024,1024]{2,1,0:T(8,128)(2,1)} %up_a.7, ...), custom_call_target="tpu_custom_call" | custom-call | flops 11000000512 | bytes 1 | tf_op jit(solution)/shard_map/expert_kernel/pallas_call | solution.py:718
  231.8 10.8 %expert_kernel.7 = (bf16[512,2048]{1,0:T(8,128)(2,1)}, bf16[512,2048]{1,0:T(8,128)(2,1)}, bf16[512,1024]{1,0:T(8,128)(2,1)}) custom-call(s32[1]{0:T(128)} %bitcast.9.lo, bf16[512,1024]{1,0:T(8,128)(2,1)} %copy-done.13, bf16[512,2048]{1,0:T(8,128)(2,1)} %get-tuple-element.215.act_back, bf16[2,1024,1024]{2,1,0:T(8,128)(2,1)} %up_a.7, ...), custom_call_target="tpu_custom_call" | custom-call | flops 11000000512 | bytes 1 | tf_op jit(solution)/shard_map/expert_kernel/pallas_call | solution.py:718
  242.6 9.1 %down_outer_kernel.2.down = f32[2,1024,1024]{2,1,0:T(8,128)} custom-call(s32[1]{0:T(128)} %bitcast.9.lo, bf16[512,2048]{1,0:T(8,128)(2,1)} %get-tuple-element.256.refs_0_.act_0, bf16[512,2048]{1,0:T(8,128)(2,1)} %get-tuple-element.253.refs_1_.act_0, bf16[512,2048]{1,0:T(8,128)(2,1)} %get-tuple-element.257.refs_2_.act_1, ...), custom_call_target="tpu_custom_call" | custom-call | flops 9900000256 | bytes 1 | tf_op jit(solution)/shard_map/down_outer_kernel/pallas_call | solution.py:718
  257.0 8.0 %all-to-all-start.5 = ((bf16[8,64,1024]{2,1,0:T(8,128)(2,1)}), bf16[8,64,1024]{2,1,0:T(8,128)(2,1)S(1)}, u32[]{:S(2)}, u32[]{:S(2)}) async-start(bf16[8,64,1024]{2,1,0:T(8,128)(2,1)} %bitcast.47), calls=%async_computation.5 | async-start | bytes 2097152 | tf_op jit(solution)/shard_map/all_to_all | solution.py:895
  265.0 8.9 %expert_out_kernel.2 = bf16[1024,1024]{1,0:T(8,128)(2,1)} custom-call(s32[1]{0:T(128)} %bitcast.9.lo, bf16[512,2048]{1,0:T(8,128)(2,1)} %get-tuple-element.253.refs_1_.act_0, bf16[512,2048]{1,0:T(8,128)(2,1)} %get-tuple-element.255.refs_3_.act_1, bf16[2,1024,1024]{2,1,0:T(8,128)(2,1)} %down_a.7, bf16[2,1024,1024]{2,1,0:T(8,128)(2,1)} %collective-permute-done.18.down_b.up_b), custom_call_target="tpu_custom_call" | custom-call | flops 9900000256 | bytes 1 | tf_op jit(solution)/shard_map/expert_out_kernel/pallas_call | solution.py:718
  275.7 9.7 %up_outer_kernel.2 = (bf16[1024,1024]{1,0:T(8,128)(2,1)}, f32[8,1024]{1,0:T(8,128)}) custom-call(s32[1]{0:T(128)} %bitcast.9.lo, bf16[512,1024]{1,0:T(8,128)(2,1)} %bitcast.40, bf16[512,1024]{1,0:T(8,128)(2,1)} %copy-done.11, bf16[512,1024]{1,0:T(8,128)(2,1)} %bitcast.44, bf16[512,1024]{1,0:T(8,128)(2,1)} %copy-done.13, ...), custom_call_target="tpu_custom_call" | custom-call | flops 9900000256 | bytes 1 | tf_op jit(solution)/shard_map/up_outer_kernel/pallas_call | solution.py:718
  288.2 8.2 %all-to-all-start.6 = ((bf16[8,64,1024]{2,1,0:T(8,128)(2,1)}), bf16[8,64,1024]{2,1,0:T(8,128)(2,1)S(1)}, u32[]{:S(2)}, u32[]{:S(2)}) async-start(bf16[8,64,1024]{2,1,0:T(8,128)(2,1)} %bitcast.46), calls=%async_computation.6 | async-start | bytes 2097152 | tf_op jit(solution)/shard_map/all_to_all | solution.py:895
  301.5 8.7 %down_outer_kernel.3 = bf16[1024,1024]{1,0:T(8,128)(2,1)} custom-call(s32[1]{0:T(128)} %bitcast.9.lo, bf16[512,2048]{1,0:T(8,128)(2,1)} %get-tuple-element.256.refs_0_.act_0, bf16[512,2048]{1,0:T(8,128)(2,1)} %get-tuple-element.253.refs_1_.act_0, bf16[512,2048]{1,0:T(8,128)(2,1)} %get-tuple-element.257.refs_2_.act_1, ...), custom_call_target="tpu_custom_call" | custom-call | flops 9900000256 | bytes 1 | tf_op jit(solution)/shard_map/down_outer_kernel/pallas_call | solution.py:718
  310.2 9.0 %expert_out_kernel.3.near = bf16[1024,1024]{1,0:T(8,128)(2,1)} custom-call(s32[1]{0:T(128)} %bitcast.9.lo, bf16[512,2048]{1,0:T(8,128)(2,1)} %get-tuple-element.256.refs_0_.act_0, bf16[512,2048]{1,0:T(8,128)(2,1)} %get-tuple-element.257.refs_2_.act_1, bf16[2,1024,1024]{2,1,0:T(8,128)(2,1)} %down_a.7, bf16[2,1024,1024]{2,1,0:T(8,128)(2,1)} %collective-permute-done.18.down_b.up_b), custom_call_target="tpu_custom_call" | custom-call | flops 2969999872 | bytes 1 | tf_op jit(solution)/shard_map/expert_out_kernel/pallas_call | solution.py:718
  319.2 9.5 %up_outer_kernel.3 = (f32[2,1024,1024]{2,1,0:T(8,128)}, f32[8,1024]{1,0:T(8,128)}) custom-call(s32[1]{0:T(128)} %bitcast.9.lo, bf16[512,1024]{1,0:T(8,128)(2,1)} %bitcast.41, bf16[512,1024]{1,0:T(8,128)(2,1)} %copy-done.11, bf16[512,1024]{1,0:T(8,128)(2,1)} %bitcast.45, bf16[512,1024]{1,0:T(8,128)(2,1)} %copy-done.13, ...), custom_call_target="tpu_custom_call" | custom-call | flops 2969999872 | bytes 1 | tf_op jit(solution)/shard_map/up_outer_kernel/pallas_call | solution.py:718
  337.4 6.8 %turn_kernel.1 = (f32[512,1024]{1,0:T(8,128)}, bf16[512,1024]{1,0:T(8,128)(2,1)}, f32[8,1024]{1,0:T(8,128)}, bf16[512,256]{1,0:T(8,128)(2,1)}, bf16[512,256]{1,0...) custom-call(bf16[1024,256]{1,0:T(8,128)(2,1)} %bitcast.54, bf16[1024,256]{1,0:T(8,128)(2,1)} %copy-done.21, ...), custom_call_target="tpu_custom_call" | custom-call | flops 1 | bytes 1 | tf_op jit(solution)/shard_map/turn_kernel/pallas_call | solution.py:70
  356.8 5.7 %all-to-all-start.7 = ((bf16[8,128,1024]{2,1,0:T(8,128)(2,1)}), bf16[8,128,1024]{2,1,0:T(8,128)(2,1)S(1)}, u32[]{:S(2)}, u32[]{:S(2)}) async-start(bf16[8,128,1024]{2,1,0:T(8,128)(2,1)} %bitcast.56), calls=%async_computation.7 | async-start | bytes 4194304 | tf_op jit(solution)/shard_map/all_to_all | solution.py:895
  365.9 22.4 %attend_back.2 = (bf16[2048,128]{1,0:T(8,128)(2,1)}, bf16[2048,128]{1,0:T(8,128)(2,1)}, bf16[2048,128]{1,0:T(8,128)(2,1)}) custom-call(s32[1]{0:T(128)} %bitcast.t_ref, bf16[2048,256]{1,0:T(8,128)(2,1)} %get-tuple-element.286.q_ref, bf16[2048,256]{1,0:T(8,128)(2,1)} %get-tuple-element.190.k_ref, bf16[2048,256]{1,0:T(8,128)(2,1)} %get-tuple-element.191.v_ref, ...), custom_call_target="tpu_custom_call" | custom-call | flops 20899999744 | bytes 1 | tf_op jit(solution)/shard_map/attend_back/pallas_call | solution.py:516
  391.3 22.5 %attend_back.3 = (bf16[2048,128]{1,0:T(8,128)(2,1)}, bf16[2048,128]{1,0:T(8,128)(2,1)}, bf16[2048,128]{1,0:T(8,128)(2,1)}) custom-call(s32[1]{0:T(128)} %bitcast.t_ref, bf16[2048,256]{1,0:T(8,128)(2,1)} %get-tuple-element.286.q_ref, bf16[2048,256]{1,0:T(8,128)(2,1)} %get-tuple-element.190.k_ref, bf16[2048,256]{1,0:T(8,128)(2,1)} %get-tuple-element.191.v_ref, ...), custom_call_target="tpu_custom_call" | custom-call | flops 20899999744 | bytes 1 | tf_op jit(solution)/shard_map/attend_back/pallas_call | solution.py:516
  419.9 9.2 %input_weight_kernel.1 = (bf16[512,768]{1,0:T(8,128)(2,1)}, bf16[528,768]{1,0:T(8,128)(2,1)}, f32[8,768]{1,0:T(8,128)}) custom-call(s32[1]{0:T(128)} %bitcast.1.place, bf16[528,1024]{1,0:T(8,128)(2,1)} %get-tuple-element.175.refs_0_, bf16[528,1024]{1,0:T(8,128)(2,1)} %copy-done.10, bf16[528,1024]{1,0:T(8,128)(2,1)} %copy-done.9, ...), custom_call_target="tpu_custom_call" | custom-call | flops 9900000256 | bytes 1 | tf_op jit(solution)/shard_map/input_weight_kernel/pallas_call | solution.py:70
  434.3 5.5 %collective-permute-start.37 = (bf16[528,768]{1,0:T(8,128)(2,1)}, bf16[528,768]{1,0:T(8,128)(2,1)}, u32[]{:S(2)}, u32[]{:S(2)}) collective-permute-start(bf16[528,768]{1,0:T(8,128)(2,1)} %get-tuple-element.301), channel_id=1, source_target_pairs={{0,4},{4,0},{8,12},{12,8},{16,20},{20,16},{24,28},{28,24},{1,5},{5... | collective-permute-start | bytes 2433032 | tf_op jit(solution)/shard_map/ppermute | solution.py:93
  453.6 6.2 %collective-permute-done.37.got = bf16[528,768]{1,0:T(8,128)(2,1)} collective-permute-done((bf16[528,768]{1,0:T(8,128)(2,1)}, bf16[528,768]{1,0:T(8,128)(2,1)}, u32[]{:S(2)}, u32[]{:S(2)}) %collective-permute-start.37) | collective-permute-done | bytes 811040 | tf_op jit(solution)/shard_map/ppermute | solution.py:93
  469.1 5.8 %fill_kernel.1 = (f32[2,1024,1024]{2,1,0:T(8,128)}, f32[2,1024,1024]{2,1,0:T(8,128)}) custom-call(s32[1]{0:T(128)} %bitcast.9.lo, f32[2,1024,1024]{2,1,0:T(8,128)} %get-tuple-element.309.up, f32[2,1024,1024]{2,1,0:T(8,128)} %down_outer_kernel.2.down, ...), custom_call_target="tpu_custom_call", output_to_operand_aliasing={{0}: (1, {}), {1}: (2, {})} | custom-call | flops 1 | bytes 1 | tf_op jit(solution)/shard_map/fill_kernel/pallas_call | solution.py:718
  (245 shorter events, 189.4 us)
Async XLA Ops:
  5.4 24.9 %collective-permute-start.5 = (bf16[528,1024]{1,0:T(8,128)(2,1)}, bf16[528,1024]{1,0:T(8,128)(2,1)S(1)}, u32[]{:S(2)}, u32[]{:S(2)}) collective-permute-start(bf16[528,1024]{1,0:T(8,128)(2,1)} %get-tuple-element.175.refs_0_), channel_id=1, source_target_pairs={{0,2},{1,3},{2,0},{3,1},{4,6},{5,7},{6,4},{7,5},{8,10},{9,11},{10,... | collective-permute-start | bytes 3244040 | tf_op jit(solution)/shard_map/ppermute | solution.py:88
  42.2 27.5 %all-to-all-start = ((bf16[8,64,1024]{2,1,0:T(8,128)(2,1)}), bf16[8,64,1024]{2,1,0:T(8,128)(2,1)}, u32[]{:S(2)}, u32[]{:S(2)}) async-start(bf16[8,64,1024]{2,1,0:T(8,128)(2,1)} %bitcast.63), calls=%async_computation | async-start | bytes 2097152 | tf_op jit(solution)/shard_map/all_to_all | solution.py:895
  61.4 65.5 %collective-permute-start.18 = (bf16[2,1024,1024]{2,1,0:T(8,128)(2,1)}, bf16[2,1024,1024]{2,1,0:T(8,128)(2,1)}, u32[]{:S(2)}, u32[]{:S(2)}) collective-permute-start(bf16[2,1024,1024]{2,1,0:T(8,128)(2,1)} %halves_kernel.1), channel_id=1, source_target_pairs={{0,1},{1,0},{2,3},{3,2},{4,5},{5,4},{6,7},{7,6},{8,9},{9,8},{10,11... | collective-permute-start | bytes 12582920 | tf_op jit(solution)/shard_map/ppermute | solution.py:88
  62.2 33.2 %collective-permute-start.10 = (bf16[528,1024]{1,0:T(8,128)(2,1)S(1)}, bf16[528,1024]{1,0:T(8,128)(2,1)S(1)}, u32[]{:S(2)}, u32[]{:S(2)}) collective-permute-start(bf16[528,1024]{1,0:T(8,128)(2,1)S(1)} %copy-done.35), channel_id=1, source_target_pairs={{0,1},{1,0},{2,3},{3,2},{4,5},{5,4},{6,7},{7,6},{8,9},{9,8},{10,11... | collective-permute-start | bytes 3244040 | tf_op jit(solution)/shard_map/ppermute | solution.py:88
  69.8 56.6 %collective-permute-start.17 = (bf16[512,1024]{1,0:T(8,128)(2,1)}, bf16[512,1024]{1,0:T(8,128)(2,1)}, u32[]{:S(2)}, u32[]{:S(2)}) collective-permute-start(bf16[512,1024]{1,0:T(8,128)(2,1)} %bitcast.6.near.refs_4_), channel_id=1, source_target_pairs={{0,2},{1,3},{2,0},{3,1},{4,6},{5,7},{6,4},{7,5},{8,10},{9,11},{10,... | collective-permute-start | bytes 3145736 | tf_op jit(solution)/shard_map/ppermute | solution.py:88
  71.0 28.5 %all-to-all-start.1 = ((bf16[8,128,256]{2,1,0:T(8,128)(2,1)}), bf16[8,128,256]{2,1,0:T(8,128)(2,1)S(1)}, u32[]{:S(2)}, u32[]{:S(2)}) async-start(bf16[8,128,256]{2,1,0:T(8,128)(2,1)} %bitcast.7), calls=%async_computation.1 | async-start | bytes 1048576 | tf_op jit(solution)/shard_map/all_to_all | solution.py:895
  99.5 25.7 %collective-permute-start.15 = (bf16[1024,256]{1,0:T(8,128)(2,1)S(1)}, bf16[1024,256]{1,0:T(8,128)(2,1)S(1)}, u32[]{:S(2)}, u32[]{:S(2)}) collective-permute-start(bf16[1024,256]{1,0:T(8,128)(2,1)S(1)} %bitcast.51), channel_id=1, source_target_pairs={{0,2},{1,3},{2,0},{3,1},{4,6},{5,7},{6,4},{7,5},{8,10},{9,11},{10,... | collective-permute-start | bytes 1572872 | tf_op jit(solution)/shard_map/ppermute | solution.py:88
  99.7 39.3 %collective-permute-start.14 = (bf16[1024,256]{1,0:T(8,128)(2,1)S(1)}, bf16[1024,256]{1,0:T(8,128)(2,1)S(1)}, u32[]{:S(2)}, u32[]{:S(2)}) collective-permute-start(bf16[1024,256]{1,0:T(8,128)(2,1)S(1)} %bitcast.52), channel_id=1, source_target_pairs={{0,1},{1,0},{2,3},{3,2},{4,5},{5,4},{6,7},{7,6},{8,9},{9,8},{10,11... | collective-permute-start | bytes 1572872 | tf_op jit(solution)/shard_map/ppermute | solution.py:88
  101.3 47.3 %all-to-all-start.2 = ((bf16[8,64,1024]{2,1,0:T(8,128)(2,1)}), bf16[8,64,1024]{2,1,0:T(8,128)(2,1)S(1)}, u32[]{:S(2)}, u32[]{:S(2)}) async-start(bf16[8,64,1024]{2,1,0:T(8,128)(2,1)} %bitcast.61), calls=%async_computation.2 | async-start | bytes 2097152 | tf_op jit(solution)/shard_map/all_to_all | solution.py:895
  148.6 29.0 %all-to-all-start.3 = ((bf16[8,64,1024]{2,1,0:T(8,128)(2,1)}), bf16[8,64,1024]{2,1,0:T(8,128)(2,1)S(1)}, u32[]{:S(2)}, u32[]{:S(2)}) async-start(bf16[8,64,1024]{2,1,0:T(8,128)(2,1)} %bitcast.62), calls=%async_computation.3 | async-start | bytes 2097152 | tf_op jit(solution)/shard_map/all_to_all | solution.py:895
  154.0 24.9 %collective-permute-start.19 = (bf16[512,1024]{1,0:T(8,128)(2,1)S(1)}, bf16[512,1024]{1,0:T(8,128)(2,1)}, u32[]{:S(2)}, u32[]{:S(2)}) collective-permute-start(bf16[512,1024]{1,0:T(8,128)(2,1)S(1)} %bitcast.57), channel_id=1, source_target_pairs={{0,2},{1,3},{2,0},{3,1},{4,6},{5,7},{6,4},{7,5},{8,10},{9,11},{10,... | collective-permute-start | bytes 3145736 | tf_op jit(solution)/shard_map/ppermute | solution.py:88
  156.9 37.7 %collective-permute-start.20 = (f32[1,1024]{1,0:T(1,128)S(1)}, f32[1,1024]{1,0:T(1,128)S(1)}, u32[]{:S(2)}, u32[]{:S(2)}) collective-permute-start(f32[1,1024]{1,0:T(1,128)S(1)} %constant_dynamic-slice_fusion.2), channel_id=1, source_target_pairs={{0,1},{1,0},{2,3},{3,2},{4,5},{5,4},{6,7},{7,6},{8,9},{9,8},{10,11... | collective-permute-start | bytes 12296 | tf_op jit(solution)/shard_map/ppermute | solution.py:88
  177.6 27.9 %collective-permute-start.23 = (bf16[512,1024]{1,0:T(8,128)(2,1)S(1)}, bf16[512,1024]{1,0:T(8,128)(2,1)S(1)}, u32[]{:S(2)}, u32[]{:S(2)}) collective-permute-start(bf16[512,1024]{1,0:T(8,128)(2,1)S(1)} %bitcast.38), channel_id=1, source_target_pairs={{0,2},{1,3},{2,0},{3,1},{4,6},{5,7},{6,4},{7,5},{8,10},{9,11},{10,... | collective-permute-start | bytes 3145736 | tf_op jit(solution)/shard_map/ppermute | solution.py:88
  178.8 29.1 %all-to-all-start.4 = ((bf16[8,64,1024]{2,1,0:T(8,128)(2,1)}), bf16[8,64,1024]{2,1,0:T(8,128)(2,1)S(1)}, u32[]{:S(2)}, u32[]{:S(2)}) async-start(bf16[8,64,1024]{2,1,0:T(8,128)(2,1)} %bitcast.50), calls=%async_computation.4 | async-start | bytes 2097152 | tf_op jit(solution)/shard_map/all_to_all | solution.py:895
  207.9 22.9 %collective-permute-start.24 = (bf16[512,1024]{1,0:T(8,128)(2,1)S(1)}, bf16[512,1024]{1,0:T(8,128)(2,1)S(1)}, u32[]{:S(2)}, u32[]{:S(2)}) collective-permute-start(bf16[512,1024]{1,0:T(8,128)(2,1)S(1)} %bitcast.42), channel_id=1, source_target_pairs={{0,2},{1,3},{2,0},{3,1},{4,6},{5,7},{6,4},{7,5},{8,10},{9,11},{10,... | collective-permute-start | bytes 3145736 | tf_op jit(solution)/shard_map/ppermute | solution.py:88
  218.6 34.7 %collective-permute-start.26 = (bf16[512,1024]{1,0:T(8,128)(2,1)}, bf16[512,1024]{1,0:T(8,128)(2,1)S(1)}, u32[]{:S(2)}, u32[]{:S(2)}) collective-permute-start(bf16[512,1024]{1,0:T(8,128)(2,1)} %get-tuple-element.225), channel_id=1, source_target_pairs={{0,2},{1,3},{2,0},{3,1},{4,6},{5,7},{6,4},{7,5},{8,10},{9,11},{10,... | collective-permute-start | bytes 3145736 | tf_op jit(solution)/shard_map/ppermute | solution.py:88
  242.6 33.1 %collective-permute-start.25 = (bf16[512,1024]{1,0:T(8,128)(2,1)}, bf16[512,1024]{1,0:T(8,128)(2,1)S(1)}, u32[]{:S(2)}, u32[]{:S(2)}) collective-permute-start(bf16[512,1024]{1,0:T(8,128)(2,1)} %get-tuple-element.234), channel_id=1, source_target_pairs={{0,2},{1,3},{2,0},{3,1},{4,6},{5,7},{6,4},{7,5},{8,10},{9,11},{10,... | collective-permute-start | bytes 3145736 | tf_op jit(solution)/shard_map/ppermute | solution.py:88
  257.0 31.2 %all-to-all-start.5 = ((bf16[8,64,1024]{2,1,0:T(8,128)(2,1)}), bf16[8,64,1024]{2,1,0:T(8,128)(2,1)S(1)}, u32[]{:S(2)}, u32[]{:S(2)}) async-start(bf16[8,64,1024]{2,1,0:T(8,128)(2,1)} %bitcast.47), calls=%async_computation.5 | async-start | bytes 2097152 | tf_op jit(solution)/shard_map/all_to_all | solution.py:895
  275.7 53.0 %collective-permute-start.27 = (bf16[1024,1024]{1,0:T(8,128)(2,1)}, bf16[1024,1024]{1,0:T(8,128)(2,1)}, u32[]{:S(2)}, u32[]{:S(2)}) collective-permute-start(bf16[1024,1024]{1,0:T(8,128)(2,1)} %expert_out_kernel.2), channel_id=1, source_target_pairs={{0,2},{1,3},{2,0},{3,1},{4,6},{5,7},{6,4},{7,5},{8,10},{9,11},{10,... | collective-permute-start | bytes 6291464 | tf_op jit(solution)/shard_map/ppermute | solution.py:88
  288.2 40.5 %all-to-all-start.6 = ((bf16[8,64,1024]{2,1,0:T(8,128)(2,1)}), bf16[8,64,1024]{2,1,0:T(8,128)(2,1)S(1)}, u32[]{:S(2)}, u32[]{:S(2)}) async-start(bf16[8,64,1024]{2,1,0:T(8,128)(2,1)} %bitcast.46), calls=%async_computation.6 | async-start | bytes 2097152 | tf_op jit(solution)/shard_map/all_to_all | solution.py:895
  299.4 29.4 %collective-permute-start.28 = (f32[2,1024]{1,0:T(2,128)S(1)}, f32[2,1024]{1,0:T(2,128)S(1)}, u32[]{:S(2)}, u32[]{:S(2)}) collective-permute-start(f32[2,1024]{1,0:T(2,128)S(1)} %pad_maximum_fusion.1), channel_id=1, source_target_pairs={{0,1},{1,0},{2,3},{3,2},{4,5},{5,4},{6,7},{7,6},{8,9},{9,8},{10,11... | collective-permute-start | bytes 24584 | tf_op jit(solution)/shard_map/ppermute | solution.py:88
  349.3 42.0 %collective-permute-start.35 = (bf16[1024,1024]{1,0:T(8,128)(2,1)}, bf16[1024,1024]{1,0:T(8,128)(2,1)}, u32[]{:S(2)}, u32[]{:S(2)}) collective-permute-start(bf16[1024,1024]{1,0:T(8,128)(2,1)} %get-tuple-element.250), channel_id=1, source_target_pairs={{0,1},{1,0},{2,3},{3,2},{4,5},{5,4},{6,7},{7,6},{8,9},{9,8},{10,11... | collective-permute-start | bytes 6291464 | tf_op jit(solution)/shard_map/ppermute | solution.py:88
  349.7 41.6 %collective-permute-start.36 = (bf16[1024,1024]{1,0:T(8,128)(2,1)}, bf16[1024,1024]{1,0:T(8,128)(2,1)}, u32[]{:S(2)}, u32[]{:S(2)}) collective-permute-start(bf16[1024,1024]{1,0:T(8,128)(2,1)} %down_outer_kernel.3), channel_id=1, source_target_pairs={{0,1},{1,0},{2,3},{3,2},{4,5},{5,4},{6,7},{7,6},{8,9},{9,8},{10,11... | collective-permute-start | bytes 6291464 | tf_op jit(solution)/shard_map/ppermute | solution.py:88
  356.8 86.8 %all-to-all-start.7 = ((bf16[8,128,1024]{2,1,0:T(8,128)(2,1)}), bf16[8,128,1024]{2,1,0:T(8,128)(2,1)S(1)}, u32[]{:S(2)}, u32[]{:S(2)}) async-start(bf16[8,128,1024]{2,1,0:T(8,128)(2,1)} %bitcast.56), calls=%async_computation.7 | async-start | bytes 4194304 | tf_op jit(solution)/shard_map/all_to_all | solution.py:895
  365.2 23.1 %collective-permute-start.34 = (bf16[1024,256]{1,0:T(8,128)(2,1)}, bf16[1024,256]{1,0:T(8,128)(2,1)S(1)}, u32[]{:S(2)}, u32[]{:S(2)}) collective-permute-start(bf16[1024,256]{1,0:T(8,128)(2,1)} %get-tuple-element.284), channel_id=1, source_target_pairs={{0,2},{1,3},{2,0},{3,1},{4,6},{5,7},{6,4},{7,5},{8,10},{9,11},{10,... | collective-permute-start | bytes 1572872 | tf_op jit(solution)/shard_map/ppermute | solution.py:88
  419.0 20.8 %collective-permute-start.38 = (bf16[512,1024]{1,0:T(8,128)(2,1)}, bf16[512,1024]{1,0:T(8,128)(2,1)}, u32[]{:S(2)}, u32[]{:S(2)}) collective-permute-start(bf16[512,1024]{1,0:T(8,128)(2,1)} %get-tuple-element.292), channel_id=1, source_target_pairs={{0,1},{1,0},{2,3},{3,2},{4,5},{5,4},{6,7},{7,6},{8,9},{9,8},{10,11... | collective-permute-start | bytes 3145736 | tf_op jit(solution)/shard_map/ppermute | solution.py:88
  434.3 28.0 %collective-permute-start.40 = (bf16[512,1024]{1,0:T(8,128)(2,1)}, bf16[512,1024]{1,0:T(8,128)(2,1)S(1)}, u32[]{:S(2)}, u32[]{:S(2)}) collective-permute-start(bf16[512,1024]{1,0:T(8,128)(2,1)} %get-tuple-element.313), channel_id=1, source_target_pairs={{0,1},{1,0},{2,3},{3,2},{4,5},{5,4},{6,7},{7,6},{8,9},{9,8},{10,11... | collective-permute-start | bytes 3145736 | tf_op jit(solution)/shard_map/ppermute | solution.py:88
  434.3 25.5 %collective-permute-start.37 = (bf16[528,768]{1,0:T(8,128)(2,1)}, bf16[528,768]{1,0:T(8,128)(2,1)}, u32[]{:S(2)}, u32[]{:S(2)}) collective-permute-start(bf16[528,768]{1,0:T(8,128)(2,1)} %get-tuple-element.301), channel_id=1, source_target_pairs={{0,4},{4,0},{8,12},{12,8},{16,20},{20,16},{24,28},{28,24},{1,5},{5... | collective-permute-start | bytes 2433032 | tf_op jit(solution)/shard_map/ppermute | solution.py:93
  442.5 32.4 %collective-permute-start.41 = (bf16[512,1024]{1,0:T(8,128)(2,1)}, bf16[512,1024]{1,0:T(8,128)(2,1)}, u32[]{:S(2)}, u32[]{:S(2)}) collective-permute-start(bf16[512,1024]{1,0:T(8,128)(2,1)} %sum_kernel.13), channel_id=1, source_target_pairs={{0,2},{1,3},{2,0},{3,1},{4,6},{5,7},{6,4},{7,5},{8,10},{9,11},{10,... | collective-permute-start | bytes 3145736 | tf_op jit(solution)/shard_map/ppermute | solution.py:88
  448.8 41.6 %collective-permute-start.39 = (bf16[512,1024]{1,0:T(8,128)(2,1)}, bf16[512,1024]{1,0:T(8,128)(2,1)S(1)}, u32[]{:S(2)}, u32[]{:S(2)}) collective-permute-start(bf16[512,1024]{1,0:T(8,128)(2,1)} %get-tuple-element.312), channel_id=1, source_target_pairs={{0,1},{1,0},{2,3},{3,2},{4,5},{5,4},{6,7},{7,6},{8,9},{9,8},{10,11... | collective-permute-start | bytes 3145736 | tf_op jit(solution)/shard_map/ppermute | solution.py:88
  449.9 48.2 %all-to-all-start.8 = ((bf16[8,128,256]{2,1,0:T(8,128)(2,1)}), bf16[8,128,256]{2,1,0:T(8,128)(2,1)S(1)}, u32[]{:S(2)}, u32[]{:S(2)}) async-start(bf16[8,128,256]{2,1,0:T(8,128)(2,1)} %bitcast.25), calls=%async_computation.8 | async-start | bytes 1048576 | tf_op jit(solution)/shard_map/all_to_all | solution.py:895
  462.3 20.4 %collective-permute-start.44 = (bf16[144,768]{1,0:T(8,128)(2,1)}, bf16[144,768]{1,0:T(8,128)(2,1)S(1)}, u32[]{:S(2)}, u32[]{:S(2)}) collective-permute-start(bf16[144,768]{1,0:T(8,128)(2,1)} %get-tuple-element.308), channel_id=1, source_target_pairs={{0,24},{4,28},{8,16},{12,20},{16,8},{20,12},{24,0},{28,4},{1,25},{... | collective-permute-start | bytes 663560 | tf_op jit(solution)/shard_map/ppermute | solution.py:93
  (70 other events, 916.3 us)

commit v4 on v3

--- a/solution.py
+++ b/solution.py
@@ -31,12 +31,10 @@
 
 
 TIMES = {
-    "attend": 15,
+    "attend": 22,
     "middle_kernel": 5,
     "place_kernel": 3,
-    "attend_back": 19,
-    "project_kernel": 7,
-    "halves_kernel": 5,
+    "attend_back": 30,
     "act_back_kernel": 9,
     "expert_kernel": 10,
     "expert_out_kernel": 9,
@@ -44,8 +42,7 @@
     "down_outer_kernel": 9,
     "output_weight_kernel": 4,
     "out_sum_kernel": 4,
-    "input_weight_kernel": 9,
-    "input_back_kernel": 5,
+    "projection_back_kernel": 13,
 }
 
 
@@ -108,6 +105,10 @@
     return plain_call(sum_kernel, parts, [struct(parts[0].shape, dtype)])[0]
 
 
+def pairs_sum_kernel(a, b, c, d, out):
+    out[...] = (a[...] + b[...]) + (c[...] + d[...])
+
+
 def turned_sum_kernel(blocks, out):
     rows = out.shape[1]
     total = blocks[:rows, :].astype(f32)
@@ -130,7 +131,7 @@
     rows = kept.shape[0]
     size = own.shape[0]
     kept[...] = own[:rows, :].astype(f32) + got[:rows, :].astype(f32)
-    vectors[...] = vector[...] + one_part(got[size:, :])
+    vectors[...] = one_part(two_parts(vector[...])) + one_part(got[size:, :])
     parts = two_parts(vectors[...])
     for at, out in enumerate(outs):
         here = slice((at + 1) * rows, (at + 2) * rows)
@@ -142,13 +143,15 @@
     out, vectors = refs[-2:]
     rows, width = out.shape[1:]
     total = kept[...]
-    sums = vector[...]
+    sums = [one_part(two_parts(vector[...]))]
     for ref in refs[:-2]:
         total = total + ref[:rows, :].astype(f32)
-        sums = sums + one_part(ref[rows:, :])
+        sums.append(one_part(ref[rows:, :]))
+    while len(sums) > 1:
+        sums = [a + b for a, b in zip(sums[0::2], sums[1::2])]
     for j in range(out.shape[0]):
         out[j] = total[:, j * width : (j + 1) * width]
-    vectors[...] = sums
+    vectors[...] = sums[0]
 
 
 def normed(values):
@@ -286,43 +289,34 @@
         out[...] = (a[rows, :].astype(f32) + b[rows, :].astype(f32)).astype(bf16)
 
 
-def input_back_kernel(count, turns, *refs):
-    backs, w_in, outs = refs[:count], refs[count], refs[count + 1 :]
-    pairs = count // 3
-    width = w_in.shape[1] // 3
-    block = outs[0].shape[0]
-    for at, r in enumerate(turns):
-        here = pl.ds(r * block, block)
-        total = None
-        for j in range(3):
-            back = jnp.concatenate([backs[3 * p + j][here, :] for p in range(pairs)], axis=1)
-            part = mxu(back, w_in[:, j * width : (j + 1) * width], NT)
-            total = part if total is None else total + part
-        outs[at][...] = total.astype(bf16)
-
-
 def lane_sums(x):
     total = jnp.sum(x, axis=1, keepdims=True)
     return jnp.broadcast_to(total, (x.shape[0], 128)).T[:8]
 
 
-def input_weight_kernel(n, rows, count, place, *refs):
-    xs, backs, w_in, sums2 = refs[:TP], refs[TP : TP + count], refs[TP + count], refs[TP + count + 1]
-    keep, away, vectors, small, total = refs[TP + count + 2 :]
-    pairs = count // 3
+def projection_back_kernel(n, rows, place, *refs):
+    xs, backs, w_in, sums2 = refs[:TP], refs[TP : TP + 3], refs[TP + 3], refs[TP + 4]
+    outs, keep, away, vectors, small, total = refs[TP + 5 : -5], *refs[-5:]
     width = w_in.shape[1] // 3
     block = backs[0].shape[0] // TP
     ones = jnp.ones((8, block), bf16)
     for j in range(3):
-        part = jnp.zeros((total.shape[0], width), f32)
-        column = jnp.zeros((8, width), f32)
+        part, column = None, None
         for r in range(TP):
             here = pl.ds(r * block, block)
-            back = jnp.concatenate([backs[3 * p + j][here, :] for p in range(pairs)], axis=1)
-            part += mxu(xs[r][:block, :], back, TN)
-            column += mxu(ones, back)
+            back = backs[j][here, :]
+            term, ends = mxu(xs[r][:block, :], back, TN), mxu(ones, back)
+            part = term if part is None else part + term
+            column = ends if column is None else column + ends
         total[:, j * width : (j + 1) * width] = part
         small[8 * j : 8 * j + 8, :] = column
+    for r in range(TP):
+        here = pl.ds(r * block, block)
+        term = None
+        for j in range(3):
+            product = mxu(backs[j][here, :], w_in[:, j * width : (j + 1) * width], NT)
+            term = product if term is None else term + product
+        outs[r][...] = term.astype(bf16)
     for turn in range(n):
         base = pl.multiple_of((place[0] ^ turn) * rows, rows)
         dest = away if turn % 2 else keep
@@ -365,47 +359,52 @@
     return pl.multiple_of(((kb // per) ^ t) * block + lax.rem(kb, per) * BLOCK_K, BLOCK_K)
 
 
+def lanes(p):
+    return slice(128 * p, 128 * (p + 1))
+
+
 def attend_kernel(t_ref, q_ref, k_ref, v_ref, a_ref, b_ref, *rest):
-    outs, lse_ref, vt = rest[-TP - 2 : -2], rest[-2], rest[-1]
+    outs, lse_ref, vt = rest[:TP], rest[TP], rest[TP + 1]
     i = pl.program_id(0)
-    bq = q_ref.shape[0]
+    bq, width = q_ref.shape
     bk = BLOCK_K
+    pairs = range(width // 128)
+    heads = [(p, h) for p in pairs for h in (0, 1)]
 
     @pl.when(i == 0)
     def _():
         vt[...] = v_ref[...].T
 
-    qt = q_ref[...].T
-    qz = [half_rows(qt, h) for h in (0, 1)]
+    qts = [q_ref[:, lanes(p)].T for p in pairs]
+    qz = [half_rows(qts[p], h) for p, h in heads]
     a = a_ref[...]
     b = b_ref[...]
 
     def body(kb, carry):
         base = key_base(kb, bq, t_ref[0])
-        kblk = k_ref[pl.ds(base, bk), :]
+        here = pl.ds(base, bk)
         j = kb * bk + lax.broadcasted_iota(i32, (bk, bq), 0)
         mask = (j >= a) & (j <= b)
+        products = [mxu(k_ref[here, lanes(p)], z) for (p, h), z in zip(heads, qz)]
+        ss = [jnp.where(mask, s, MASKED) for s in products]
+        tops = [
+            jnp.maximum(c[0], jnp.max(s, axis=0, keepdims=True)) for c, s in zip(carry, ss)
+        ]
+        ps = [jnp.exp(s - top) for s, top in zip(ss, tops)]
         out = []
-        for h in (0, 1):
-            m, l, acc = carry[h]
-            s = jnp.where(mask, mxu(kblk, qz[h]), MASKED)
-            mn = jnp.maximum(m, jnp.max(s, axis=0, keepdims=True))
-            p = jnp.exp(s - mn)
-            al = jnp.exp(m - mn)
-            l = al * l + jnp.sum(p, axis=0, keepdims=True)
-            acc = acc * al + mxu(
-                vt[pl.ds(HEAD_DIM * h, HEAD_DIM), pl.ds(base, bk)], p.astype(bf16)
-            )
-            out.append((mn, l, acc))
+        for at, (m, l, acc) in enumerate(carry):
+            al = jnp.exp(m - tops[at])
+            l = al * l + jnp.sum(ps[at], axis=0, keepdims=True)
+            part = mxu(vt[pl.ds(HEAD_DIM * at, HEAD_DIM), here], ps[at].astype(bf16))
+            out.append((tops[at], l, acc * al + part))
         return tuple(out)
 
     init = tuple(
         (jnp.full((1, bq), MASKED, f32), jnp.zeros((1, bq), f32), jnp.zeros((HEAD_DIM, bq), f32))
-        for _ in (0, 1)
+        for _ in heads
     )
     res = lax.fori_loop(jnp.min(a) // bk, jnp.max(b) // bk + 1, body, init)
-    ot = jnp.concatenate([acc / l for m, l, acc in res], axis=0)
-    o = ot.T.astype(bf16)
+    o = jnp.concatenate([acc / l for m, l, acc in res], axis=0).T.astype(bf16)
     for r in range(TP):
 
         @pl.when(i == r)
@@ -413,14 +412,14 @@
             outs[r][...] = o
 
     lse_ref[...] = jnp.concatenate(
-        [m + jnp.log(l) for m, l, acc in res] + [jnp.zeros((6, bq), f32)], axis=0
-    )
-
-
-def attention_fwd(pair, q, k, v, a, b, t, before):
+        [m + jnp.log(l) for m, l, acc in res] + [jnp.zeros((8 - len(heads), bq), f32)], axis=0
+    )
+
+
+def attention_fwd(q, k, v, a, b, t):
     S, W = q.shape
     bq = S // TP
-    whole = pl.BlockSpec((S, 128), lambda i, *_: (0, pair))
+    whole = pl.BlockSpec((S, W), lambda i, *_: (0, 0))
     row = pl.BlockSpec((1, bq), lambda i, *_: (0, i))
     return pl.pallas_call(
         attend_kernel,
@@ -428,25 +427,25 @@
         grid_spec=pltpu.PrefetchScalarGridSpec(
             num_scalar_prefetch=1,
             grid=(TP,),
-            in_specs=[pl.BlockSpec((bq, 128), lambda i, *_: (i, pair)), whole, whole, row, row]
-            + [pl.BlockSpec(memory_space=pl.ANY)] * len(before),
-            out_specs=[pl.BlockSpec((bq, 128), lambda i, *_: (0, pair))] * TP
+            in_specs=[pl.BlockSpec((bq, W), lambda i, *_: (i, 0)), whole, whole, row, row],
+            out_specs=[pl.BlockSpec((bq, W), lambda i, *_: (0, 0))] * TP
             + [pl.BlockSpec((8, bq), lambda i, *_: (0, i))],
-            scratch_shapes=[pltpu.VMEM((128, S), bf16)],
+            scratch_shapes=[pltpu.VMEM((W, S), bf16)],
         ),
         out_shape=[struct((bq, W), bf16)] * TP + [struct((8, S), f32)],
-        input_output_aliases={6 + r: r for r in range(len(before))},
         compiler_params=pltpu.CompilerParams(vmem_limit_bytes=VMEM),
         cost_estimate=cost("attend"),
-    )(t, q, k, v, a, b, *before)
+    )(t, q, k, v, a, b)
 
 
 def attend_back_kernel(t_ref, q_ref, k_ref, v_ref, *rest):
     dos, os = rest[:TP], rest[TP : 2 * TP]
     lse_ref, a_ref, b_ref, dq_ref, dk_ref, dv_ref, kt, dk_acc, dv_acc, do_s, o_s = rest[2 * TP :]
     i = pl.program_id(0)
-    bq = q_ref.shape[0]
+    bq, width = q_ref.shape
     bk = BLOCK_K
+    pairs = range(width // 128)
+    heads = [(p, h) for p in pairs for h in (0, 1)]
 
     @pl.when(i == 0)
     def _():
@@ -461,42 +460,47 @@
             do_s[...] = dos[r][...]
             o_s[...] = os[r][...]
 
-    q = q_ref[...]
-    do = do_s[...]
-    qt = q.T
-    dot_ = do.T
-    qz = [half_rows(qt, h) for h in (0, 1)]
-    dz = [half_rows(dot_, h) for h in (0, 1)]
-    qcat = jnp.concatenate([half_lanes(q, 0), half_lanes(q, 1)], axis=0)
-    dcat = jnp.concatenate([half_lanes(do, 0), half_lanes(do, 1)], axis=0)
-    prod = (do.astype(f32) * o_s[...].astype(f32)).T
+    def split(x):
+        turned = [x[:, lanes(p)].T for p in pairs]
+        rows = [half_rows(turned[p], h) for p, h in heads]
+        both = [
+            jnp.concatenate([half_lanes(x[:, lanes(p)], h) for h in (0, 1)], axis=0) for p in pairs
+        ]
+        return rows, both
+
+    qz, qcat = split(q_ref[...])
+    dz, dcat = split(do_s[...])
+    prod = (do_s[...].astype(f32) * o_s[...].astype(f32)).T
     delta = [
-        jnp.sum(prod[:HEAD_DIM], axis=0, keepdims=True),
-        jnp.sum(prod[HEAD_DIM:], axis=0, keepdims=True),
+        jnp.sum(prod[HEAD_DIM * at : HEAD_DIM * (at + 1)], axis=0, keepdims=True)
+        for at in range(len(heads))
     ]
-    lse = [lse_ref[0:1, :], lse_ref[1:2, :]]
+    lse = [lse_ref[at : at + 1, :] for at in range(len(heads))]
     a = a_ref[...]
     b = b_ref[...]
 
     def body(kb, carry):
         base = key_base(kb, bq, t_ref[0])
         here = pl.ds(base, bk)
-        kblk = k_ref[here, :]
-        vblk = v_ref[here, :]
         j = kb * bk + lax.broadcasted_iota(i32, (bk, bq), 0)
         mask = (j >= a) & (j <= b)
-        ps, dss, out = [], [], []
-        for h in (0, 1):
-            p = jnp.exp(jnp.where(mask, mxu(kblk, qz[h]) - lse[h], MASKED))
-            ds = (p * (mxu(vblk, dz[h]) - delta[h])).astype(bf16)
+        ss = [mxu(k_ref[here, lanes(p)], z) for (p, h), z in zip(heads, qz)]
+        dps = [mxu(v_ref[here, lanes(p)], z) for (p, h), z in zip(heads, dz)]
+        ps, dss = [], []
+        for at in range(len(heads)):
+            p = jnp.exp(jnp.where(mask, ss[at] - lse[at], MASKED))
+            dss.append((p * (dps[at] - delta[at])).astype(bf16))
             ps.append(p.astype(bf16))
-            dss.append(ds)
-            out.append(carry[h] + mxu(kt[pl.ds(HEAD_DIM * h, HEAD_DIM), here], ds))
-        dv_acc[here, :] += mxu(jnp.concatenate(ps, axis=1), dcat)
-        dk_acc[here, :] += mxu(jnp.concatenate(dss, axis=1), qcat)
-        return tuple(out)
-
-    init = tuple(jnp.zeros((HEAD_DIM, bq), f32) for _ in (0, 1))
+        for p in pairs:
+            both = slice(2 * p, 2 * p + 2)
+            dv_acc[here, lanes(p)] += mxu(jnp.concatenate(ps[both], axis=1), dcat[p])
+            dk_acc[here, lanes(p)] += mxu(jnp.concatenate(dss[both], axis=1), qcat[p])
+        return tuple(
+            c + mxu(kt[pl.ds(HEAD_DIM * at, HEAD_DIM), here], dss[at])
+            for at, c in enumerate(carry)
+        )
+
+    init = tuple(jnp.zeros((HEAD_DIM, bq), f32) for _ in heads)
     dqt = lax.fori_loop(jnp.min(a) // bk, jnp.max(b) // bk + 1, body, init)
     dq_ref[...] = (jnp.concatenate(dqt, axis=0).T * 0.125).astype(bf16)
 
@@ -506,12 +510,12 @@
         dv_ref[...] = dv_acc[...].astype(bf16)
 
 
-def attention_bwd(pair, q, k, v, dos, os, lse, a, b, t):
-    S = q.shape[0]
+def attention_bwd(q, k, v, dos, os, lse, a, b, t):
+    S, W = q.shape
     bq = S // TP
-    context = pl.BlockSpec((bq, 128), lambda i, *_: (0, pair))
-    whole = pl.BlockSpec((S, 128), lambda i, *_: (0, pair))
-    out = pl.BlockSpec((S, 128), lambda i, *_: (0, 0))
+    block = pl.BlockSpec((bq, W), lambda i, *_: (0, 0))
+    rows = pl.BlockSpec((bq, W), lambda i, *_: (i, 0))
+    whole = pl.BlockSpec((S, W), lambda i, *_: (0, 0))
     row = pl.BlockSpec((1, bq), lambda i, *_: (0, i))
     return pl.pallas_call(
         attend_back_kernel,
@@ -519,19 +523,19 @@
         grid_spec=pltpu.PrefetchScalarGridSpec(
             num_scalar_prefetch=1,
             grid=(TP,),
-            in_specs=[pl.BlockSpec((bq, 128), lambda i, *_: (i, pair)), whole, whole]
-            + [context] * (2 * TP)
+            in_specs=[rows, whole, whole]
+            + [block] * (2 * TP)
             + [pl.BlockSpec((8, bq), lambda i, *_: (0, i)), row, row],
-            out_specs=[pl.BlockSpec((bq, 128), lambda i, *_: (i, 0)), out, out],
+            out_specs=[rows, whole, whole],
             scratch_shapes=[
-                pltpu.VMEM((128, S), bf16),
-                pltpu.VMEM((S, 128), f32),
-                pltpu.VMEM((S, 128), f32),
-                pltpu.VMEM((bq, 128), bf16),
-                pltpu.VMEM((bq, 128), bf16),
+                pltpu.VMEM((W, S), bf16),
+                pltpu.VMEM((S, W), f32),
+                pltpu.VMEM((S, W), f32),
+                pltpu.VMEM((bq, W), bf16),
+                pltpu.VMEM((bq, W), bf16),
             ],
         ),
-        out_shape=[struct((S, 128), bf16)] * 3,
+        out_shape=[struct((S, W), bf16)] * 3,
         compiler_params=pltpu.CompilerParams(vmem_limit_bytes=VMEM),
         cost_estimate=cost("attend_back"),
     )(t, q, k, v, *dos, *os, lse, a, b)
@@ -926,6 +930,8 @@
     x3 = send_tp(after(x2, arrived), 1)
     xs = [x0, x1, x2, x3]
 
+    w_out0 = exchange(after(copies, x1))
+
     here = jnp.concatenate([place, turn])
     length = TP * rows
     first, end = intervals(here, piece_starts, xs, rows)
@@ -950,46 +956,29 @@
         [cot_other],
         [struct((8, rows), i32), slotted],
     )
-    near_own = exchange(cot_sent_own)
     halves_sent = expert.halves(*after((expert_up, expert_down), queries))
-    w_out0 = exchange(after(copies, near_own))
-
-    halves_other = send_tp(after(halves_sent, queries), 1)
+    halves_other = send_tp(halves_sent, 1)
+    near_own = exchange(after(cot_sent_own, w_out0))
     down_bias = lax.dynamic_index_in_dim(expert_down_bias, lo, keepdims=True)
 
     w_out2 = send_tp(w_out0, 2)
     w_out1 = send_tp(w_out0, 1)
-    pairs = head_width // 128
-    contexts, totals = [], []
-    firsts = [(near_own, halves_sent), (cot_other, w_out0)]
-    cot_pieces = []
-    for p in range(pairs):
-        *contexts, total = attention_fwd(
-            p,
-            after(queries, firsts[min(p, 1)], totals),
-            keys,
-            values,
-            first,
-            end,
-            turn,
-            contexts,
-        )
-        if p == 0:
-            near_other = exchange(after(cot_sent_other, w_out0, total))
-            far_own = send_tp(near_own, 2)
-            cot_pieces = [near_own, far_own, near_other, send_tp(near_other, 2)]
-        totals.append(total)
-    w_outs = [w_out0, w_out1, w_out2, send_tp(after(w_out2, total), 1)]
+    *contexts, totals = attention_fwd(
+        after(queries, w_out0, halves_sent), keys, values, first, end, turn
+    )
     ctxs = [contexts[0]] + [send_tp(contexts[r], r) for r in range(1, TP)]
+    w_outs = [w_out0, w_out1, w_out2, send_tp(after(w_out2, ctxs[1]), 1)]
+    near_other = exchange(after(cot_sent_other, near_own, totals))
+    far_own = send_tp(after(near_own, ctxs[3]), 2)
+    cot_pieces = [near_own, far_own, near_other, send_tp(near_other, 2)]
     expert.hold(expert_up, expert_up_bias, None, expert_down, halves_other)
     act_backs, cot_sums = [None] * 4, [None] * 2
-    act_backs[0], act_backs[1], cot_sums[0] = expert.act_back(*cot_pieces[:2])
     mixed, second, upper, lower = plain_call(
         middle_kernel,
         ctxs
         + w_outs
         + [
-            after(residual_in, act_backs[0]),
+            after(residual_in, near_own, halves_other),
             row(output_bias),
             row(second_norm_gain),
             row(second_norm_shift),
@@ -1000,11 +989,12 @@
 
     bias_sent = lax.dynamic_index_in_dim(after(expert_up_bias, second), 1 - lo, keepdims=True)
     expert.hold(expert_up, expert_up_bias, send_tp(bias_sent, 1), expert_down, halves_other)
+    act_backs[0], act_backs[1], cot_sums[0] = expert.act_back(*cot_pieces[:2])
     act_backs[2], act_backs[3], cot_sums[1] = expert.act_back(*cot_pieces[2:])
     cot_sum = added(*cot_sums, dtype=f32)[:1]
     sent_own = plain_call(place_kernel, [second, s_own], [slotted])[0]
     sent_other = plain_call(
-        place_halves_kernel, [send_tp(upper, 1), send_tp(lower, 1), s_other], [slotted]
+        place_halves_kernel, [send_tp(upper, 1), send_tp(lower, 1), after(s_other, act_backs[0])], [slotted]
     )[0]
     rows_own = exchange(after(sent_own, near_other))
     rows_other = exchange(after(sent_other, rows_own, cot_pieces[3]))
@@ -1055,8 +1045,6 @@
         ctxs + [mixed_low],
         [struct((2 * width, head_width), bf16)] * 2,
     )
-    up_bias_back = ordered(lo, up_sum[0], sent[0])
-    down_bias_back = ordered(lo, cot_sum[0], sent[1])
 
     dos = [ctx_backs[0]] + [send_tp(ctx_backs[r], r) for r in range(1, TP)]
     wo_sum, wo_there = plain_call(
@@ -1071,43 +1059,20 @@
         [struct((2 * n * cap, width), bf16)],
     )[0]
     out_home = exchange(out_sent)
-    projected_backs = []
-    firsts = [(wo_sum, out_sent), None]
-    for p in range(pairs):
-        back = attention_bwd(
-            p,
-            after(queries, firsts[min(p, 1)], projected_backs),
-            keys,
-            values,
-            dos,
-            contexts,
-            totals[p],
-            first,
-            end,
-            turn,
-        )
-        projected_backs += back
-        if p == 0:
-            wo = added(wo_sum, after(wo_got, back))
-            firsts[1] = (wo, up_got, down_got)
-
-    def input_back(turns, first):
-        return plain_call(
-            functools.partial(input_back_kernel, 3 * pairs, turns),
-            projected_backs + [after(w_in, first)],
-            [struct((rows, width), bf16)] * 2,
-        )
-
-    part3, part2 = input_back((3, 2), projected_backs[0])
-    got3 = send_tp(part3, 1)
-    keep, away, vector = plain_call(
-        functools.partial(input_weight_kernel, n, shard, 3 * pairs),
-        xs + projected_backs + [after(w_in, part3), sums2],
-        [
+    projected_backs = attention_bwd(
+        after(queries, wo_sum, out_sent), keys, values, dos, contexts, totals, first, end, turn
+    )
+    wo = added(wo_sum, after(wo_got, projected_backs))
+
+    part0, part1, part2, part3, keep, away, vector = plain_call(
+        functools.partial(projection_back_kernel, n, shard),
+        xs + list(projected_backs) + [after(w_in, up_got, down_got, wo), sums2],
+        [struct((rows, width), bf16)] * TP
+        + [
             struct((n // 2 * shard, 3 * head_width), bf16),
             struct((n // 2 * shard + EXTRA, 3 * head_width), bf16),
-        ]
-        + [struct((8, 3 * head_width), f32)],
+            struct((8, 3 * head_width), f32),
+        ],
         scratch=[
             pltpu.VMEM((24, head_width), f32),
             pltpu.VMEM((width, 3 * head_width), f32),
@@ -1115,13 +1080,12 @@
         scalars=[place],
     )
     got = send_fsdp(away, 1)
-    part1, part0 = input_back((1, 0), keep)
-    sum2 = added(part2, after(got3, keep))
+    sum2 = added(part2, send_tp(part3, 1))
     got2 = send_tp(sum2, 2)
     sum0 = added(part0, send_tp(part1, 1))
     out_own, out_away = plain_call(
         functools.partial(collect_both_kernel, cap),
-        [s_own, s_other, after(out_home, part0)],
+        [s_own, s_other, after(out_home, sum2)],
         [struct((rows, width), bf16)] * 2,
     )
     out_other = send_tp(out_away, 1)
@@ -1133,6 +1097,9 @@
         + [struct((shard + EXTRA, 3 * head_width), bf16)] * (n // 2 - 1),
     )
     wi_kept = (kept, folds)
+    sent = after(sent, folds)
+    up_bias_back = ordered(lo, up_sum[0], sent[0])
+    down_bias_back = ordered(lo, cot_sum[0], sent[1])
     wo_home = exchange(after(wo, out_own))
     output_weight_back = plain_call(
         turned_sum_kernel, [wo_home], [struct((head_width, shard), f32)]
@@ -1148,7 +1115,7 @@
 
     back_residual = plain_call(
         last_kernel,
-        [residual_in, row(first_norm_gain), sum0, got2, mixed_back],
+        [residual_in, row(first_norm_gain), sum0, got2, after(mixed_back, folds)],
         [struct((rows, width), f32)],
     )[0]
 
@@ -1157,8 +1124,12 @@
     bias_sum = bias_sum.reshape(2, head_width // HEAD_DIM, n, HEAD_DIM // n)
     input_bias_back = lax.dynamic_index_in_dim(bias_sum, g, axis=2, keepdims=False)
     vector = after(vector, up_back, back_residual)
-    vector = added(after(vector, block_output), send_tp(vector, 1), dtype=f32)
-    vector = added(after(vector, output_weight_back), send_tp(vector, 2), dtype=f32)
+    turned = [send_tp(vector, r) for r in (1, 2, 3)]
+    vector = plain_call(
+        pairs_sum_kernel,
+        [after(vector, block_output, output_weight_back)] + turned,
+        [struct(vector.shape, f32)],
+    )[0]
     tails = vector[5:].reshape(-1)[: 5 * head_width].reshape(5, head_width)
     vectors = jnp.concatenate([vector[:5], tails], axis=1)
     first_gain_back = (vectors[0] - first_norm_shift * vectors[1]) / first_norm_gain

time: 515 us -> 486 us (0.944)
  Pallas kernels: 317 us -> 275 us
  starting transfers between devices: 100 us -> 106 us
  waiting for transfers between devices: 61.7 us -> 67.5 us
    all_to_all x9, waiting for transfers between devices: 23.4 us -> 3.51 us  [exchange(): return lax.all_to_all(x, 'fsdp', split_axis=0, concat_axis=0, tiled=True)]
    ppermute x36 -> x37, waiting for transfers between devices: 12 us -> 31.2 us  [send_tp(): return lax.ppermute(x, 'tp', [(i, i ^ turn) for i in range(TP)])]
    pallas_call x2 -> x1, Pallas kernels: 44.9 us -> 27.9 us  [attention_bwd(): pl.pallas_call(attend_back_kernel, name='attend_back', grid_spec=pltpu.Pr...]
    pallas_call x2 -> x1, Pallas kernels: 35.2 us -> 19.2 us  [attention_fwd(): pl.pallas_call(attend_kernel, name='attend', grid_spec=pltpu.PrefetchScal...]
    all_to_all x9, starting transfers between devices: 54.4 us -> 67.3 us  [exchange(): return lax.all_to_all(x, 'fsdp', split_axis=0, concat_axis=0, tiled=True)]
    pallas_call x30 -> x27, Pallas kernels: 109 us -> 100 us  [plain_call(): pl.pallas_call(kernel, name=kernel_name(kernel), grid=(1,), in_specs=[sme...]
    ppermute x11, waiting for transfers between devices: 26.3 us -> 32.8 us  [send_fsdp(): return lax.ppermute(x, 'fsdp', [(i, i ^ turn) for i in range(n)])]
    ppermute x11, starting transfers between devices: 15.5 us -> 10 us  [send_fsdp(): return lax.ppermute(x, 'fsdp', [(i, i ^ turn) for i in range(n)])]
  transfers between devices with their start and end apart: 56 -> 57, of which waited for: 17 -> 19; matrix products, arithmetic and copies ran while one was open for 2% -> 1% of each run, Pallas kernels for 59% -> 53%
where the time goes in v4:
time: 486 us; the launch traced here: 478 us
  Pallas kernels  275 us (57%)
  starting transfers between devices  106 us (22%)
  waiting for transfers between devices  67.5 us (14%)
  local copies, waits for them, and re-layouts  24.9 us (5%)
    pallas_call x14, Pallas kernels, call(): pl.pallas_call(kernel, name=kernel_name(kernel), grid_spec=pltpu.Prefetch...  126 us
    pallas_call x27, Pallas kernels, plain_call(): pl.pallas_call(kernel, name=kernel_name(kernel), grid=(1,), in_specs=[sme...  100 us
    all_to_all x9, starting transfers between devices, exchange(): return lax.all_to_all(x, 'fsdp', split_axis=0, concat_axis=0, tiled=True)  67.3 us
    ppermute x11, waiting for transfers between devices, send_fsdp(): return lax.ppermute(x, 'fsdp', [(i, i ^ turn) for i in range(n)])  32.8 us
    ppermute x37, waiting for transfers between devices, send_tp(): return lax.ppermute(x, 'tp', [(i, i ^ turn) for i in range(TP)])  31.2 us
    ppermute x37, starting transfers between devices, send_tp(): return lax.ppermute(x, 'tp', [(i, i ^ turn) for i in range(TP)])  28.7 us
    pallas_call x1, Pallas kernels, attention_bwd(): pl.pallas_call(attend_back_kernel, name='attend_back', grid_spec=pltpu.Pr...  27.9 us
    pallas_call x1, Pallas kernels, attention_fwd(): pl.pallas_call(attend_kernel, name='attend', grid_spec=pltpu.PrefetchScal...  19.2 us
  transfers between devices with their start and end apart: 57, of which 19 were waited for; matrix products, arithmetic and copies ran while one was open for 1% of the time, Pallas kernels for 53%

profile of v4, /device:TPU:9, one launch (start us, length us, event | category | flops | bytes accessed | tf_op | source)
XLA Modules:
  0.0 477.9 jit_solution(15444172249912633587)
XLA Ops:
  12.8 11.1 %collective-permute-done.2.refs_10_ = bf16[144,768]{1,0:T(8,128)(2,1)S(1)} collective-permute-done((bf16[144,768]{1,0:T(8,128)(2,1)}, bf16[144,768]{1,0:T(8,128)(2,1)S(1)}, u32[]{:S(2)}, u32[]{:S(2)}) %collective-permute-start.2) | collective-permute-done | bytes 221216 | tf_op jit(solution)/shard_map/ppermute | solution.py:90
  46.4 6.4 %collective-permute-done.9.refs_11_ = bf16[144,768]{1,0:T(8,128)(2,1)} collective-permute-done((bf16[144,768]{1,0:T(8,128)(2,1)}, bf16[144,768]{1,0:T(8,128)(2,1)}, u32[]{:S(2)}, u32[]{:S(2)}) %collective-permute-start.9) | collective-permute-done | bytes 221216 | tf_op jit(solution)/shard_map/ppermute | solution.py:90
  52.8 7.6 %project_kernel.1 = (bf16[2048,256]{1,0:T(8,128)(2,1)}, bf16[2048,256]{1,0:T(8,128)(2,1)}, bf16[2048,256]{1,0:T(8,128)(2,1)}, bf16[1024,768]{1,0:T(8,128)(2,1)}) custom-call(s32[1]{0:T(128)} %bitcast.1.place, bf16[528,1024]{1,0:T(8,128)(2,1)} %get-tuple-element.165.refs_0_, bf16[528,1024]{1,0:T(8,128)(2,1)} %copy-done.3, bf16[528,1024]{1,0:T(8,128)(2,1)} %copy-done.2, ...), custom_call_target="tpu_custom_call" | custom-call | flops 1 | bytes 1 | tf_op jit(solution)/shard_map/project_kernel/pallas_call | solution.py:67
  69.9 5.7 %all-to-all-start.1 = ((bf16[8,64,1024]{2,1,0:T(8,128)(2,1)}), bf16[8,64,1024]{2,1,0:T(8,128)(2,1)S(1)}, u32[]{:S(2)}, u32[]{:S(2)}) async-start(bf16[8,64,1024]{2,1,0:T(8,128)(2,1)} %bitcast.8), calls=%async_computation.1 | async-start | bytes 2097152 | tf_op jit(solution)/shard_map/all_to_all | solution.py:899
  75.6 19.2 %attend.1 = (bf16[512,256]{1,0:T(8,128)(2,1)}, bf16[512,256]{1,0:T(8,128)(2,1)}, bf16[512,256]{1,0:T(8,128)(2,1)}, bf16[512,256]{1,0:T(8,128)(2,1)}, f32[8,2048]{1,0:T(8,128)}) custom-call(s32[1]{0:T(128)} %bitcast.t_ref, bf16[2048,256]{1,0:T(8,128)(2,1)} %get-tuple-element.263.q_ref, bf16[2048,256]{1,0:T(8,128)(2,1)} %get-tuple-element.178.k_ref, ...), custom_call_target="tpu_custom_call" | custom-call | flops 24199999488 | bytes 1 | tf_op jit(solution)/shard_map/attend/pallas_call | solution.py:424
  98.7 9.4 %all-to-all-start.2 = ((bf16[8,64,1024]{2,1,0:T(8,128)(2,1)}), bf16[8,64,1024]{2,1,0:T(8,128)(2,1)}, u32[]{:S(2)}, u32[]{:S(2)}) async-start(bf16[8,64,1024]{2,1,0:T(8,128)(2,1)} %bitcast.57), calls=%async_computation.2 | async-start | bytes 2097152 | tf_op jit(solution)/shard_map/all_to_all | solution.py:899
  113.1 7.5 %collective-permute-done.12.refs_3_ = bf16[512,256]{1,0:T(8,128)(2,1)S(1)} collective-permute-done((bf16[512,256]{1,0:T(8,128)(2,1)S(1)}, bf16[512,256]{1,0:T(8,128)(2,1)S(1)}, u32[]{:S(2)}, u32[]{:S(2)}) %collective-permute-start.12) | collective-permute-done | bytes 262176 | tf_op jit(solution)/shard_map/ppermute | solution.py:85
  126.6 5.6 %middle_kernel.1 = (f32[512,1024]{1,0:T(8,128)}, bf16[512,1024]{1,0:T(8,128)(2,1)}, bf16[256,1024]{1,0:T(8,128)(2,1)}, bf16[256,1024]{1,0:T(8,128)(2,1)}) custom-call(bf16[512,256]{1,0:T(8,128)(2,1)} %get-tuple-element.182.refs_0_.rest_4_, bf16[512,256]{1,0:T(8,128)(2,1)} %copy-done.45, bf16[512,256]{1,0:T(8,128)(2,1)} %copy-done.47, ...), custom_call_target="tpu_custom_call" | custom-call | flops 5500000256 | bytes 1 | tf_op jit(solution)/shard_map/middle_kernel/pallas_call | solution.py:67
  135.2 5.7 %all-to-all-start.3 = ((bf16[8,64,1024]{2,1,0:T(8,128)(2,1)}), bf16[8,64,1024]{2,1,0:T(8,128)(2,1)S(1)}, u32[]{:S(2)}, u32[]{:S(2)}) async-start(bf16[8,64,1024]{2,1,0:T(8,128)(2,1)} %bitcast.58), calls=%async_computation.3 | async-start | bytes 2097152 | tf_op jit(solution)/shard_map/all_to_all | solution.py:899
  147.6 9.3 %act_back_kernel.3 = (bf16[512,2048]{1,0:T(8,128)(2,1)}, bf16[512,2048]{1,0:T(8,128)(2,1)}, f32[8,1024]{1,0:T(8,128)}) custom-call(s32[1]{0:T(128)} %bitcast.7.lo, bf16[512,1024]{1,0:T(8,128)(2,1)} %bitcast.54, bf16[512,1024]{1,0:T(8,128)(2,1)} %collective-permute-done.19.far.refs_5_, bf16[2,1024,1024]{2,1,0:T(8,128)(2,1)} %down_a.7, ...), custom_call_target="tpu_custom_call" | custom-call | flops 9900000256 | bytes 1 | tf_op jit(solution)/shard_map/act_back_kernel/pallas_call | solution.py:722
  163.2 6.8 %collective-permute-done.18.far.refs_7_ = bf16[512,1024]{1,0:T(8,128)(2,1)} collective-permute-done((bf16[512,1024]{1,0:T(8,128)(2,1)}, bf16[512,1024]{1,0:T(8,128)(2,1)}, u32[]{:S(2)}, u32[]{:S(2)}) %collective-permute-start.18) | collective-permute-done | bytes 1048608 | tf_op jit(solution)/shard_map/ppermute | solution.py:85
  175.5 9.4 %act_back_kernel.2 = (bf16[512,2048]{1,0:T(8,128)(2,1)}, bf16[512,2048]{1,0:T(8,128)(2,1)}, f32[8,1024]{1,0:T(8,128)}) custom-call(s32[1]{0:T(128)} %bitcast.7.lo, bf16[512,1024]{1,0:T(8,128)(2,1)} %bitcast.14.near.refs_6_, bf16[512,1024]{1,0:T(8,128)(2,1)} %collective-permute-done.18.far.refs_7_, bf16[2,1024,1024]{2,1,0:T(8,128)(2,1)} %down_a.7, ...), custom_call_target="tpu_custom_call" | custom-call | flops 9900000256 | bytes 1 | tf_op jit(solution)/shard_map/act_back_kernel/pallas_call | solution.py:722
  185.5 10.3 %expert_kernel.4 = (bf16[512,2048]{1,0:T(8,128)(2,1)}, bf16[512,2048]{1,0:T(8,128)(2,1)}, bf16[512,1024]{1,0:T(8,128)(2,1)}) custom-call(s32[1]{0:T(128)} %bitcast.7.lo, bf16[512,1024]{1,0:T(8,128)(2,1)} %bitcast.39, bf16[512,2048]{1,0:T(8,128)(2,1)} %get-tuple-element.201.act_back, bf16[2,1024,1024]{2,1,0:T(8,128)(2,1)} %up_a.7, ...), custom_call_target="tpu_custom_call" | custom-call | flops 11000000512 | bytes 1 | tf_op jit(solution)/shard_map/expert_kernel/pallas_call | solution.py:722
  197.8 10.4 %expert_kernel.5 = (bf16[512,2048]{1,0:T(8,128)(2,1)}, bf16[512,2048]{1,0:T(8,128)(2,1)}, bf16[512,1024]{1,0:T(8,128)(2,1)}) custom-call(s32[1]{0:T(128)} %bitcast.7.lo, bf16[512,1024]{1,0:T(8,128)(2,1)} %copy-done.12, bf16[512,2048]{1,0:T(8,128)(2,1)} %get-tuple-element.210.act_back, bf16[2,1024,1024]{2,1,0:T(8,128)(2,1)} %up_a.7, ...), custom_call_target="tpu_custom_call" | custom-call | flops 11000000512 | bytes 1 | tf_op jit(solution)/shard_map/expert_kernel/pallas_call | solution.py:722
  209.5 10.3 %expert_kernel.6 = (bf16[512,2048]{1,0:T(8,128)(2,1)}, bf16[512,2048]{1,0:T(8,128)(2,1)}, bf16[512,1024]{1,0:T(8,128)(2,1)}) custom-call(s32[1]{0:T(128)} %bitcast.7.lo, bf16[512,1024]{1,0:T(8,128)(2,1)} %bitcast.43, bf16[512,2048]{1,0:T(8,128)(2,1)} %get-tuple-element.213.act_back, bf16[2,1024,1024]{2,1,0:T(8,128)(2,1)} %up_a.7, ...), custom_call_target="tpu_custom_call" | custom-call | flops 11000000512 | bytes 1 | tf_op jit(solution)/shard_map/expert_kernel/pallas_call | solution.py:722
  220.7 10.7 %expert_kernel.7 = (bf16[512,2048]{1,0:T(8,128)(2,1)}, bf16[512,2048]{1,0:T(8,128)(2,1)}, bf16[512,1024]{1,0:T(8,128)(2,1)}) custom-call(s32[1]{0:T(128)} %bitcast.7.lo, bf16[512,1024]{1,0:T(8,128)(2,1)} %copy-done.13, bf16[512,2048]{1,0:T(8,128)(2,1)} %get-tuple-element.198.act_back, bf16[2,1024,1024]{2,1,0:T(8,128)(2,1)} %up_a.7, ...), custom_call_target="tpu_custom_call" | custom-call | flops 11000000512 | bytes 1 | tf_op jit(solution)/shard_map/expert_kernel/pallas_call | solution.py:722
  231.8 9.1 %down_outer_kernel.2.down = f32[2,1024,1024]{2,1,0:T(8,128)} custom-call(s32[1]{0:T(128)} %bitcast.7.lo, bf16[512,2048]{1,0:T(8,128)(2,1)} %get-tuple-element.242.refs_0_.act_0, bf16[512,2048]{1,0:T(8,128)(2,1)} %get-tuple-element.239.refs_1_.act_0, bf16[512,2048]{1,0:T(8,128)(2,1)} %get-tuple-element.243.refs_2_.act_1, ...), custom_call_target="tpu_custom_call" | custom-call | flops 9900000256 | bytes 1 | tf_op jit(solution)/shard_map/down_outer_kernel/pallas_call | solution.py:722
  245.9 9.5 %all-to-all-start.5 = ((bf16[8,64,1024]{2,1,0:T(8,128)(2,1)}), bf16[8,64,1024]{2,1,0:T(8,128)(2,1)S(1)}, u32[]{:S(2)}, u32[]{:S(2)}) async-start(bf16[8,64,1024]{2,1,0:T(8,128)(2,1)} %bitcast.47), calls=%async_computation.5 | async-start | bytes 2097152 | tf_op jit(solution)/shard_map/all_to_all | solution.py:899
  255.5 8.9 %expert_out_kernel.2 = bf16[1024,1024]{1,0:T(8,128)(2,1)} custom-call(s32[1]{0:T(128)} %bitcast.7.lo, bf16[512,2048]{1,0:T(8,128)(2,1)} %get-tuple-element.239.refs_1_.act_0, bf16[512,2048]{1,0:T(8,128)(2,1)} %get-tuple-element.241.refs_3_.act_1, bf16[2,1024,1024]{2,1,0:T(8,128)(2,1)} %down_a.7, bf16[2,1024,1024]{2,1,0:T(8,128)(2,1)} %collective-permute-done.16.down_b.up_b), custom_call_target="tpu_custom_call" | custom-call | flops 9900000256 | bytes 1 | tf_op jit(solution)/shard_map/expert_out_kernel/pallas_call | solution.py:722
  264.9 9.4 %up_outer_kernel.2 = (bf16[1024,1024]{1,0:T(8,128)(2,1)}, f32[8,1024]{1,0:T(8,128)}) custom-call(s32[1]{0:T(128)} %bitcast.7.lo, bf16[512,1024]{1,0:T(8,128)(2,1)} %bitcast.40, bf16[512,1024]{1,0:T(8,128)(2,1)} %copy-done.12, bf16[512,1024]{1,0:T(8,128)(2,1)} %bitcast.44, bf16[512,1024]{1,0:T(8,128)(2,1)} %copy-done.13, ...), custom_call_target="tpu_custom_call" | custom-call | flops 9900000256 | bytes 1 | tf_op jit(solution)/shard_map/up_outer_kernel/pallas_call | solution.py:722
  277.2 9.7 %all-to-all-start.6 = ((bf16[8,64,1024]{2,1,0:T(8,128)(2,1)}), bf16[8,64,1024]{2,1,0:T(8,128)(2,1)S(1)}, u32[]{:S(2)}, u32[]{:S(2)}) async-start(bf16[8,64,1024]{2,1,0:T(8,128)(2,1)} %bitcast.46), calls=%async_computation.6 | async-start | bytes 2097152 | tf_op jit(solution)/shard_map/all_to_all | solution.py:899
  291.9 8.7 %down_outer_kernel.3 = bf16[1024,1024]{1,0:T(8,128)(2,1)} custom-call(s32[1]{0:T(128)} %bitcast.7.lo, bf16[512,2048]{1,0:T(8,128)(2,1)} %get-tuple-element.242.refs_0_.act_0, bf16[512,2048]{1,0:T(8,128)(2,1)} %get-tuple-element.239.refs_1_.act_0, bf16[512,2048]{1,0:T(8,128)(2,1)} %get-tuple-element.243.refs_2_.act_1, ...), custom_call_target="tpu_custom_call" | custom-call | flops 9900000256 | bytes 1 | tf_op jit(solution)/shard_map/down_outer_kernel/pallas_call | solution.py:722
  300.7 8.9 %expert_out_kernel.3.near = bf16[1024,1024]{1,0:T(8,128)(2,1)} custom-call(s32[1]{0:T(128)} %bitcast.7.lo, bf16[512,2048]{1,0:T(8,128)(2,1)} %get-tuple-element.242.refs_0_.act_0, bf16[512,2048]{1,0:T(8,128)(2,1)} %get-tuple-element.243.refs_2_.act_1, bf16[2,1024,1024]{2,1,0:T(8,128)(2,1)} %down_a.7, bf16[2,1024,1024]{2,1,0:T(8,128)(2,1)} %collective-permute-done.16.down_b.up_b), custom_call_target="tpu_custom_call" | custom-call | flops 2969999872 | bytes 1 | tf_op jit(solution)/shard_map/expert_out_kernel/pallas_call | solution.py:722
  309.6 9.5 %up_outer_kernel.3 = (f32[2,1024,1024]{2,1,0:T(8,128)}, f32[8,1024]{1,0:T(8,128)}) custom-call(s32[1]{0:T(128)} %bitcast.7.lo, bf16[512,1024]{1,0:T(8,128)(2,1)} %bitcast.41, bf16[512,1024]{1,0:T(8,128)(2,1)} %copy-done.12, bf16[512,1024]{1,0:T(8,128)(2,1)} %bitcast.45, bf16[512,1024]{1,0:T(8,128)(2,1)} %copy-done.13, ...), custom_call_target="tpu_custom_call" | custom-call | flops 2969999872 | bytes 1 | tf_op jit(solution)/shard_map/up_outer_kernel/pallas_call | solution.py:722
  327.8 6.9 %turn_kernel.1 = (f32[512,1024]{1,0:T(8,128)}, bf16[512,1024]{1,0:T(8,128)(2,1)}, f32[8,1024]{1,0:T(8,128)}, bf16[512,256]{1,0:T(8,128)(2,1)}, bf16[512,256]{1,0...) custom-call(bf16[1024,256]{1,0:T(8,128)(2,1)} %bitcast.6.refs_4_.refs_0_, ...), custom_call_target="tpu_custom_call" | custom-call | flops 1 | bytes 1 | tf_op jit(solution)/shard_map/turn_kernel/pallas_call | solution.py:67
  346.4 5.7 %all-to-all-start.7 = ((bf16[8,128,1024]{2,1,0:T(8,128)(2,1)}), bf16[8,128,1024]{2,1,0:T(8,128)(2,1)S(1)}, u32[]{:S(2)}, u32[]{:S(2)}) async-start(bf16[8,128,1024]{2,1,0:T(8,128)(2,1)} %bitcast.52), calls=%async_computation.7 | async-start | bytes 4194304 | tf_op jit(solution)/shard_map/all_to_all | solution.py:899
  357.0 27.9 %attend_back.1 = (bf16[2048,256]{1,0:T(8,128)(2,1)}, bf16[2048,256]{1,0:T(8,128)(2,1)}, bf16[2048,256]{1,0:T(8,128)(2,1)}) custom-call(s32[1]{0:T(128)} %bitcast.t_ref, bf16[2048,256]{1,0:T(8,128)(2,1)} %get-tuple-element.263.q_ref, bf16[2048,256]{1,0:T(8,128)(2,1)} %get-tuple-element.178.k_ref, bf16[2048,256]{1,0:T(8,128)(2,1)} %get-tuple-element.179.v_ref, ...), custom_call_target="tpu_custom_call" | custom-call | flops 32999999488 | bytes 1 | tf_op jit(solution)/shard_map/attend_back/pallas_call | solution.py:520
  387.8 12.6 %projection_back_kernel.1 = (bf16[512,1024]{1,0:T(8,128)(2,1)}, bf16[512,1024]{1,0:T(8,128)(2,1)}, bf16[512,1024]{1,0:T(8,128)(2,1)}, bf16[512,1024]{1,0:T(8,128...) custom-call(s32[1]{0:T(128)} %bitcast.1.place, ...), custom_call_target="tpu_custom_call" | custom-call | flops 14300000256 | bytes 1 | tf_op jit(solution)/shard_map/projection_back_kernel/pallas_call | solution.py:67
  414.3 11.5 %all-to-all-start.8 = ((bf16[8,128,256]{2,1,0:T(8,128)(2,1)}), bf16[8,128,256]{2,1,0:T(8,128)(2,1)S(1)}, u32[]{:S(2)}, u32[]{:S(2)}) async-start(bf16[8,128,256]{2,1,0:T(8,128)(2,1)} %bitcast.25), calls=%async_computation.8 | async-start | bytes 1048576 | tf_op jit(solution)/shard_map/all_to_all | solution.py:899
  434.5 5.8 %fill_kernel.1 = (f32[2,1024,1024]{2,1,0:T(8,128)}, f32[2,1024,1024]{2,1,0:T(8,128)}) custom-call(s32[1]{0:T(128)} %bitcast.7.lo, f32[2,1024,1024]{2,1,0:T(8,128)} %get-tuple-element.287.up, f32[2,1024,1024]{2,1,0:T(8,128)} %down_outer_kernel.2.down, ...), custom_call_target="tpu_custom_call", output_to_operand_aliasing={{0}: (1, {}), {1}: (2, {})} | custom-call | flops 1 | bytes 1 | tf_op jit(solution)/shard_map/fill_kernel/pallas_call | solution.py:722
  441.9 5.4 %last_kernel.1 = f32[512,1024]{1,0:T(8,128)} custom-call(bf16[512,1024]{1,0:T(8,128)(2,1)} %residual.1, f32[1,1024]{1,0:T(1,128)} %bitcast.63, bf16[512,1024]{1,0:T(8,128)(2,1)} %sum_kernel.13.own, bf16[512,1024]{1,0:T(8,128)(2,1)} %copy-done.14, f32[512,1024]{1,0:T(8,128)} %get-tuple-element.294.mixed_back), custom_call_target="tpu_custom_call" | custom-call | flops 1 | bytes 1 | tf_op jit(solution)/shard_map/last_kernel/pallas_call | solution.py:67
  451.8 6.2 %collective-permute-done.44.refs_2_ = bf16[144,768]{1,0:T(8,128)(2,1)S(1)} collective-permute-done((bf16[144,768]{1,0:T(8,128)(2,1)}, bf16[144,768]{1,0:T(8,128)(2,1)S(1)}, u32[]{:S(2)}, u32[]{:S(2)}) %collective-permute-start.44) | collective-permute-done | bytes 221216 | tf_op jit(solution)/shard_map/ppermute | solution.py:90
  (249 shorter events, 175.1 us)
Async XLA Ops:
  5.4 24.9 %collective-permute-start.5 = (bf16[528,1024]{1,0:T(8,128)(2,1)}, bf16[528,1024]{1,0:T(8,128)(2,1)S(1)}, u32[]{:S(2)}, u32[]{:S(2)}) collective-permute-start(bf16[528,1024]{1,0:T(8,128)(2,1)} %get-tuple-element.165.refs_0_), channel_id=1, source_target_pairs={{0,2},{1,3},{2,0},{3,1},{4,6},{5,7},{6,4},{7,5},{8,10},{9,11},{10,... | collective-permute-start | bytes 3244040 | tf_op jit(solution)/shard_map/ppermute | solution.py:85
  33.9 18.8 %collective-permute-start.9 = (bf16[144,768]{1,0:T(8,128)(2,1)}, bf16[144,768]{1,0:T(8,128)(2,1)}, u32[]{:S(2)}, u32[]{:S(2)}) collective-permute-start(bf16[144,768]{1,0:T(8,128)(2,1)} %copy-done.31), channel_id=1, source_target_pairs={{0,4},{4,0},{8,12},{12,8},{16,20},{20,16},{24,28},{28,24},{1,5},{5... | collective-permute-start | bytes 663560 | tf_op jit(solution)/shard_map/ppermute | solution.py:90
  35.2 33.5 %all-to-all-start = ((bf16[8,128,256]{2,1,0:T(8,128)(2,1)}), bf16[8,128,256]{2,1,0:T(8,128)(2,1)}, u32[]{:S(2)}, u32[]{:S(2)}) async-start(bf16[8,128,256]{2,1,0:T(8,128)(2,1)} %bitcast.59), calls=%async_computation | async-start | bytes 1048576 | tf_op jit(solution)/shard_map/all_to_all | solution.py:899
  65.0 55.8 %collective-permute-start.16 = (bf16[2,1024,1024]{2,1,0:T(8,128)(2,1)}, bf16[2,1024,1024]{2,1,0:T(8,128)(2,1)}, u32[]{:S(2)}, u32[]{:S(2)}) collective-permute-start(bf16[2,1024,1024]{2,1,0:T(8,128)(2,1)} %halves_kernel.1), channel_id=1, source_target_pairs={{0,1},{1,0},{2,3},{3,2},{4,5},{5,4},{6,7},{7,6},{8,9},{9,8},{10,11... | collective-permute-start | bytes 12582920 | tf_op jit(solution)/shard_map/ppermute | solution.py:85
  67.1 27.7 %collective-permute-start.17 = (bf16[528,1024]{1,0:T(8,128)(2,1)}, bf16[528,1024]{1,0:T(8,128)(2,1)S(1)}, u32[]{:S(2)}, u32[]{:S(2)}) collective-permute-start(bf16[528,1024]{1,0:T(8,128)(2,1)} %get-tuple-element.191), channel_id=1, source_target_pairs={{0,1},{1,0},{2,3},{3,2},{4,5},{5,4},{6,7},{7,6},{8,9},{9,8},{10,11... | collective-permute-start | bytes 3244040 | tf_op jit(solution)/shard_map/ppermute | solution.py:85
  68.7 42.6 %collective-permute-start.14 = (bf16[1024,256]{1,0:T(8,128)(2,1)}, bf16[1024,256]{1,0:T(8,128)(2,1)S(1)}, u32[]{:S(2)}, u32[]{:S(2)}) collective-permute-start(bf16[1024,256]{1,0:T(8,128)(2,1)} %bitcast.6.refs_4_.refs_0_), channel_id=1, source_target_pairs={{0,2},{1,3},{2,0},{3,1},{4,6},{5,7},{6,4},{7,5},{8,10},{9,11},{10,... | collective-permute-start | bytes 1572872 | tf_op jit(solution)/shard_map/ppermute | solution.py:85
  69.9 28.8 %all-to-all-start.1 = ((bf16[8,64,1024]{2,1,0:T(8,128)(2,1)}), bf16[8,64,1024]{2,1,0:T(8,128)(2,1)S(1)}, u32[]{:S(2)}, u32[]{:S(2)}) async-start(bf16[8,64,1024]{2,1,0:T(8,128)(2,1)} %bitcast.8), calls=%async_computation.1 | async-start | bytes 2097152 | tf_op jit(solution)/shard_map/all_to_all | solution.py:899
  98.7 36.5 %all-to-all-start.2 = ((bf16[8,64,1024]{2,1,0:T(8,128)(2,1)}), bf16[8,64,1024]{2,1,0:T(8,128)(2,1)}, u32[]{:S(2)}, u32[]{:S(2)}) async-start(bf16[8,64,1024]{2,1,0:T(8,128)(2,1)} %bitcast.57), calls=%async_computation.2 | async-start | bytes 2097152 | tf_op jit(solution)/shard_map/all_to_all | solution.py:899
  120.6 27.0 %collective-permute-start.19 = (bf16[512,1024]{1,0:T(8,128)(2,1)S(1)}, bf16[512,1024]{1,0:T(8,128)(2,1)}, u32[]{:S(2)}, u32[]{:S(2)}) collective-permute-start(bf16[512,1024]{1,0:T(8,128)(2,1)S(1)} %bitcast.53), channel_id=1, source_target_pairs={{0,2},{1,3},{2,0},{3,1},{4,6},{5,7},{6,4},{7,5},{8,10},{9,11},{10,... | collective-permute-start | bytes 3145736 | tf_op jit(solution)/shard_map/ppermute | solution.py:85
  135.2 27.8 %all-to-all-start.3 = ((bf16[8,64,1024]{2,1,0:T(8,128)(2,1)}), bf16[8,64,1024]{2,1,0:T(8,128)(2,1)S(1)}, u32[]{:S(2)}, u32[]{:S(2)}) async-start(bf16[8,64,1024]{2,1,0:T(8,128)(2,1)} %bitcast.58), calls=%async_computation.3 | async-start | bytes 2097152 | tf_op jit(solution)/shard_map/all_to_all | solution.py:899
  140.9 29.1 %collective-permute-start.18 = (bf16[512,1024]{1,0:T(8,128)(2,1)}, bf16[512,1024]{1,0:T(8,128)(2,1)}, u32[]{:S(2)}, u32[]{:S(2)}) collective-permute-start(bf16[512,1024]{1,0:T(8,128)(2,1)} %bitcast.14.near.refs_6_), channel_id=1, source_target_pairs={{0,2},{1,3},{2,0},{3,1},{4,6},{5,7},{6,4},{7,5},{8,10},{9,11},{10,... | collective-permute-start | bytes 3145736 | tf_op jit(solution)/shard_map/ppermute | solution.py:85
  141.8 43.1 %collective-permute-start.20 = (f32[1,1024]{1,0:T(1,128)S(1)}, f32[1,1024]{1,0:T(1,128)S(1)}, u32[]{:S(2)}, u32[]{:S(2)}) collective-permute-start(f32[1,1024]{1,0:T(1,128)S(1)} %constant_dynamic-slice_fusion.2), channel_id=1, source_target_pairs={{0,1},{1,0},{2,3},{3,2},{4,5},{5,4},{6,7},{7,6},{8,9},{9,8},{10,11... | collective-permute-start | bytes 12296 | tf_op jit(solution)/shard_map/ppermute | solution.py:85
  163.0 32.8 %collective-permute-start.23 = (bf16[512,1024]{1,0:T(8,128)(2,1)S(1)}, bf16[512,1024]{1,0:T(8,128)(2,1)S(1)}, u32[]{:S(2)}, u32[]{:S(2)}) collective-permute-start(bf16[512,1024]{1,0:T(8,128)(2,1)S(1)} %bitcast.38), channel_id=1, source_target_pairs={{0,2},{1,3},{2,0},{3,1},{4,6},{5,7},{6,4},{7,5},{8,10},{9,11},{10,... | collective-permute-start | bytes 3145736 | tf_op jit(solution)/shard_map/ppermute | solution.py:85
  170.0 27.6 %all-to-all-start.4 = ((bf16[8,64,1024]{2,1,0:T(8,128)(2,1)}), bf16[8,64,1024]{2,1,0:T(8,128)(2,1)S(1)}, u32[]{:S(2)}, u32[]{:S(2)}) async-start(bf16[8,64,1024]{2,1,0:T(8,128)(2,1)} %bitcast.50), calls=%async_computation.4 | async-start | bytes 2097152 | tf_op jit(solution)/shard_map/all_to_all | solution.py:899
  197.6 22.1 %collective-permute-start.24 = (bf16[512,1024]{1,0:T(8,128)(2,1)S(1)}, bf16[512,1024]{1,0:T(8,128)(2,1)S(1)}, u32[]{:S(2)}, u32[]{:S(2)}) collective-permute-start(bf16[512,1024]{1,0:T(8,128)(2,1)S(1)} %bitcast.42), channel_id=1, source_target_pairs={{0,2},{1,3},{2,0},{3,1},{4,6},{5,7},{6,4},{7,5},{8,10},{9,11},{10,... | collective-permute-start | bytes 3145736 | tf_op jit(solution)/shard_map/ppermute | solution.py:85
  208.3 33.9 %collective-permute-start.26 = (bf16[512,1024]{1,0:T(8,128)(2,1)}, bf16[512,1024]{1,0:T(8,128)(2,1)S(1)}, u32[]{:S(2)}, u32[]{:S(2)}) collective-permute-start(bf16[512,1024]{1,0:T(8,128)(2,1)} %get-tuple-element.211), channel_id=1, source_target_pairs={{0,2},{1,3},{2,0},{3,1},{4,6},{5,7},{6,4},{7,5},{8,10},{9,11},{10,... | collective-permute-start | bytes 3145736 | tf_op jit(solution)/shard_map/ppermute | solution.py:85
  231.5 33.2 %collective-permute-start.25 = (bf16[512,1024]{1,0:T(8,128)(2,1)}, bf16[512,1024]{1,0:T(8,128)(2,1)S(1)}, u32[]{:S(2)}, u32[]{:S(2)}) collective-permute-start(bf16[512,1024]{1,0:T(8,128)(2,1)} %get-tuple-element.220), channel_id=1, source_target_pairs={{0,2},{1,3},{2,0},{3,1},{4,6},{5,7},{6,4},{7,5},{8,10},{9,11},{10,... | collective-permute-start | bytes 3145736 | tf_op jit(solution)/shard_map/ppermute | solution.py:85
  245.9 31.3 %all-to-all-start.5 = ((bf16[8,64,1024]{2,1,0:T(8,128)(2,1)}), bf16[8,64,1024]{2,1,0:T(8,128)(2,1)S(1)}, u32[]{:S(2)}, u32[]{:S(2)}) async-start(bf16[8,64,1024]{2,1,0:T(8,128)(2,1)} %bitcast.47), calls=%async_computation.5 | async-start | bytes 2097152 | tf_op jit(solution)/shard_map/all_to_all | solution.py:899
  264.7 54.5 %collective-permute-start.27 = (bf16[1024,1024]{1,0:T(8,128)(2,1)}, bf16[1024,1024]{1,0:T(8,128)(2,1)}, u32[]{:S(2)}, u32[]{:S(2)}) collective-permute-start(bf16[1024,1024]{1,0:T(8,128)(2,1)} %expert_out_kernel.2), channel_id=1, source_target_pairs={{0,2},{1,3},{2,0},{3,1},{4,6},{5,7},{6,4},{7,5},{8,10},{9,11},{10,... | collective-permute-start | bytes 6291464 | tf_op jit(solution)/shard_map/ppermute | solution.py:85
  277.2 42.0 %all-to-all-start.6 = ((bf16[8,64,1024]{2,1,0:T(8,128)(2,1)}), bf16[8,64,1024]{2,1,0:T(8,128)(2,1)S(1)}, u32[]{:S(2)}, u32[]{:S(2)}) async-start(bf16[8,64,1024]{2,1,0:T(8,128)(2,1)} %bitcast.46), calls=%async_computation.6 | async-start | bytes 2097152 | tf_op jit(solution)/shard_map/all_to_all | solution.py:899
  289.8 29.4 %collective-permute-start.28 = (f32[2,1024]{1,0:T(2,128)S(1)}, f32[2,1024]{1,0:T(2,128)S(1)}, u32[]{:S(2)}, u32[]{:S(2)}) collective-permute-start(f32[2,1024]{1,0:T(2,128)S(1)} %pad_maximum_fusion.1), channel_id=1, source_target_pairs={{0,1},{1,0},{2,3},{3,2},{4,5},{5,4},{6,7},{7,6},{8,9},{9,8},{10,11... | collective-permute-start | bytes 24584 | tf_op jit(solution)/shard_map/ppermute | solution.py:85
  339.7 48.1 %collective-permute-start.34 = (bf16[1024,1024]{1,0:T(8,128)(2,1)}, bf16[1024,1024]{1,0:T(8,128)(2,1)}, u32[]{:S(2)}, u32[]{:S(2)}) collective-permute-start(bf16[1024,1024]{1,0:T(8,128)(2,1)} %get-tuple-element.236), channel_id=1, source_target_pairs={{0,1},{1,0},{2,3},{3,2},{4,5},{5,4},{6,7},{7,6},{8,9},{9,8},{10,11... | collective-permute-start | bytes 6291464 | tf_op jit(solution)/shard_map/ppermute | solution.py:85
  346.4 62.1 %all-to-all-start.7 = ((bf16[8,128,1024]{2,1,0:T(8,128)(2,1)}), bf16[8,128,1024]{2,1,0:T(8,128)(2,1)S(1)}, u32[]{:S(2)}, u32[]{:S(2)}) async-start(bf16[8,128,1024]{2,1,0:T(8,128)(2,1)} %bitcast.52), calls=%async_computation.7 | async-start | bytes 4194304 | tf_op jit(solution)/shard_map/all_to_all | solution.py:899
  352.1 35.7 %collective-permute-start.35 = (bf16[1024,1024]{1,0:T(8,128)(2,1)}, bf16[1024,1024]{1,0:T(8,128)(2,1)}, u32[]{:S(2)}, u32[]{:S(2)}) collective-permute-start(bf16[1024,1024]{1,0:T(8,128)(2,1)} %down_outer_kernel.3), channel_id=1, source_target_pairs={{0,1},{1,0},{2,3},{3,2},{4,5},{5,4},{6,7},{7,6},{8,9},{9,8},{10,11... | collective-permute-start | bytes 6291464 | tf_op jit(solution)/shard_map/ppermute | solution.py:85
  355.7 29.1 %collective-permute-start.36 = (bf16[1024,256]{1,0:T(8,128)(2,1)}, bf16[1024,256]{1,0:T(8,128)(2,1)S(1)}, u32[]{:S(2)}, u32[]{:S(2)}) collective-permute-start(bf16[1024,256]{1,0:T(8,128)(2,1)} %get-tuple-element.271), channel_id=1, source_target_pairs={{0,2},{1,3},{2,0},{3,1},{4,6},{5,7},{6,4},{7,5},{8,10},{9,11},{10,... | collective-permute-start | bytes 1572872 | tf_op jit(solution)/shard_map/ppermute | solution.py:85
  401.1 25.5 %collective-permute-start.40 = (bf16[512,1024]{1,0:T(8,128)(2,1)}, bf16[512,1024]{1,0:T(8,128)(2,1)}, u32[]{:S(2)}, u32[]{:S(2)}) collective-permute-start(bf16[512,1024]{1,0:T(8,128)(2,1)} %get-tuple-element.292), channel_id=1, source_target_pairs={{0,1},{1,0},{2,3},{3,2},{4,5},{5,4},{6,7},{7,6},{8,9},{9,8},{10,11... | collective-permute-start | bytes 3145736 | tf_op jit(solution)/shard_map/ppermute | solution.py:85
  401.2 28.2 %collective-permute-start.38 = (bf16[528,768]{1,0:T(8,128)(2,1)}, bf16[528,768]{1,0:T(8,128)(2,1)}, u32[]{:S(2)}, u32[]{:S(2)}) collective-permute-start(bf16[528,768]{1,0:T(8,128)(2,1)} %get-tuple-element.281), channel_id=1, source_target_pairs={{0,4},{4,0},{8,12},{12,8},{16,20},{20,16},{24,28},{28,24},{1,5},{5... | collective-permute-start | bytes 2433032 | tf_op jit(solution)/shard_map/ppermute | solution.py:90
  408.2 32.7 %collective-permute-start.41 = (bf16[512,1024]{1,0:T(8,128)(2,1)}, bf16[512,1024]{1,0:T(8,128)(2,1)S(1)}, u32[]{:S(2)}, u32[]{:S(2)}) collective-permute-start(bf16[512,1024]{1,0:T(8,128)(2,1)} %sum_kernel.11), channel_id=1, source_target_pairs={{0,2},{1,3},{2,0},{3,1},{4,6},{5,7},{6,4},{7,5},{8,10},{9,11},{10,... | collective-permute-start | bytes 3145736 | tf_op jit(solution)/shard_map/ppermute | solution.py:85
  413.7 53.8 %collective-permute-start.39 = (bf16[512,1024]{1,0:T(8,128)(2,1)}, bf16[512,1024]{1,0:T(8,128)(2,1)S(1)}, u32[]{:S(2)}, u32[]{:S(2)}) collective-permute-start(bf16[512,1024]{1,0:T(8,128)(2,1)} %get-tuple-element.290), channel_id=1, source_target_pairs={{0,1},{1,0},{2,3},{3,2},{4,5},{5,4},{6,7},{7,6},{8,9},{9,8},{10,11... | collective-permute-start | bytes 3145736 | tf_op jit(solution)/shard_map/ppermute | solution.py:85
  414.3 50.5 %all-to-all-start.8 = ((bf16[8,128,256]{2,1,0:T(8,128)(2,1)}), bf16[8,128,256]{2,1,0:T(8,128)(2,1)S(1)}, u32[]{:S(2)}, u32[]{:S(2)}) async-start(bf16[8,128,256]{2,1,0:T(8,128)(2,1)} %bitcast.25), calls=%async_computation.8 | async-start | bytes 1048576 | tf_op jit(solution)/shard_map/all_to_all | solution.py:899
  431.8 19.9 %collective-permute-start.43 = (bf16[144,768]{1,0:T(8,128)(2,1)}, bf16[144,768]{1,0:T(8,128)(2,1)S(1)}, u32[]{:S(2)}, u32[]{:S(2)}) collective-permute-start(bf16[144,768]{1,0:T(8,128)(2,1)} %get-tuple-element.285), channel_id=1, source_target_pairs={{0,16},{4,20},{8,24},{12,28},{16,0},{20,4},{24,8},{28,12},{1,17},{... | collective-permute-start | bytes 663560 | tf_op jit(solution)/shard_map/ppermute | solution.py:90
  434.2 23.8 %collective-permute-start.44 = (bf16[144,768]{1,0:T(8,128)(2,1)}, bf16[144,768]{1,0:T(8,128)(2,1)S(1)}, u32[]{:S(2)}, u32[]{:S(2)}) collective-permute-start(bf16[144,768]{1,0:T(8,128)(2,1)} %get-tuple-element.286), channel_id=1, source_target_pairs={{0,24},{4,28},{8,16},{12,20},{16,8},{20,12},{24,0},{28,4},{1,25},{... | collective-permute-start | bytes 663560 | tf_op jit(solution)/shard_map/ppermute | solution.py:90
  (75 other events, 999.0 us)

commit v5 on v4

--- a/solution.py
+++ b/solution.py
@@ -32,8 +32,9 @@
 
 TIMES = {
     "attend": 22,
-    "middle_kernel": 5,
-    "place_kernel": 3,
+    "middle_kernel": 8,
+    "project_kernel": 7,
+    "halves_kernel": 5,
     "attend_back": 30,
     "act_back_kernel": 9,
     "expert_kernel": 10,
@@ -75,6 +76,24 @@
         compiler_params=pltpu.CompilerParams(vmem_limit_bytes=VMEM),
         cost_estimate=cost(kernel_name(kernel)),
     )(*scalars, *ins)
+
+
+def row_call(kernel, ins, outs, rows, tile=128):
+    spec = lambda x: (
+        pl.BlockSpec((tile,) + x.shape[1:], lambda i: (i, 0))
+        if x.shape[0] == rows
+        else whole_spec(x)
+    )
+    return pl.pallas_call(
+        kernel,
+        name=kernel_name(kernel),
+        grid=(rows // tile,),
+        in_specs=[spec(x) for x in ins],
+        out_specs=[spec(x) for x in outs],
+        out_shape=list(outs),
+        compiler_params=pltpu.CompilerParams(vmem_limit_bytes=VMEM),
+        cost_estimate=cost(kernel_name(kernel)),
+    )(*ins)
 
 
 def struct(shape, dtype):
@@ -260,7 +279,12 @@
     total = cot[...].astype(f32) + norm_back(second_back, unit, inverse, gain[...])
     back[...] = total
     low[...] = total.astype(bf16)
-    sums[...] = jnp.concatenate(
+
+    @pl.when(pl.program_id(0) == 0)
+    def _():
+        sums[...] = jnp.zeros_like(sums)
+
+    sums[...] += jnp.concatenate(
         [
             jnp.sum(second_back * unit, axis=0, keepdims=True),
             jnp.sum(second_back, axis=0, keepdims=True),
@@ -635,10 +659,10 @@
 
 def expert_kernel(lo, x, act_back, up_a, up_b, bias_a, bias_b, act, pre_back, x_back):
     width = up_a.shape[1]
+    pres = [mxu(x[...], up[...]) + bias[...] for up, bias in ((up_a, bias_a), (up_b, bias_b))]
     total = None
-    for j, (up, bias) in enumerate(((up_a, bias_a), (up_b, bias_b))):
+    for j, (pre, up) in enumerate(zip(pres, (up_a, up_b))):
         here = slice(j * width, (j + 1) * width)
-        pre = mxu(x[...], up[...]) + bias[...]
         square = pre * pre
         tan = jnp.tanh(0.7978845608028654 * pre * (1.0 + 0.044715 * square))
         half = 0.5 + 0.5 * tan
@@ -930,8 +954,6 @@
     x3 = send_tp(after(x2, arrived), 1)
     xs = [x0, x1, x2, x3]
 
-    w_out0 = exchange(after(copies, x1))
-
     here = jnp.concatenate([place, turn])
     length = TP * rows
     first, end = intervals(here, piece_starts, xs, rows)
@@ -958,27 +980,29 @@
     )
     halves_sent = expert.halves(*after((expert_up, expert_down), queries))
     halves_other = send_tp(halves_sent, 1)
-    near_own = exchange(after(cot_sent_own, w_out0))
+    near_own = exchange(cot_sent_own)
+    w_out0 = exchange(after(copies, near_own))
     down_bias = lax.dynamic_index_in_dim(expert_down_bias, lo, keepdims=True)
 
-    w_out2 = send_tp(w_out0, 2)
-    w_out1 = send_tp(w_out0, 1)
     *contexts, totals = attention_fwd(
-        after(queries, w_out0, halves_sent), keys, values, first, end, turn
-    )
+        after(queries, near_own, halves_sent), keys, values, first, end, turn
+    )
+    w_late = after(w_out0, totals)
+    w_out2, w_out1 = send_tp(w_late, 2), send_tp(w_late, 1)
     ctxs = [contexts[0]] + [send_tp(contexts[r], r) for r in range(1, TP)]
     w_outs = [w_out0, w_out1, w_out2, send_tp(after(w_out2, ctxs[1]), 1)]
-    near_other = exchange(after(cot_sent_other, near_own, totals))
-    far_own = send_tp(after(near_own, ctxs[3]), 2)
+    near_other = exchange(after(cot_sent_other, w_out0, totals))
+    far_own = send_tp(near_own, 2)
     cot_pieces = [near_own, far_own, near_other, send_tp(near_other, 2)]
     expert.hold(expert_up, expert_up_bias, None, expert_down, halves_other)
     act_backs, cot_sums = [None] * 4, [None] * 2
+    act_backs[0], act_backs[1], cot_sums[0] = expert.act_back(*cot_pieces[:2])
     mixed, second, upper, lower = plain_call(
         middle_kernel,
         ctxs
         + w_outs
         + [
-            after(residual_in, near_own, halves_other),
+            after(residual_in, act_backs[0]),
             row(output_bias),
             row(second_norm_gain),
             row(second_norm_shift),
@@ -989,12 +1013,11 @@
 
     bias_sent = lax.dynamic_index_in_dim(after(expert_up_bias, second), 1 - lo, keepdims=True)
     expert.hold(expert_up, expert_up_bias, send_tp(bias_sent, 1), expert_down, halves_other)
-    act_backs[0], act_backs[1], cot_sums[0] = expert.act_back(*cot_pieces[:2])
     act_backs[2], act_backs[3], cot_sums[1] = expert.act_back(*cot_pieces[2:])
     cot_sum = added(*cot_sums, dtype=f32)[:1]
     sent_own = plain_call(place_kernel, [second, s_own], [slotted])[0]
     sent_other = plain_call(
-        place_halves_kernel, [send_tp(upper, 1), send_tp(lower, 1), after(s_other, act_backs[0])], [slotted]
+        place_halves_kernel, [send_tp(upper, 1), send_tp(lower, 1), s_other], [slotted]
     )[0]
     rows_own = exchange(after(sent_own, near_other))
     rows_other = exchange(after(sent_other, rows_own, cot_pieces[3]))
@@ -1020,12 +1043,11 @@
     out_got = send_tp(after(out_far, got_other), 2)
     late = after(tuple(acts), back_sent_other)
     down_away = expert.down_outer(late, cot_pieces, 1, False)
-    out_near = expert.out(*after((acts[0], acts[2]), down_away), part=0.3)
-    up_own, up_sum = expert.up_outer(pieces, after(tuple(pre_backs), out_near), 0, True, part=0.3)
+    out_near = expert.out(*after((acts[0], acts[2]), down_away), part=0.5)
     up_got, down_got = send_tp(up_away, 1), send_tp(down_away, 1)
     sent = send_tp(jnp.concatenate([up_sum_away[:1], cot_sum], axis=0), 1)
     back_own, back_away = collect(
-        s_own, s_other, back_home_own, after(back_home_other, up_own, out_got, sent)
+        s_own, s_other, back_home_own, after(back_home_other, out_near, out_got, sent)
     )
     back_other = send_tp(back_away, 1)
 
@@ -1097,9 +1119,6 @@
         + [struct((shard + EXTRA, 3 * head_width), bf16)] * (n // 2 - 1),
     )
     wi_kept = (kept, folds)
-    sent = after(sent, folds)
-    up_bias_back = ordered(lo, up_sum[0], sent[0])
-    down_bias_back = ordered(lo, cot_sum[0], sent[1])
     wo_home = exchange(after(wo, out_own))
     output_weight_back = plain_call(
         turned_sum_kernel, [wo_home], [struct((head_width, shard), f32)]
@@ -1110,13 +1129,18 @@
         [struct((3, shard, head_width), f32), struct((8, 3 * head_width), f32)],
     )
 
-    up_back, down_back = expert.fill(after(up_own, wi_kept), down_own, up_got, down_got)
+    up_own, up_sum = expert.up_outer(pieces, after(tuple(pre_backs), wi_kept), 0, True, part=0.0)
+    up_back, down_back = expert.fill(up_own, down_own, up_got, down_got)
+    sent = after(sent, folds)
+    up_bias_back = ordered(lo, up_sum[0], sent[0])
+    down_bias_back = ordered(lo, cot_sum[0], sent[1])
     block_output = added(mixed, after(out_own, up_back), out_other)
 
-    back_residual = plain_call(
+    back_residual = row_call(
         last_kernel,
         [residual_in, row(first_norm_gain), sum0, got2, after(mixed_back, folds)],
         [struct((rows, width), f32)],
+        rows,
     )[0]
 
     tails = vector[5:].reshape(-1)

time: 486 us -> 484 us (level)
  waiting for transfers between devices: 67.5 us -> 55.3 us
  starting transfers between devices: 106 us -> 115 us
    all_to_all x9, waiting for transfers between devices: 3.51 us -> 24 us  [exchange(): return lax.all_to_all(x, 'fsdp', split_axis=0, concat_axis=0, tiled=True)]
    ppermute x37, waiting for transfers between devices: 31.2 us -> 12.3 us  [send_tp(): return lax.ppermute(x, 'tp', [(i, i ^ turn) for i in range(TP)])]
    ppermute x11, waiting for transfers between devices: 32.8 us -> 18.9 us  [send_fsdp(): return lax.ppermute(x, 'fsdp', [(i, i ^ turn) for i in range(n)])]
    ppermute x11, starting transfers between devices: 10 us -> 17.9 us  [send_fsdp(): return lax.ppermute(x, 'fsdp', [(i, i ^ turn) for i in range(n)])]
    pallas_call x27 -> x26, Pallas kernels: 100 us -> 94.9 us  [plain_call(): pl.pallas_call(kernel, name=kernel_name(kernel), grid=(1,), in_specs=[sme...]
    pallas_call x0 -> x1, Pallas kernels: none -> 5.09 us  [row_call(): pl.pallas_call(kernel, name=kernel_name(kernel), grid=(rows // tile,), in...]
    unnamed x100 -> x88, local copies, waits for them, and re-layouts: 16.9 us -> 15.3 us
  transfers between devices with their start and end apart: 57 -> 57, of which waited for: 19 -> 18; matrix products, arithmetic and copies ran while one was open for 1% -> 2% of each run, Pallas kernels for 53% -> 54%
where the time goes in v5:
time: 484 us; the launch traced here: 476 us
  Pallas kernels  277 us (57%)
  starting transfers between devices  115 us (24%)
  waiting for transfers between devices  55.3 us (11%)
  local copies, waits for them, and re-layouts  24 us (5%)
    pallas_call x14, Pallas kernels, call(): pl.pallas_call(kernel, name=kernel_name(kernel), grid_spec=pltpu.Prefetch...  126 us
    pallas_call x26, Pallas kernels, plain_call(): pl.pallas_call(kernel, name=kernel_name(kernel), grid=(1,), in_specs=[sme...  94.9 us
    all_to_all x9, starting transfers between devices, exchange(): return lax.all_to_all(x, 'fsdp', split_axis=0, concat_axis=0, tiled=True)  64.3 us
    ppermute x37, starting transfers between devices, send_tp(): return lax.ppermute(x, 'tp', [(i, i ^ turn) for i in range(TP)])  32.4 us
    pallas_call x1, Pallas kernels, attention_bwd(): pl.pallas_call(attend_back_kernel, name='attend_back', grid_spec=pltpu.Pr...  29.6 us
    all_to_all x9, waiting for transfers between devices, exchange(): return lax.all_to_all(x, 'fsdp', split_axis=0, concat_axis=0, tiled=True)  24 us
    pallas_call x1, Pallas kernels, attention_fwd(): pl.pallas_call(attend_kernel, name='attend', grid_spec=pltpu.PrefetchScal...  20.4 us
    ppermute x11, waiting for transfers between devices, send_fsdp(): return lax.ppermute(x, 'fsdp', [(i, i ^ turn) for i in range(n)])  18.9 us
  transfers between devices with their start and end apart: 57, of which 18 were waited for; matrix products, arithmetic and copies ran while one was open for 2% of the time, Pallas kernels for 54%

profile of v5, /device:TPU:9, one launch (start us, length us, event | category | flops | bytes accessed | tf_op | source)
XLA Modules:
  0.0 476.2 jit_solution(3952658188541986280)
XLA Ops:
  12.8 11.2 %collective-permute-done.2.refs_10_ = bf16[144,768]{1,0:T(8,128)(2,1)} collective-permute-done((bf16[144,768]{1,0:T(8,128)(2,1)}, bf16[144,768]{1,0:T(8,128)(2,1)}, u32[]{:S(2)}, u32[]{:S(2)}) %collective-permute-start.2) | collective-permute-done | bytes 221216 | tf_op jit(solution)/shard_map/ppermute | solution.py:109
  48.7 7.5 %project_kernel.1 = (bf16[2048,256]{1,0:T(8,128)(2,1)}, bf16[2048,256]{1,0:T(8,128)(2,1)}, bf16[2048,256]{1,0:T(8,128)(2,1)}, bf16[1024,768]{1,0:T(8,128)(2,1)}) custom-call(s32[1]{0:T(128)} %bitcast.1.place, bf16[528,1024]{1,0:T(8,128)(2,1)} %get-tuple-element.162.refs_0_, bf16[528,1024]{1,0:T(8,128)(2,1)} %copy-done.10, bf16[528,1024]{1,0:T(8,128)(2,1)} %copy-done.9, ...), custom_call_target="tpu_custom_call" | custom-call | flops 7700000256 | bytes 1 | tf_op jit(solution)/shard_map/project_kernel/pallas_call | solution.py:68
  63.3 6.5 %all-to-all-done = bf16[8,64,1024]{2,1,0:T(8,128)(2,1)} async-done(((bf16[8,64,1024]{2,1,0:T(8,128)(2,1)}), bf16[8,64,1024]{2,1,0:T(8,128)(2,1)}, u32[]{:S(2)}, u32[]{:S(2)}) %all-to-all-start) | async-done | bytes 1048608 | tf_op jit(solution)/shard_map/all_to_all | solution.py:923
  71.1 6.8 %all-to-all-start.1 = ((bf16[8,128,256]{2,1,0:T(8,128)(2,1)}), bf16[8,128,256]{2,1,0:T(8,128)(2,1)S(1)}, u32[]{:S(2)}, u32[]{:S(2)}) async-start(bf16[8,128,256]{2,1,0:T(8,128)(2,1)} %bitcast.8), calls=%async_computation.1 | async-start | bytes 1048576 | tf_op jit(solution)/shard_map/all_to_all | solution.py:923
  77.9 20.4 %attend.1 = (bf16[512,256]{1,0:T(8,128)(2,1)}, bf16[512,256]{1,0:T(8,128)(2,1)}, bf16[512,256]{1,0:T(8,128)(2,1)}, bf16[512,256]{1,0:T(8,128)(2,1)}, f32[8,2048]{1,0:T(8,128)}) custom-call(s32[1]{0:T(128)} %bitcast.t_ref, bf16[2048,256]{1,0:T(8,128)(2,1)} %get-tuple-element.253.q_ref, bf16[2048,256]{1,0:T(8,128)(2,1)} %get-tuple-element.173.k_ref, ...), custom_call_target="tpu_custom_call" | custom-call | flops 24199999488 | bytes 1 | tf_op jit(solution)/shard_map/attend/pallas_call | solution.py:448
  104.1 9.6 %all-to-all-start.2 = ((bf16[8,64,1024]{2,1,0:T(8,128)(2,1)}), bf16[8,64,1024]{2,1,0:T(8,128)(2,1)S(1)}, u32[]{:S(2)}, u32[]{:S(2)}) async-start(bf16[8,64,1024]{2,1,0:T(8,128)(2,1)} %bitcast.63), calls=%async_computation.2 | async-start | bytes 2097152 | tf_op jit(solution)/shard_map/all_to_all | solution.py:923
  116.5 9.3 %act_back_kernel.2 = (bf16[512,2048]{1,0:T(8,128)(2,1)}, bf16[512,2048]{1,0:T(8,128)(2,1)}, f32[8,1024]{1,0:T(8,128)}) custom-call(s32[1]{0:T(128)} %bitcast.7.lo, bf16[512,1024]{1,0:T(8,128)(2,1)} %bitcast.6.near.refs_4_, bf16[512,1024]{1,0:T(8,128)(2,1)} %collective-permute-done.16.far.refs_5_, bf16[2,1024,1024]{2,1,0:T(8,128)(2,1)} %down_a.7, ...), custom_call_target="tpu_custom_call" | custom-call | flops 9900000256 | bytes 1 | tf_op jit(solution)/shard_map/act_back_kernel/pallas_call | solution.py:746
  128.7 5.6 %middle_kernel.1 = (f32[512,1024]{1,0:T(8,128)}, bf16[512,1024]{1,0:T(8,128)(2,1)}, bf16[256,1024]{1,0:T(8,128)(2,1)}, bf16[256,1024]{1,0:T(8,128)(2,1)}) custom-call(bf16[512,256]{1,0:T(8,128)(2,1)} %get-tuple-element.177.refs_0_.rest_4_, bf16[512,256]{1,0:T(8,128)(2,1)} %collective-permute-done.10.refs_1_, bf16[512,256]{1,0:T(8,128)(2,1)} %copy-done.40, ...), custom_call_target="tpu_custom_call" | custom-call | flops 8800000000 | bytes 1 | tf_op jit(solution)/shard_map/middle_kernel/pallas_call | solution.py:68
  137.7 5.6 %all-to-all-start.3 = ((bf16[8,64,1024]{2,1,0:T(8,128)(2,1)}), bf16[8,64,1024]{2,1,0:T(8,128)(2,1)S(1)}, u32[]{:S(2)}, u32[]{:S(2)}) async-start(bf16[8,64,1024]{2,1,0:T(8,128)(2,1)} %bitcast.49), calls=%async_computation.3 | async-start | bytes 2097152 | tf_op jit(solution)/shard_map/all_to_all | solution.py:923
  152.0 14.6 %all-to-all-done.3 = bf16[8,64,1024]{2,1,0:T(8,128)(2,1)S(1)} async-done(((bf16[8,64,1024]{2,1,0:T(8,128)(2,1)}), bf16[8,64,1024]{2,1,0:T(8,128)(2,1)S(1)}, u32[]{:S(2)}, u32[]{:S(2)}) %all-to-all-start.3) | async-done | bytes 1048608 | tf_op jit(solution)/shard_map/all_to_all | solution.py:923
  167.9 6.5 %all-to-all-start.4 = ((bf16[8,64,1024]{2,1,0:T(8,128)(2,1)}), bf16[8,64,1024]{2,1,0:T(8,128)(2,1)S(1)}, u32[]{:S(2)}, u32[]{:S(2)}) async-start(bf16[8,64,1024]{2,1,0:T(8,128)(2,1)} %bitcast.52), calls=%async_computation.4 | async-start | bytes 2097152 | tf_op jit(solution)/shard_map/all_to_all | solution.py:923
  174.4 9.4 %act_back_kernel.3 = (bf16[512,2048]{1,0:T(8,128)(2,1)}, bf16[512,2048]{1,0:T(8,128)(2,1)}, f32[8,1024]{1,0:T(8,128)}) custom-call(s32[1]{0:T(128)} %bitcast.7.lo, bf16[512,1024]{1,0:T(8,128)(2,1)} %bitcast.60, bf16[512,1024]{1,0:T(8,128)(2,1)} %collective-permute-done.19.far.refs_7_, bf16[2,1024,1024]{2,1,0:T(8,128)(2,1)} %down_a.7, ...), custom_call_target="tpu_custom_call" | custom-call | flops 9900000256 | bytes 1 | tf_op jit(solution)/shard_map/act_back_kernel/pallas_call | solution.py:746
  184.4 10.2 %expert_kernel.4 = (bf16[512,2048]{1,0:T(8,128)(2,1)}, bf16[512,2048]{1,0:T(8,128)(2,1)}, bf16[512,1024]{1,0:T(8,128)(2,1)}) custom-call(s32[1]{0:T(128)} %bitcast.7.lo, bf16[512,1024]{1,0:T(8,128)(2,1)} %bitcast.39, bf16[512,2048]{1,0:T(8,128)(2,1)} %get-tuple-element.186.act_back, bf16[2,1024,1024]{2,1,0:T(8,128)(2,1)} %up_a.7, ...), custom_call_target="tpu_custom_call" | custom-call | flops 11000000512 | bytes 1 | tf_op jit(solution)/shard_map/expert_kernel/pallas_call | solution.py:746
  197.3 10.6 %expert_kernel.5 = (bf16[512,2048]{1,0:T(8,128)(2,1)}, bf16[512,2048]{1,0:T(8,128)(2,1)}, bf16[512,1024]{1,0:T(8,128)(2,1)}) custom-call(s32[1]{0:T(128)} %bitcast.7.lo, bf16[512,1024]{1,0:T(8,128)(2,1)} %copy-done.12, bf16[512,2048]{1,0:T(8,128)(2,1)} %get-tuple-element.205.act_back, bf16[2,1024,1024]{2,1,0:T(8,128)(2,1)} %up_a.7, ...), custom_call_target="tpu_custom_call" | custom-call | flops 11000000512 | bytes 1 | tf_op jit(solution)/shard_map/expert_kernel/pallas_call | solution.py:746
  209.1 10.2 %expert_kernel.6 = (bf16[512,2048]{1,0:T(8,128)(2,1)}, bf16[512,2048]{1,0:T(8,128)(2,1)}, bf16[512,1024]{1,0:T(8,128)(2,1)}) custom-call(s32[1]{0:T(128)} %bitcast.7.lo, bf16[512,1024]{1,0:T(8,128)(2,1)} %bitcast.43, bf16[512,2048]{1,0:T(8,128)(2,1)} %get-tuple-element.208.act_back, bf16[2,1024,1024]{2,1,0:T(8,128)(2,1)} %up_a.7, ...), custom_call_target="tpu_custom_call" | custom-call | flops 11000000512 | bytes 1 | tf_op jit(solution)/shard_map/expert_kernel/pallas_call | solution.py:746
  221.1 10.7 %expert_kernel.7 = (bf16[512,2048]{1,0:T(8,128)(2,1)}, bf16[512,2048]{1,0:T(8,128)(2,1)}, bf16[512,1024]{1,0:T(8,128)(2,1)}) custom-call(s32[1]{0:T(128)} %bitcast.7.lo, bf16[512,1024]{1,0:T(8,128)(2,1)} %copy-done.13, bf16[512,2048]{1,0:T(8,128)(2,1)} %get-tuple-element.196.act_back, bf16[2,1024,1024]{2,1,0:T(8,128)(2,1)} %up_a.7, ...), custom_call_target="tpu_custom_call" | custom-call | flops 11000000512 | bytes 1 | tf_op jit(solution)/shard_map/expert_kernel/pallas_call | solution.py:746
  231.8 9.1 %down_outer_kernel.2.down = f32[2,1024,1024]{2,1,0:T(8,128)} custom-call(s32[1]{0:T(128)} %bitcast.7.lo, bf16[512,2048]{1,0:T(8,128)(2,1)} %get-tuple-element.237.refs_0_.act_0, bf16[512,2048]{1,0:T(8,128)(2,1)} %get-tuple-element.234.refs_1_.act_0, bf16[512,2048]{1,0:T(8,128)(2,1)} %get-tuple-element.238.refs_2_.act_1, ...), custom_call_target="tpu_custom_call" | custom-call | flops 9900000256 | bytes 1 | tf_op jit(solution)/shard_map/down_outer_kernel/pallas_call | solution.py:746
  246.4 8.0 %all-to-all-start.5 = ((bf16[8,64,1024]{2,1,0:T(8,128)(2,1)}), bf16[8,64,1024]{2,1,0:T(8,128)(2,1)S(1)}, u32[]{:S(2)}, u32[]{:S(2)}) async-start(bf16[8,64,1024]{2,1,0:T(8,128)(2,1)} %bitcast.47), calls=%async_computation.5 | async-start | bytes 2097152 | tf_op jit(solution)/shard_map/all_to_all | solution.py:923
  254.4 8.9 %expert_out_kernel.2 = bf16[1024,1024]{1,0:T(8,128)(2,1)} custom-call(s32[1]{0:T(128)} %bitcast.7.lo, bf16[512,2048]{1,0:T(8,128)(2,1)} %get-tuple-element.234.refs_1_.act_0, bf16[512,2048]{1,0:T(8,128)(2,1)} %get-tuple-element.236.refs_3_.act_1, bf16[2,1024,1024]{2,1,0:T(8,128)(2,1)} %down_a.7, bf16[2,1024,1024]{2,1,0:T(8,128)(2,1)} %collective-permute-done.17.down_b.up_b), custom_call_target="tpu_custom_call" | custom-call | flops 9900000256 | bytes 1 | tf_op jit(solution)/shard_map/expert_out_kernel/pallas_call | solution.py:746
  265.1 9.7 %up_outer_kernel.2 = (bf16[1024,1024]{1,0:T(8,128)(2,1)}, f32[8,1024]{1,0:T(8,128)}) custom-call(s32[1]{0:T(128)} %bitcast.7.lo, bf16[512,1024]{1,0:T(8,128)(2,1)} %bitcast.40, bf16[512,1024]{1,0:T(8,128)(2,1)} %copy-done.12, bf16[512,1024]{1,0:T(8,128)(2,1)} %bitcast.44, bf16[512,1024]{1,0:T(8,128)(2,1)} %copy-done.13, ...), custom_call_target="tpu_custom_call" | custom-call | flops 9900000256 | bytes 1 | tf_op jit(solution)/shard_map/up_outer_kernel/pallas_call | solution.py:746
  277.5 8.2 %all-to-all-start.6 = ((bf16[8,64,1024]{2,1,0:T(8,128)(2,1)}), bf16[8,64,1024]{2,1,0:T(8,128)(2,1)S(1)}, u32[]{:S(2)}, u32[]{:S(2)}) async-start(bf16[8,64,1024]{2,1,0:T(8,128)(2,1)} %bitcast.46), calls=%async_computation.6 | async-start | bytes 2097152 | tf_op jit(solution)/shard_map/all_to_all | solution.py:923
  290.8 8.7 %down_outer_kernel.3 = bf16[1024,1024]{1,0:T(8,128)(2,1)} custom-call(s32[1]{0:T(128)} %bitcast.7.lo, bf16[512,2048]{1,0:T(8,128)(2,1)} %get-tuple-element.237.refs_0_.act_0, bf16[512,2048]{1,0:T(8,128)(2,1)} %get-tuple-element.234.refs_1_.act_0, bf16[512,2048]{1,0:T(8,128)(2,1)} %get-tuple-element.238.refs_2_.act_1, ...), custom_call_target="tpu_custom_call" | custom-call | flops 9900000256 | bytes 1 | tf_op jit(solution)/shard_map/down_outer_kernel/pallas_call | solution.py:746
  299.5 9.0 %expert_out_kernel.3.near = bf16[1024,1024]{1,0:T(8,128)(2,1)} custom-call(s32[1]{0:T(128)} %bitcast.7.lo, bf16[512,2048]{1,0:T(8,128)(2,1)} %get-tuple-element.237.refs_0_.act_0, bf16[512,2048]{1,0:T(8,128)(2,1)} %get-tuple-element.238.refs_2_.act_1, bf16[2,1024,1024]{2,1,0:T(8,128)(2,1)} %down_a.7, bf16[2,1024,1024]{2,1,0:T(8,128)(2,1)} %collective-permute-done.17.down_b.up_b), custom_call_target="tpu_custom_call" | custom-call | flops 4950000128 | bytes 1 | tf_op jit(solution)/shard_map/expert_out_kernel/pallas_call | solution.py:746
  321.7 6.9 %turn_kernel.1 = (f32[512,1024]{1,0:T(8,128)}, bf16[512,1024]{1,0:T(8,128)(2,1)}, f32[8,1024]{1,0:T(8,128)}, bf16[512,256]{1,0:T(8,128)(2,1)}, bf16[512,256]{1,0...) custom-call(bf16[1024,256]{1,0:T(8,128)(2,1)} %bitcast.56, bf16[1024,256]{1,0:T(8,128)(2,1)} %copy-done.23, ...), custom_call_target="tpu_custom_call" | custom-call | flops 1 | bytes 1 | tf_op jit(solution)/shard_map/turn_kernel/pallas_call | solution.py:68
  340.2 8.3 %all-to-all-start.7 = ((bf16[8,128,1024]{2,1,0:T(8,128)(2,1)}), bf16[8,128,1024]{2,1,0:T(8,128)(2,1)S(1)}, u32[]{:S(2)}, u32[]{:S(2)}) async-start(bf16[8,128,1024]{2,1,0:T(8,128)(2,1)} %bitcast.58), calls=%async_computation.7 | async-start | bytes 4194304 | tf_op jit(solution)/shard_map/all_to_all | solution.py:923
  352.5 29.6 %attend_back.1 = (bf16[2048,256]{1,0:T(8,128)(2,1)}, bf16[2048,256]{1,0:T(8,128)(2,1)}, bf16[2048,256]{1,0:T(8,128)(2,1)}) custom-call(s32[1]{0:T(128)} %bitcast.t_ref, bf16[2048,256]{1,0:T(8,128)(2,1)} %get-tuple-element.253.q_ref, bf16[2048,256]{1,0:T(8,128)(2,1)} %get-tuple-element.173.k_ref, bf16[2048,256]{1,0:T(8,128)(2,1)} %get-tuple-element.174.v_ref, ...), custom_call_target="tpu_custom_call" | custom-call | flops 32999999488 | bytes 1 | tf_op jit(solution)/shard_map/attend_back/pallas_call | solution.py:544
  385.0 12.6 %projection_back_kernel.1 = (bf16[512,1024]{1,0:T(8,128)(2,1)}, bf16[512,1024]{1,0:T(8,128)(2,1)}, bf16[512,1024]{1,0:T(8,128)(2,1)}, bf16[512,1024]{1,0:T(8,128...) custom-call(s32[1]{0:T(128)} %bitcast.1.place, ...), custom_call_target="tpu_custom_call" | custom-call | flops 14300000256 | bytes 1 | tf_op jit(solution)/shard_map/projection_back_kernel/pallas_call | solution.py:68
  398.6 7.9 %collective-permute-start.38 = (bf16[528,768]{1,0:T(8,128)(2,1)}, bf16[528,768]{1,0:T(8,128)(2,1)}, u32[]{:S(2)}, u32[]{:S(2)}) collective-permute-start(bf16[528,768]{1,0:T(8,128)(2,1)} %get-tuple-element.271), channel_id=1, source_target_pairs={{0,4},{4,0},{8,12},{12,8},{16,20},{20,16},{24,28},{28,24},{1,5},{5... | collective-permute-start | bytes 2433032 | tf_op jit(solution)/shard_map/ppermute | solution.py:109
  417.7 6.5 %all-to-all-start.8 = ((bf16[8,128,256]{2,1,0:T(8,128)(2,1)}), bf16[8,128,256]{2,1,0:T(8,128)(2,1)S(1)}, u32[]{:S(2)}, u32[]{:S(2)}) async-start(bf16[8,128,256]{2,1,0:T(8,128)(2,1)} %bitcast.25), calls=%async_computation.8 | async-start | bytes 1048576 | tf_op jit(solution)/shard_map/all_to_all | solution.py:923
  432.0 9.5 %up_outer_kernel.3 = (f32[2,1024,1024]{2,1,0:T(8,128)}, f32[8,1024]{1,0:T(8,128)}) custom-call(s32[1]{0:T(128)} %bitcast.7.lo, bf16[512,1024]{1,0:T(8,128)(2,1)} %bitcast.41, bf16[512,1024]{1,0:T(8,128)(2,1)} %copy-done.12, bf16[512,1024]{1,0:T(8,128)(2,1)} %bitcast.45, bf16[512,1024]{1,0:T(8,128)(2,1)} %copy-done.13, ...), custom_call_target="tpu_custom_call" | custom-call | flops 1 | bytes 1 | tf_op jit(solution)/shard_map/up_outer_kernel/pallas_call | solution.py:746
  441.6 5.8 %fill_kernel.1 = (f32[2,1024,1024]{2,1,0:T(8,128)}, f32[2,1024,1024]{2,1,0:T(8,128)}) custom-call(s32[1]{0:T(128)} %bitcast.7.lo, f32[2,1024,1024]{2,1,0:T(8,128)} %get-tuple-element.281.up, f32[2,1024,1024]{2,1,0:T(8,128)} %down_outer_kernel.2.down, ...), custom_call_target="tpu_custom_call", output_to_operand_aliasing={{0}: (1, {}), {1}: (2, {})} | custom-call | flops 1 | bytes 1 | tf_op jit(solution)/shard_map/fill_kernel/pallas_call | solution.py:746
  449.8 5.1 %last_kernel.1 = f32[512,1024]{1,0:T(8,128)} custom-call(bf16[512,1024]{1,0:T(8,128)(2,1)} %residual.1, f32[1,1024]{1,0:T(1,128)} %bitcast.67, bf16[512,1024]{1,0:T(8,128)(2,1)} %sum_kernel.13.own, bf16[512,1024]{1,0:T(8,128)(2,1)} %copy-done.15, f32[512,1024]{1,0:T(8,128)} %get-tuple-element.288.mixed_back), custom_call_target="tpu_custom_call" | custom-call | flops 1 | bytes 1 | tf_op jit(solution)/shard_map/last_kernel/pallas_call | solution.py:87
  (237 shorter events, 166.1 us)
Async XLA Ops:
  5.4 24.9 %collective-permute-start.5 = (bf16[528,1024]{1,0:T(8,128)(2,1)}, bf16[528,1024]{1,0:T(8,128)(2,1)S(1)}, u32[]{:S(2)}, u32[]{:S(2)}) collective-permute-start(bf16[528,1024]{1,0:T(8,128)(2,1)} %get-tuple-element.162.refs_0_), channel_id=1, source_target_pairs={{0,2},{1,3},{2,0},{3,1},{4,6},{5,7},{6,4},{7,5},{8,10},{9,11},{10,... | collective-permute-start | bytes 3244040 | tf_op jit(solution)/shard_map/ppermute | solution.py:104
  42.2 27.6 %all-to-all-start = ((bf16[8,64,1024]{2,1,0:T(8,128)(2,1)}), bf16[8,64,1024]{2,1,0:T(8,128)(2,1)}, u32[]{:S(2)}, u32[]{:S(2)}) async-start(bf16[8,64,1024]{2,1,0:T(8,128)(2,1)} %bitcast.51), calls=%async_computation | async-start | bytes 2097152 | tf_op jit(solution)/shard_map/all_to_all | solution.py:923
  61.0 55.5 %collective-permute-start.17 = (bf16[2,1024,1024]{2,1,0:T(8,128)(2,1)}, bf16[2,1024,1024]{2,1,0:T(8,128)(2,1)}, u32[]{:S(2)}, u32[]{:S(2)}) collective-permute-start(bf16[2,1024,1024]{2,1,0:T(8,128)(2,1)} %halves_kernel.1), channel_id=1, source_target_pairs={{0,1},{1,0},{2,3},{3,2},{4,5},{5,4},{6,7},{7,6},{8,9},{9,8},{10,11... | collective-permute-start | bytes 12582920 | tf_op jit(solution)/shard_map/ppermute | solution.py:104
  61.8 38.4 %collective-permute-start.18 = (bf16[528,1024]{1,0:T(8,128)(2,1)}, bf16[528,1024]{1,0:T(8,128)(2,1)S(1)}, u32[]{:S(2)}, u32[]{:S(2)}) collective-permute-start(bf16[528,1024]{1,0:T(8,128)(2,1)} %get-tuple-element.190), channel_id=1, source_target_pairs={{0,1},{1,0},{2,3},{3,2},{4,5},{5,4},{6,7},{7,6},{8,9},{9,8},{10,11... | collective-permute-start | bytes 3244040 | tf_op jit(solution)/shard_map/ppermute | solution.py:104
  69.8 46.2 %collective-permute-start.16 = (bf16[512,1024]{1,0:T(8,128)(2,1)}, bf16[512,1024]{1,0:T(8,128)(2,1)}, u32[]{:S(2)}, u32[]{:S(2)}) collective-permute-start(bf16[512,1024]{1,0:T(8,128)(2,1)} %bitcast.6.near.refs_4_), channel_id=1, source_target_pairs={{0,2},{1,3},{2,0},{3,1},{4,6},{5,7},{6,4},{7,5},{8,10},{9,11},{10,... | collective-permute-start | bytes 3145736 | tf_op jit(solution)/shard_map/ppermute | solution.py:104
  71.1 27.2 %all-to-all-start.1 = ((bf16[8,128,256]{2,1,0:T(8,128)(2,1)}), bf16[8,128,256]{2,1,0:T(8,128)(2,1)S(1)}, u32[]{:S(2)}, u32[]{:S(2)}) async-start(bf16[8,128,256]{2,1,0:T(8,128)(2,1)} %bitcast.8), calls=%async_computation.1 | async-start | bytes 1048576 | tf_op jit(solution)/shard_map/all_to_all | solution.py:923
  104.1 33.6 %all-to-all-start.2 = ((bf16[8,64,1024]{2,1,0:T(8,128)(2,1)}), bf16[8,64,1024]{2,1,0:T(8,128)(2,1)S(1)}, u32[]{:S(2)}, u32[]{:S(2)}) async-start(bf16[8,64,1024]{2,1,0:T(8,128)(2,1)} %bitcast.63), calls=%async_computation.2 | async-start | bytes 2097152 | tf_op jit(solution)/shard_map/all_to_all | solution.py:923
  137.7 28.9 %all-to-all-start.3 = ((bf16[8,64,1024]{2,1,0:T(8,128)(2,1)}), bf16[8,64,1024]{2,1,0:T(8,128)(2,1)S(1)}, u32[]{:S(2)}, u32[]{:S(2)}) async-start(bf16[8,64,1024]{2,1,0:T(8,128)(2,1)} %bitcast.49), calls=%async_computation.3 | async-start | bytes 2097152 | tf_op jit(solution)/shard_map/all_to_all | solution.py:923
  143.3 24.6 %collective-permute-start.19 = (bf16[512,1024]{1,0:T(8,128)(2,1)S(1)}, bf16[512,1024]{1,0:T(8,128)(2,1)}, u32[]{:S(2)}, u32[]{:S(2)}) collective-permute-start(bf16[512,1024]{1,0:T(8,128)(2,1)S(1)} %bitcast.59), channel_id=1, source_target_pairs={{0,2},{1,3},{2,0},{3,1},{4,6},{5,7},{6,4},{7,5},{8,10},{9,11},{10,... | collective-permute-start | bytes 3145736 | tf_op jit(solution)/shard_map/ppermute | solution.py:104
  146.5 37.4 %collective-permute-start.20 = (f32[1,1024]{1,0:T(1,128)S(1)}, f32[1,1024]{1,0:T(1,128)S(1)}, u32[]{:S(2)}, u32[]{:S(2)}) collective-permute-start(f32[1,1024]{1,0:T(1,128)S(1)} %constant_dynamic-slice_fusion.2), channel_id=1, source_target_pairs={{0,1},{1,0},{2,3},{3,2},{4,5},{5,4},{6,7},{7,6},{8,9},{9,8},{10,11... | collective-permute-start | bytes 12296 | tf_op jit(solution)/shard_map/ppermute | solution.py:104
  166.6 28.0 %collective-permute-start.23 = (bf16[512,1024]{1,0:T(8,128)(2,1)S(1)}, bf16[512,1024]{1,0:T(8,128)(2,1)S(1)}, u32[]{:S(2)}, u32[]{:S(2)}) collective-permute-start(bf16[512,1024]{1,0:T(8,128)(2,1)S(1)} %bitcast.38), channel_id=1, source_target_pairs={{0,2},{1,3},{2,0},{3,1},{4,6},{5,7},{6,4},{7,5},{8,10},{9,11},{10,... | collective-permute-start | bytes 3145736 | tf_op jit(solution)/shard_map/ppermute | solution.py:104
  167.9 29.4 %all-to-all-start.4 = ((bf16[8,64,1024]{2,1,0:T(8,128)(2,1)}), bf16[8,64,1024]{2,1,0:T(8,128)(2,1)S(1)}, u32[]{:S(2)}, u32[]{:S(2)}) async-start(bf16[8,64,1024]{2,1,0:T(8,128)(2,1)} %bitcast.52), calls=%async_computation.4 | async-start | bytes 2097152 | tf_op jit(solution)/shard_map/all_to_all | solution.py:923
  197.2 22.9 %collective-permute-start.24 = (bf16[512,1024]{1,0:T(8,128)(2,1)S(1)}, bf16[512,1024]{1,0:T(8,128)(2,1)S(1)}, u32[]{:S(2)}, u32[]{:S(2)}) collective-permute-start(bf16[512,1024]{1,0:T(8,128)(2,1)S(1)} %bitcast.42), channel_id=1, source_target_pairs={{0,2},{1,3},{2,0},{3,1},{4,6},{5,7},{6,4},{7,5},{8,10},{9,11},{10,... | collective-permute-start | bytes 3145736 | tf_op jit(solution)/shard_map/ppermute | solution.py:104
  207.9 34.7 %collective-permute-start.26 = (bf16[512,1024]{1,0:T(8,128)(2,1)}, bf16[512,1024]{1,0:T(8,128)(2,1)S(1)}, u32[]{:S(2)}, u32[]{:S(2)}) collective-permute-start(bf16[512,1024]{1,0:T(8,128)(2,1)} %get-tuple-element.206), channel_id=1, source_target_pairs={{0,2},{1,3},{2,0},{3,1},{4,6},{5,7},{6,4},{7,5},{8,10},{9,11},{10,... | collective-permute-start | bytes 3145736 | tf_op jit(solution)/shard_map/ppermute | solution.py:104
  231.8 33.3 %collective-permute-start.25 = (bf16[512,1024]{1,0:T(8,128)(2,1)}, bf16[512,1024]{1,0:T(8,128)(2,1)S(1)}, u32[]{:S(2)}, u32[]{:S(2)}) collective-permute-start(bf16[512,1024]{1,0:T(8,128)(2,1)} %get-tuple-element.215), channel_id=1, source_target_pairs={{0,2},{1,3},{2,0},{3,1},{4,6},{5,7},{6,4},{7,5},{8,10},{9,11},{10,... | collective-permute-start | bytes 3145736 | tf_op jit(solution)/shard_map/ppermute | solution.py:104
  246.4 31.2 %all-to-all-start.5 = ((bf16[8,64,1024]{2,1,0:T(8,128)(2,1)}), bf16[8,64,1024]{2,1,0:T(8,128)(2,1)S(1)}, u32[]{:S(2)}, u32[]{:S(2)}) async-start(bf16[8,64,1024]{2,1,0:T(8,128)(2,1)} %bitcast.47), calls=%async_computation.5 | async-start | bytes 2097152 | tf_op jit(solution)/shard_map/all_to_all | solution.py:923
  265.1 44.7 %collective-permute-start.27 = (bf16[1024,1024]{1,0:T(8,128)(2,1)}, bf16[1024,1024]{1,0:T(8,128)(2,1)}, u32[]{:S(2)}, u32[]{:S(2)}) collective-permute-start(bf16[1024,1024]{1,0:T(8,128)(2,1)} %expert_out_kernel.2), channel_id=1, source_target_pairs={{0,2},{1,3},{2,0},{3,1},{4,6},{5,7},{6,4},{7,5},{8,10},{9,11},{10,... | collective-permute-start | bytes 6291464 | tf_op jit(solution)/shard_map/ppermute | solution.py:104
  277.5 32.3 %all-to-all-start.6 = ((bf16[8,64,1024]{2,1,0:T(8,128)(2,1)}), bf16[8,64,1024]{2,1,0:T(8,128)(2,1)S(1)}, u32[]{:S(2)}, u32[]{:S(2)}) async-start(bf16[8,64,1024]{2,1,0:T(8,128)(2,1)} %bitcast.46), calls=%async_computation.6 | async-start | bytes 2097152 | tf_op jit(solution)/shard_map/all_to_all | solution.py:923
  288.7 19.8 %collective-permute-start.28 = (f32[2,1024]{1,0:T(2,128)S(1)}, f32[2,1024]{1,0:T(2,128)S(1)}, u32[]{:S(2)}, u32[]{:S(2)}) collective-permute-start(f32[2,1024]{1,0:T(2,128)S(1)} %pad_maximum_fusion.1), channel_id=1, source_target_pairs={{0,1},{1,0},{2,3},{3,2},{4,5},{5,4},{6,7},{7,6},{8,9},{9,8},{10,11... | collective-permute-start | bytes 24584 | tf_op jit(solution)/shard_map/ppermute | solution.py:104
  333.8 51.2 %collective-permute-start.34 = (bf16[1024,1024]{1,0:T(8,128)(2,1)}, bf16[1024,1024]{1,0:T(8,128)(2,1)}, u32[]{:S(2)}, u32[]{:S(2)}) collective-permute-start(bf16[1024,1024]{1,0:T(8,128)(2,1)} %get-tuple-element.231), channel_id=1, source_target_pairs={{0,1},{1,0},{2,3},{3,2},{4,5},{5,4},{6,7},{7,6},{8,9},{9,8},{10,11... | collective-permute-start | bytes 6291464 | tf_op jit(solution)/shard_map/ppermute | solution.py:104
  333.9 18.3 %collective-permute-start.31 = (bf16[512,256]{1,0:T(8,128)(2,1)}, bf16[512,256]{1,0:T(8,128)(2,1)}, u32[]{:S(2)}, u32[]{:S(2)}) collective-permute-start(bf16[512,256]{1,0:T(8,128)(2,1)} %get-tuple-element.254), channel_id=1, source_target_pairs={{0,1},{1,0},{2,3},{3,2},{4,5},{5,4},{6,7},{7,6},{8,9},{9,8},{10,11... | collective-permute-start | bytes 786440 | tf_op jit(solution)/shard_map/ppermute | solution.py:104
  340.2 71.2 %all-to-all-start.7 = ((bf16[8,128,1024]{2,1,0:T(8,128)(2,1)}), bf16[8,128,1024]{2,1,0:T(8,128)(2,1)S(1)}, u32[]{:S(2)}, u32[]{:S(2)}) async-start(bf16[8,128,1024]{2,1,0:T(8,128)(2,1)} %bitcast.58), calls=%async_computation.7 | async-start | bytes 4194304 | tf_op jit(solution)/shard_map/all_to_all | solution.py:923
  348.5 36.4 %collective-permute-start.35 = (bf16[1024,1024]{1,0:T(8,128)(2,1)}, bf16[1024,1024]{1,0:T(8,128)(2,1)}, u32[]{:S(2)}, u32[]{:S(2)}) collective-permute-start(bf16[1024,1024]{1,0:T(8,128)(2,1)} %down_outer_kernel.3), channel_id=1, source_target_pairs={{0,1},{1,0},{2,3},{3,2},{4,5},{5,4},{6,7},{7,6},{8,9},{9,8},{10,11... | collective-permute-start | bytes 6291464 | tf_op jit(solution)/shard_map/ppermute | solution.py:104
  352.2 29.8 %collective-permute-start.36 = (bf16[1024,256]{1,0:T(8,128)(2,1)}, bf16[1024,256]{1,0:T(8,128)(2,1)S(1)}, u32[]{:S(2)}, u32[]{:S(2)}) collective-permute-start(bf16[1024,256]{1,0:T(8,128)(2,1)} %get-tuple-element.261), channel_id=1, source_target_pairs={{0,2},{1,3},{2,0},{3,1},{4,6},{5,7},{6,4},{7,5},{8,10},{9,11},{10,... | collective-permute-start | bytes 1572872 | tf_op jit(solution)/shard_map/ppermute | solution.py:104
  398.5 25.7 %collective-permute-start.40 = (bf16[512,1024]{1,0:T(8,128)(2,1)}, bf16[512,1024]{1,0:T(8,128)(2,1)}, u32[]{:S(2)}, u32[]{:S(2)}) collective-permute-start(bf16[512,1024]{1,0:T(8,128)(2,1)} %get-tuple-element.286), channel_id=1, source_target_pairs={{0,1},{1,0},{2,3},{3,2},{4,5},{5,4},{6,7},{7,6},{8,9},{9,8},{10,11... | collective-permute-start | bytes 3145736 | tf_op jit(solution)/shard_map/ppermute | solution.py:104
  398.6 28.4 %collective-permute-start.38 = (bf16[528,768]{1,0:T(8,128)(2,1)}, bf16[528,768]{1,0:T(8,128)(2,1)}, u32[]{:S(2)}, u32[]{:S(2)}) collective-permute-start(bf16[528,768]{1,0:T(8,128)(2,1)} %get-tuple-element.271), channel_id=1, source_target_pairs={{0,4},{4,0},{8,12},{12,8},{16,20},{20,16},{24,28},{28,24},{1,5},{5... | collective-permute-start | bytes 2433032 | tf_op jit(solution)/shard_map/ppermute | solution.py:109
  410.2 38.6 %collective-permute-start.41 = (bf16[512,1024]{1,0:T(8,128)(2,1)}, bf16[512,1024]{1,0:T(8,128)(2,1)S(1)}, u32[]{:S(2)}, u32[]{:S(2)}) collective-permute-start(bf16[512,1024]{1,0:T(8,128)(2,1)} %sum_kernel.11), channel_id=1, source_target_pairs={{0,2},{1,3},{2,0},{3,1},{4,6},{5,7},{6,4},{7,5},{8,10},{9,11},{10,... | collective-permute-start | bytes 3145736 | tf_op jit(solution)/shard_map/ppermute | solution.py:104
  416.7 49.1 %collective-permute-start.39 = (bf16[512,1024]{1,0:T(8,128)(2,1)}, bf16[512,1024]{1,0:T(8,128)(2,1)S(1)}, u32[]{:S(2)}, u32[]{:S(2)}) collective-permute-start(bf16[512,1024]{1,0:T(8,128)(2,1)} %get-tuple-element.284), channel_id=1, source_target_pairs={{0,1},{1,0},{2,3},{3,2},{4,5},{5,4},{6,7},{7,6},{8,9},{9,8},{10,11... | collective-permute-start | bytes 3145736 | tf_op jit(solution)/shard_map/ppermute | solution.py:104
  417.7 45.4 %all-to-all-start.8 = ((bf16[8,128,256]{2,1,0:T(8,128)(2,1)}), bf16[8,128,256]{2,1,0:T(8,128)(2,1)S(1)}, u32[]{:S(2)}, u32[]{:S(2)}) async-start(bf16[8,128,256]{2,1,0:T(8,128)(2,1)} %bitcast.25), calls=%async_computation.8 | async-start | bytes 1048576 | tf_op jit(solution)/shard_map/all_to_all | solution.py:923
  429.4 25.5 %collective-permute-start.42 = (bf16[144,768]{1,0:T(8,128)(2,1)}, bf16[144,768]{1,0:T(8,128)(2,1)S(1)}, u32[]{:S(2)}, u32[]{:S(2)}) collective-permute-start(bf16[144,768]{1,0:T(8,128)(2,1)} %get-tuple-element.274), channel_id=1, source_target_pairs={{0,8},{4,12},{8,0},{12,4},{16,24},{20,28},{24,16},{28,20},{1,9},{5... | collective-permute-start | bytes 663560 | tf_op jit(solution)/shard_map/ppermute | solution.py:109
  429.4 25.5 %collective-permute-start.43 = (bf16[144,768]{1,0:T(8,128)(2,1)}, bf16[144,768]{1,0:T(8,128)(2,1)S(1)}, u32[]{:S(2)}, u32[]{:S(2)}) collective-permute-start(bf16[144,768]{1,0:T(8,128)(2,1)} %get-tuple-element.275), channel_id=1, source_target_pairs={{0,16},{4,20},{8,24},{12,28},{16,0},{20,4},{24,8},{28,12},{1,17},{... | collective-permute-start | bytes 663560 | tf_op jit(solution)/shard_map/ppermute | solution.py:109
  431.8 24.5 %collective-permute-start.44 = (bf16[144,768]{1,0:T(8,128)(2,1)}, bf16[144,768]{1,0:T(8,128)(2,1)S(1)}, u32[]{:S(2)}, u32[]{:S(2)}) collective-permute-start(bf16[144,768]{1,0:T(8,128)(2,1)} %get-tuple-element.276), channel_id=1, source_target_pairs={{0,24},{4,28},{8,16},{12,20},{16,8},{20,12},{24,0},{28,4},{1,25},{... | collective-permute-start | bytes 663560 | tf_op jit(solution)/shard_map/ppermute | solution.py:109
  (69 other events, 890.5 us)
